TPU v7x, 256 devices: a whole 4x4x8 slice. The times are simulated.
256 devices in a mesh: dp: 64 (over x, z, core), fsdp: 4 (over y).
Axes of the slice: x: 4, y: 4, z: 8, core: 2. Of those that a mesh axis runs over, the one named last changes fastest.
Arguments:
- query_reps: bfloat16 [4096, 4096], P('dp', 'fsdp'), may hold values from -2 to 2
- positive_reps: bfloat16 [4096, 4096], P('dp', 'fsdp'), may hold values from -8 to 8
- pool_reps: bfloat16 [8192, 4096], P('dp', 'fsdp'), may hold values from -8 to 8
- neg_owner: int32 [4096, 7], P('dp'), may hold values from 0 to 63, all different within a row; in each aligned block of 64 rows (0 to 63, 64 to 127, ...) at most 14 rows name the same one
- neg_row: int32 [4096, 7], P('dp'), may hold values from 0 to 127
- resid_in: bfloat16 [16384, 4096], P('dp', 'fsdp'), may hold values from -40 to 40
- attn_out: bfloat16 [16384, 2048], P('dp'), may hold values from -6 to 6
- out_weight: bfloat16 [2048, 4096], P(None, 'fsdp'), may hold values from -0.125 to 0.125
- norm_gain: float32 [4096], P('fsdp'), may hold values from 0.25 to 1.75
Outputs:
- resid_grad: bfloat16 [16384, 4096], P('dp', 'fsdp')
- attn_grad: bfloat16 [16384, 2048], P(('dp', 'fsdp'))
- weight_grad: bfloat16 [64, 2048, 4096], P('dp', None, 'fsdp')
- matching_reps_sensitivity: bfloat16 [4096, 4096], P('dp', 'fsdp')
- pool_grad: bfloat16 [8192, 4096], P('dp', 'fsdp')
Inputs may be any that keep to these rules, and one draw needn't show every extreme that they name: `neg_owner`: the 7 negatives of one query lie with different dp indices; among the queries of one micro-batch at most 14 negatives lie with one dp index, and some dp index holds exactly 14 in some micro-batch.
All inputs are finite; a program needn't handle non-finite values.
Results may differ from a plain program's by a relative error of at most 0.015.
Values may be sent and summed in bfloat16 or wider, within the bound.
No kernel may reach another device: no remote copies, remote signals or barrier semaphores. Data moves between devices by JAX's collectives and lax.ppermute only.
A program may use at most 128 MiB of HBM per device.

v0:
```python
import jax
import jax.numpy as jnp
from jax import lax
from jax.sharding import PartitionSpec as P

D = 4096
NEG = 7
QLEN = 16
Q_GRP = 64
CH_Q = 16
POOL_GRP = 128


logit_sharpness_divisor = 0.05
objective_scale_factor = 32.0
rep_epsilon = 1e-06
norm_epsilon = 1e-05
exact_arithmetic_mode = lax.Precision.HIGHEST


def feature_sum(values):
    return lax.psum(values, "fsdp")


def per_device(
    query_reps,
    positive_reps,
    pool_reps,
    neg_owner,
    neg_row,
    resid_in,
    attn_out,
    out_weight,
    norm_gain,
):
    owner_count = lax.axis_size("dp")
    feature_cols = query_reps.shape[1]
    request_count = Q_GRP * NEG
    slot_count = min(Q_GRP, (2 * request_count + owner_count - 1) // owner_count)
    token_count = resid_in.shape[0]
    owner_flat = neg_owner.reshape(request_count)
    row_flat = neg_row.reshape(request_count)
    one_hot = (owner_flat[:, None] == jnp.arange(owner_count, dtype=jnp.int32)[None, :]).astype(
        jnp.int32
    )
    before = jnp.cumsum(one_hot, axis=0) - one_hot
    position = owner_flat * slot_count + jnp.sum(before * one_hot, axis=1)
    request_ids = (
        jnp.full((owner_count * slot_count,), POOL_GRP, jnp.int32).at[position].set(row_flat)
    )
    request_ids = request_ids.reshape(owner_count, slot_count)
    wanted = lax.all_to_all(request_ids, "dp", split_axis=0, concat_axis=0, tiled=True)
    fetched = jnp.take(
        pool_reps, wanted.reshape(owner_count * slot_count), axis=0, mode="fill", fill_value=0
    )
    replies = lax.all_to_all(
        fetched.reshape(owner_count, slot_count, feature_cols),
        "dp",
        split_axis=0,
        concat_axis=0,
        tiled=True,
    )
    negatives_b = jnp.take(
        replies.reshape(owner_count * slot_count, feature_cols), position, axis=0
    )
    negatives_b = negatives_b.reshape(Q_GRP, NEG, feature_cols)
    asker_wide_reps = query_reps.astype(jnp.float32)
    matching_wide_reps = positive_reps.astype(jnp.float32)
    distractor_wide_reps = negatives_b.astype(jnp.float32)
    hidden = resid_in.astype(jnp.float32) + jnp.dot(
        attn_out, out_weight, preferred_element_type=jnp.float32
    )
    gained = hidden * norm_gain[None, :]
    sibling_cosine_matrix = lax.dot_general(
        query_reps, positive_reps, (((1,), (1,)), ((), ())), preferred_element_type=jnp.float32
    )
    distractor_cosine_matrix = jnp.einsum(
        "qd,qkd->qk", query_reps, negatives_b, preferred_element_type=jnp.float32
    )
    partial_sums = (
        sibling_cosine_matrix,
        distractor_cosine_matrix,
        jnp.sum(asker_wide_reps * asker_wide_reps, axis=1),
        jnp.sum(matching_wide_reps * matching_wide_reps, axis=1),
        jnp.sum(distractor_wide_reps * distractor_wide_reps, axis=2),
        jnp.sum(hidden * hidden, axis=1),
    )
    totals = feature_sum(partial_sums)
    (
        sibling_cosine_matrix,
        distractor_cosine_matrix,
        query_square,
        positive_square,
        negative_square,
        hidden_square,
    ) = totals[:6]
    asker_reciprocal_length = lax.rsqrt(query_square + rep_epsilon)
    matching_reciprocal_length = lax.rsqrt(positive_square + rep_epsilon)
    distractor_reciprocal_length = lax.rsqrt(negative_square + rep_epsilon)
    sibling_logit_matrix = (
        sibling_cosine_matrix
        * asker_reciprocal_length[:, None]
        * matching_reciprocal_length[None, :]
        / logit_sharpness_divisor
    )
    distractor_logit_matrix = (
        distractor_cosine_matrix
        * asker_reciprocal_length[:, None]
        * distractor_reciprocal_length
        / logit_sharpness_divisor
    )
    exp_inbatch = jnp.exp(sibling_logit_matrix)
    exp_negative = jnp.exp(distractor_logit_matrix)
    denominator = jnp.sum(exp_inbatch, axis=1) + jnp.sum(exp_negative, axis=1)
    sibling_pair_factor = exp_inbatch / denominator[:, None] - jnp.eye(Q_GRP, dtype=jnp.float32)
    distractor_pair_factor = exp_negative / denominator[:, None]
    self_dot = objective_scale_factor * (
        jnp.sum(sibling_pair_factor * sibling_logit_matrix, axis=1)
        + jnp.sum(distractor_pair_factor * distractor_logit_matrix, axis=1)
    )
    update_step_vector = (
        objective_scale_factor
        / logit_sharpness_divisor
        * (
            jnp.dot(
                sibling_pair_factor * matching_reciprocal_length[None, :],
                matching_wide_reps,
                precision=exact_arithmetic_mode,
            )
            + jnp.einsum(
                "ak,akr->ar",
                distractor_pair_factor * distractor_reciprocal_length,
                distractor_wide_reps,
                precision=exact_arithmetic_mode,
            )
        )
    )
    query_grad = (
        asker_reciprocal_length[:, None] * update_step_vector
        - (asker_reciprocal_length * asker_reciprocal_length * self_dot)[:, None] * asker_wide_reps
    )
    matching_reps_sensitivity = lax.dot_general(
        sibling_pair_factor * asker_reciprocal_length[:, None],
        asker_wide_reps,
        (((0,), (0,)), ((), ())),
        precision=exact_arithmetic_mode,
    )
    matching_reps_sensitivity = (
        objective_scale_factor
        / logit_sharpness_divisor
        * matching_reciprocal_length[:, None]
        * matching_reps_sensitivity
    )
    matching_reps_sensitivity = (
        matching_reps_sensitivity
        - (
            matching_reciprocal_length
            * matching_reciprocal_length
            * objective_scale_factor
            * jnp.sum(sibling_pair_factor * sibling_logit_matrix, axis=0)
        )[:, None]
        * matching_wide_reps
    )
    inv_rms = lax.rsqrt(hidden_square / D + norm_epsilon)
    pooled_grad = jnp.broadcast_to(
        (query_grad[:CH_Q] / QLEN)[:, None, :], (CH_Q, QLEN, feature_cols)
    ).reshape(token_count, feature_cols)
    inner_sum = feature_sum(jnp.sum(gained * pooled_grad, axis=1))
    cubed = inv_rms * inv_rms * inv_rms
    hidden_grad = (
        inv_rms[:, None] * norm_gain[None, :] * pooled_grad
        - hidden * (cubed * inner_sum / D)[:, None]
    )
    hidden_grad = hidden_grad.astype(jnp.bfloat16)
    attn_grad = lax.psum_scatter(
        lax.dot_general(
            hidden_grad, out_weight, (((1,), (1,)), ((), ())), preferred_element_type=jnp.float32
        ).astype(jnp.bfloat16),
        "fsdp",
        scatter_dimension=0,
        tiled=True,
    )
    weight_grad = lax.dot_general(
        attn_out, hidden_grad, (((0,), (0,)), ((), ())), preferred_element_type=jnp.float32
    )
    weight_grad = weight_grad.astype(jnp.bfloat16)[None]
    asker_output_matrix = (
        objective_scale_factor
        / logit_sharpness_divisor
        * distractor_pair_factor
        * asker_reciprocal_length[:, None]
        * distractor_reciprocal_length
    )
    weight_negative = (
        objective_scale_factor
        * distractor_pair_factor
        * distractor_logit_matrix
        * distractor_reciprocal_length
        * distractor_reciprocal_length
    )
    neg_terms = (
        asker_output_matrix[:, :, None] * asker_wide_reps[:, None, :]
        - weight_negative[:, :, None] * distractor_wide_reps
    )
    outgoing = (
        jnp.zeros((owner_count * slot_count, feature_cols), jnp.float32)
        .at[position]
        .set(neg_terms.reshape(request_count, feature_cols))
    )
    grad_terms = lax.all_to_all(
        outgoing.reshape(owner_count, slot_count, feature_cols),
        "dp",
        split_axis=0,
        concat_axis=0,
        tiled=True,
    )
    grad_terms = grad_terms.reshape(owner_count * slot_count, feature_cols)
    owner_hot = (
        wanted.reshape(-1)[:, None] == jnp.arange(POOL_GRP, dtype=jnp.int32)[None, :]
    ).astype(jnp.float32)
    pool_grad = lax.dot_general(
        owner_hot, grad_terms, (((0,), (0,)), ((), ())), precision=exact_arithmetic_mode
    )
    return (
        hidden_grad,
        attn_grad,
        weight_grad,
        matching_reps_sensitivity.astype(jnp.bfloat16),
        pool_grad.astype(jnp.bfloat16),
    )


def solution(mesh):
    placed = (
        P("dp", "fsdp"),
        P("dp", "fsdp"),
        P("dp", "fsdp"),
        P("dp", None),
        P("dp", None),
        P("dp", "fsdp"),
        P("dp", None),
        P(None, "fsdp"),
        P("fsdp"),
    )
    return jax.shard_map(
        per_device,
        mesh=mesh,
        in_specs=placed,
        out_specs=(
            P("dp", "fsdp"),
            P(("dp", "fsdp"), None),
            P("dp", None, "fsdp"),
            P("dp", "fsdp"),
            P("dp", "fsdp"),
        ),
        check_vma=False,
    )
```

profile of v0, /device:TPU:1, one launch (start us, length us, event | category | flops | bytes accessed | tf_op | source)
XLA Modules:
  0.0 258.1 jit_solution(4225080729399510923)
XLA Ops:
  7.2 0.9 copy.29
  8.1 0.1 reshape.167
  8.3 1.2 reduce-window.6
  9.5 0.2 slice_reduce_fusion
  9.9 0.1 mul.261
  10.0 0.8 copy.33
  10.8 0.1 reshape.199
  11.0 2.9 %scatter_custom_fusion = s32[896]{0:T(1024)S(1)} fusion(s32[448]{0:T(512)S(1)} %bitcast.58, s32[448]{0:T(512)S(1)} %reshape.199, s32[]{:T(128)} %constant.38.clone.1), kind=kCustom, calls=%fused_computation.87 | custom fusion | bytes 3588 | tf_op jit(solution)/shard_map/scatter | solution.py:49
  14.0 22.1 %all_to_all.19 = s32[64,1,14]{2,1,0:T(1,128)S(1)} all-to-all(s32[64,1,14]{2,1,0:T(1,128)S(1)} %bitcast.55), channel_id=1, replica_groups=mesh['dp'=64,'fsdp'=4] {'dp'}, dimensions={0} | all-to-all | bytes 7168 | tf_op jit(solution)/shard_map/all_to_all | solution.py:52
  36.1 0.5 broadcast.162
  36.6 0.7 reduce.10
  37.4 0.1 reshape.172
  37.6 4.2 %gather_fusion = bf16[896,1024]{1,0:T(8,128)(2,1)} fusion(bf16[128,1024]{1,0:T(8,128)(2,1)S(1)} %copy-done.1, s32[1024]{0:T(1024)S(1)} %pad_clamp_fusion.1), kind=kCustom, calls=%fused_computation | custom fusion | bytes 3673600 | tf_op jit(solution)/shard_map/jit(_take)/gather | solution.py:53
  41.7 2.5 gather.13
  44.3 1.5 broadcast_select_fusion
  45.9 5.7 %all-to-all-start.1 = ((bf16[64,14,1024]{2,1,0:T(8,128)(2,1)}), bf16[64,14,1024]{2,1,0:T(8,128)(2,1)}, u32[]{:S(2)}, u32[]{:S(2)}) async-start(bf16[64,14,1024]{2,1,0:T(8,128)(2,1)} %broadcast_select_fusion), calls=%async_computation.1 | async-start | bytes 4194304 | tf_op jit(solution)/shard_map/all_to_all | solution.py:56
  51.7 0.1 broadcast_in_dim.77
  51.9 0.2 mul.301
  52.2 1.5 mul.302
  53.9 0.2 fusion.43
  54.1 48.7 %all-to-all-done.1 = bf16[64,14,1024]{2,1,0:T(8,128)(2,1)} async-done(((bf16[64,14,1024]{2,1,0:T(8,128)(2,1)}), bf16[64,14,1024]{2,1,0:T(8,128)(2,1)}, u32[]{:S(2)}, u32[]{:S(2)}) %all-to-all-start.1) | async-done | bytes 1835040 | tf_op jit(solution)/shard_map/all_to_all | solution.py:56
  102.9 2.6 %reshape.173 = bf16[896,1024]{1,0:T(8,128)(2,1)S(1)} reshape(bf16[64,14,1024]{2,1,0:T(8,128)(2,1)} %all-to-all-done.1) | data formatting | bytes 3670016 | tf_op jit(solution)/shard_map/reshape | solution.py:64
  105.5 2.7 %gather_fusion.1 = bf16[448,1024]{1,0:T(8,128)(2,1)} fusion(bf16[896,1024]{1,0:T(8,128)(2,1)S(1)} %reshape.173, s32[1024]{0:T(1024)S(1)} %pad_clamp_fusion), kind=kCustom, calls=%fused_computation.1 | custom fusion | bytes 1836800 | tf_op jit(solution)/shard_map/jit(_take)/gather | solution.py:63
  108.2 1.4 gather.15
  109.6 0.9 fusion.12
  110.6 0.2 copy-done.2
  110.8 0.4 multiply_reduce_fusion
  111.2 0.1 reduce_sum.113
  111.4 13.9 %all-reduce.2 = (f32[64,7]{0,1:T(8,128)S(1)}, f32[64,64]{1,0:T(8,128)S(1)}, f32[64]{0:T(128)S(1)}, f32[64]{0:T(128)S(1)}, f32[64,7]{0,1:T(8,128)S(1)}) all-reduce(f32[64,7]{0,1:T(8,128)S(1)} %copy.35, f32[64,64]{1,0:T(8,128)S(1)} %fusion.43, f32[64]{0:T(128)S(1)} %fusion.20, ...), channel_id=1, replica_groups=mesh['dp'=64,'fsdp'=4] {'fsdp'}, use_global_device_ids=true, to_apply=%region_14.15 | all-reduce | flops 5120 | bytes 40960 | tf_op jit(solution)/shard_map/psum | solution.py:22
  125.4 0.2 exponential_reduce_fusion
  125.7 0.1 mul.299
  125.9 0.1 mul.309
  126.1 5.4 %scatter_custom_fusion.1 = f32[896,1024]{1,0:T(8,128)} fusion(s32[448]{0:T(512)S(1)} %bitcast.60, f32[448,1024]{1,0:T(8,128)} %mul.302, f32[]{:T(128)} %constant.22.clone.1, bf16[448,1024]{1,0:T(8,128)(2,1)S(1)} %copy-done.2, f32[448]{0:T(512)S(1)} %mul.309, f32[448]{0:T(512)S(1)} %mul.299, pred[448]{0:T(512)(128)(4,1)S(1)} %compare_and_fusion.2, ...), kind=kCustom, calls=%fused_computation.7 | custom fusion | flops 2293760 | bytes 6427142 | tf_op jit(solution)/shard_map/scatter | solution.py:208
  131.5 4.9 %reshape.176 = f32[64,14,1024]{2,1,0:T(8,128)} reshape(f32[896,1024]{1,0:T(8,128)} %scatter_custom_fusion.1) | data formatting | bytes 7340032 | tf_op jit(solution)/shard_map/reshape | solution.py:211
  136.3 9.8 %all-to-all-start.2 = ((f32[64,14,1024]{2,1,0:T(8,128)}), f32[64,14,1024]{2,1,0:T(8,128)}, u32[]{:S(2)}, u32[]{:S(2)}) async-start(f32[64,14,1024]{2,1,0:T(8,128)} %reshape.176), calls=%async_computation.3 | async-start | bytes 8388608 | tf_op jit(solution)/shard_map/all_to_all | solution.py:210
  146.3 1.0 fusion.11
  147.4 0.2 fusion.39
  147.6 0.3 fusion.29
  148.0 3.8 %multiply_reduce_fusion.1 = (f32[256]{0:T(256)S(1)}, f32[256]{0:T(256)S(1)}, f32[256,1024]{1,0:T(8,128)S(1)}) fusion(f32[16,1024]{1,0:T(8,128)S(1)} %fusion.26, f32[1024]{0:T(1024)S(1)} %copy-done.6, bf16[256,2048]{1,0:T(8,128)(2,1)S(1)} %copy-done, bf16[2048,1024]{1,0:T(8,128)(2,1)} %param.16, bf16[256,1024]{1,0:T(8,128)(2,1)} %param.14), kind=kOutput, calls=%fused_computation.24 | convolution fusion | flops 1075576320 | bytes 6887424 | tf_op jit(solution)/shard_map/dot_general | solution.py:70
  151.8 6.8 %all-reduce.1 = (f32[256]{0:T(256)S(1)}, f32[256]{0:T(256)S(1)}) all-reduce(f32[256]{0:T(256)S(1)} %get-tuple-element.26, f32[256]{0:T(256)S(1)} %get-tuple-element.25), channel_id=1, replica_groups=mesh['dp'=64,'fsdp'=4] {'fsdp'}, use_global_device_ids=true, to_apply=%region_19.20 | all-reduce | flops 512 | bytes 4096 | tf_op jit(solution)/shard_map/psum | solution.py:22
  158.7 0.2 fusion.9
  158.9 4.7 %convolution_convert_fusion = bf16[256,2048]{1,0:T(8,128)(2,1)} fusion(bf16[256,1024]{1,0:T(8,128)(2,1)S(1)} %fusion.9, bf16[2048,1024]{1,0:T(8,128)(2,1)} %param.16), kind=kOutput, calls=%fused_computation.5 | convolution fusion | flops 1074266112 | bytes 5767168 | tf_op jit(solution)/shard_map/dot_general | solution.py:176
  163.8 3.3 %convert_bitcast_fusion = bf16[1,2048,1024]{1,2,0:T(8,128)(2,1)} fusion(bf16[256,1024]{1,0:T(8,128)(2,1)S(1)} %fusion.9, bf16[256,2048]{1,0:T(8,128)(2,1)S(1)} %copy-done), kind=kOutput, calls=%fused_computation.4 | convolution fusion | flops 1075838976 | bytes 5767168 | tf_op jit(solution)/shard_map/dot_general | solution.py:183
  167.1 6.4 %copy.38 = bf16[1,2048,1024]{2,1,0:T(8,128)(2,1)} copy(bf16[1,2048,1024]{1,2,0:T(8,128)(2,1)} %convert_bitcast_fusion) | data formatting | bytes 8388608
  173.5 1.1 fusion.7
  174.5 67.5 %all-to-all-done.2 = f32[64,14,1024]{2,1,0:T(8,128)} async-done(((f32[64,14,1024]{2,1,0:T(8,128)}), f32[64,14,1024]{2,1,0:T(8,128)}, u32[]{:S(2)}, u32[]{:S(2)}) %all-to-all-start.2) | async-done | bytes 3670048 | tf_op jit(solution)/shard_map/all_to_all | solution.py:210
  242.0 4.9 %reshape.177 = f32[896,1024]{1,0:T(8,128)} reshape(f32[64,14,1024]{2,1,0:T(8,128)} %all-to-all-done.2) | data formatting | bytes 7340032 | tf_op jit(solution)/shard_map/reshape | solution.py:217
  246.9 4.3 %convolution_convert_fusion.1 = bf16[128,1024]{1,0:T(8,128)(2,1)} fusion(f32[896,1024]{1,0:T(8,128)} %reshape.177, s32[896]{0:T(1024)S(1)} %reshape.175), kind=kOutput, calls=%fused_computation.17 | convolution fusion | flops 1409531904 | bytes 3935744 | tf_op jit(solution)/shard_map/dot_general | solution.py:221
  (50 shorter events, 1.7 us)
Async XLA Ops:
  7.2 140.9 %copy-start = (bf16[256,2048]{1,0:T(8,128)(2,1)S(1)}, bf16[256,2048]{1,0:T(8,128)(2,1)}, u32[]{:S(2)}) copy-start(bf16[256,2048]{1,0:T(8,128)(2,1)} %param.15) | copy-start | bytes 3145732
  7.2 30.4 %copy-start.1 = (bf16[128,1024]{1,0:T(8,128)(2,1)S(1)}, bf16[128,1024]{1,0:T(8,128)(2,1)}, u32[]{:S(2)}) copy-start(bf16[128,1024]{1,0:T(8,128)(2,1)} %param.11) | copy-start | bytes 786436
  45.8 6.0 %copy-start.4 = (bf16[64,1024]{1,0:T(8,128)(2,1)S(1)}, bf16[64,1024]{1,0:T(8,128)(2,1)}, u32[]{:S(2)}) copy-start(bf16[64,1024]{1,0:T(8,128)(2,1)} %param.9) | copy-start | bytes 393220
  45.9 57.0 %all-to-all-start.1 = ((bf16[64,14,1024]{2,1,0:T(8,128)(2,1)}), bf16[64,14,1024]{2,1,0:T(8,128)(2,1)}, u32[]{:S(2)}, u32[]{:S(2)}) async-start(bf16[64,14,1024]{2,1,0:T(8,128)(2,1)} %broadcast_select_fusion), calls=%async_computation.1 | async-start | bytes 4194304 | tf_op jit(solution)/shard_map/all_to_all | solution.py:56
  52.2 1.6 copy-start.5
  109.6 1.2 copy-start.2
  136.3 105.7 %all-to-all-start.2 = ((f32[64,14,1024]{2,1,0:T(8,128)}), f32[64,14,1024]{2,1,0:T(8,128)}, u32[]{:S(2)}, u32[]{:S(2)}) async-start(f32[64,14,1024]{2,1,0:T(8,128)} %reshape.176), calls=%async_computation.3 | async-start | bytes 8388608 | tf_op jit(solution)/shard_map/all_to_all | solution.py:210
  146.1 1.9 copy-start.6
  146.1 105.1 %reduce-scatter.2.cloned.1.call-start = ((), (), s32[]{:S(2)}) async-start(), calls=%async_computation.4 | async-start | bytes 1310720 | tf_op jit(solution)/shard_map/reduce_scatter | solution.py:175
  158.9 4.9 %copy-start.3 = (bf16[256,1024]{1,0:T(8,128)(2,1)}, bf16[256,1024]{1,0:T(8,128)(2,1)S(1)}, u32[]{:S(2)}) copy-start(bf16[256,1024]{1,0:T(8,128)(2,1)S(1)} %fusion.9) | copy-start | bytes 1572868
Sparse Core Ops, SparseCore 0:
  163.8 25.6 reduce-scatter.1
where the time goes:
time: 259 us; the launch traced here: 258 us
  waiting for transfers between devices  116 us (45%)
  blocking collectives  42.8 us (17%)
  local copies, waits for them, and re-layouts  38.9 us (15%)
  matrix products  19.6 us (8%)
  starting transfers between devices  15.5 us (6%)
  between operations  14.4 us (6%)
  other arithmetic  10.7 us (4%)
    all_to_all x1, waiting for transfers between devices, per_device(): lax.all_to_all(outgoing.reshape(owner_count, slot_count, feature_cols), '...  67.5 us
    all_to_all x1, waiting for transfers between devices, per_device(): lax.all_to_all(fetched.reshape(owner_count, slot_count, feature_cols), 'd...  48.7 us
    all_to_all x1, blocking collectives, per_device(): lax.all_to_all(request_ids, 'dp', split_axis=0, concat_axis=0, tiled=True)  22.1 us
    psum x2, blocking collectives, feature_sum(): return lax.psum(values, 'fsdp')  20.7 us
    all_to_all x1, starting transfers between devices, per_device(): lax.all_to_all(outgoing.reshape(owner_count, slot_count, feature_cols), '...  9.76 us
    unnamed x17, local copies, waits for them, and re-layouts  8.28 us
    gather x2, local copies, waits for them, and re-layouts, per_device(): jnp.take(pool_reps, wanted.reshape(owner_count * slot_count), axis=0, mod...  6.74 us
    all_to_all x1, starting transfers between devices, per_device(): lax.all_to_all(fetched.reshape(owner_count, slot_count, feature_cols), 'd...  5.72 us
  transfers between devices with their start and end apart: 3, of which 2 were waited for; matrix products, arithmetic and copies ran while one was open for 13% of the time, Pallas kernels for 0%

commit v1 on v0

v1 whole, which is shorter than its diff:
```python
import jax
import jax.numpy as jnp
from jax import lax
from jax.sharding import PartitionSpec as P

D = 4096
NEG = 7
QLEN = 16
Q_GRP = 64
CH_Q = 16
POOL_GRP = 128
SLOTS = 16
N_FS = 4


inv_temp = 1.0 / 0.05
loss_scale = 32.0
rep_epsilon = 1e-06
norm_epsilon = 1e-05
F32 = jnp.float32
BF16 = jnp.bfloat16


def dot(a, b, ca, cb):
    return lax.dot_general(a, b, (((ca,), (cb,)), ((), ())), preferred_element_type=F32)


def dot_exact(a, b, ca, cb):
    return lax.dot_general(
        a, b, (((ca,), (cb,)), ((), ())), precision=lax.Precision.HIGHEST, preferred_element_type=F32
    )


def split(a):
    hi = a.astype(BF16)
    return hi, (a - hi.astype(F32)).astype(BF16)


def shifted(value, step):
    return lax.ppermute(value, "fsdp", [(i, (i + step) % N_FS) for i in range(N_FS)])


def feature_total(rows):
    return rows + shifted(rows, 1) + shifted(rows, 3) + shifted(rows, 2)


def feature_scatter(rows):
    own = rows.shape[0] // N_FS
    me = lax.axis_index("fsdp")
    total = lax.dynamic_slice(rows, (me * own, 0), (own, rows.shape[1]))
    for step in (1, 3, 2):
        there = lax.rem(me + step, N_FS)
        total += shifted(lax.dynamic_slice(rows, (there * own, 0), (own, rows.shape[1])), step)
    return total


def per_device(q, pos, pool, neg_owner, neg_row, resid_in, attn_out, out_weight, norm_gain):
    owners = lax.axis_size("dp")
    cols = q.shape[1]
    requests = Q_GRP * NEG
    tokens = resid_in.shape[0]
    slot_rows = owners * SLOTS

    q_all = lax.all_gather(q, "dp", tiled=True)

    owner_t = neg_owner.T
    row_t = neg_row.T
    owner_hot = (owner_t[:, :, None] == jnp.arange(owners)[None, None, :]).astype(BF16)
    owner_hot = owner_hot.reshape(requests, owners)
    order = jnp.arange(requests)
    earlier = (order[:, None] > order[None, :]).astype(BF16)
    before = dot(earlier, owner_hot, 1, 0)
    position = jnp.sum(before * owner_hot.astype(F32), axis=1).astype(jnp.int32)
    place_hot = (position[:, None] == jnp.arange(SLOTS)[None, :]).astype(BF16)
    row_mark = (row_t + 1).astype(BF16).reshape(requests, 1)
    query_mark = jnp.broadcast_to((jnp.arange(Q_GRP) + 1).astype(BF16)[None, :], (NEG, Q_GRP))
    query_mark = query_mark.reshape(requests, 1)
    table = dot(
        owner_hot, jnp.concatenate([place_hot * row_mark, place_hot * query_mark], axis=1), 0, 0
    ).astype(jnp.int32)
    code = table[:, :SLOTS] * 128 + table[:, SLOTS:]
    wanted = lax.all_to_all(code, "dp", split_axis=0, concat_axis=0, tiled=True)
    wanted_row = wanted // 128 - 1
    wanted_query = wanted % 128 - 1
    row_hot = (wanted_row.reshape(slot_rows)[:, None] == jnp.arange(POOL_GRP)[None, :]).astype(BF16)
    fetched = dot(row_hot, pool, 1, 0).astype(BF16).reshape(owners, SLOTS, cols)
    replies = lax.all_to_all(fetched, "dp", split_axis=0, concat_axis=0, tiled=True)

    fetched, q, pos, resid_in, attn_out = lax.optimization_barrier(
        (fetched, q, pos, resid_in, attn_out)
    )
    q_wide = q.astype(F32)
    pos_wide = pos.astype(F32)
    attn_turned = attn_out.T
    hidden = resid_in.astype(F32) + dot(attn_out, out_weight, 1, 0)
    hid_hi, hid_lo = split(hidden)
    scaled_hi, scaled_lo = split(hidden * norm_gain[None, :])
    both = jnp.concatenate([pos, q], axis=0)
    scaled_dots = dot(scaled_hi, both, 1, 1) + dot(scaled_lo, both, 1, 1)
    lane = jnp.arange(2 * Q_GRP)
    scaled_dots = jnp.where(
        lane[None, :] == 2 * Q_GRP - 1, jnp.sum(hidden * hidden, axis=1)[:, None], scaled_dots
    )
    p_row = jnp.concatenate([jnp.sum(pos_wide * pos_wide, axis=1), jnp.zeros((Q_GRP,), F32)])
    early = feature_total(
        jnp.concatenate(
            [scaled_dots, dot(q, both, 1, 1), jnp.broadcast_to(p_row[None, :], (8, 2 * Q_GRP))],
            axis=0,
        )
    )
    hidden_back = feature_scatter(dot(hid_hi, out_weight, 1, 1) + dot(hid_lo, out_weight, 1, 1))
    eye = jnp.eye(Q_GRP, dtype=F32)
    q_sq = jnp.sum(early[tokens : tokens + Q_GRP, Q_GRP:] * eye, axis=1)
    p_sq = early[tokens + Q_GRP, :Q_GRP]
    h_sq = early[:tokens, 2 * Q_GRP - 1]
    inv_q = lax.rsqrt(q_sq + rep_epsilon)
    inv_p = lax.rsqrt(p_sq + rep_epsilon)
    inv_rms = lax.rsqrt(h_sq / D + norm_epsilon)
    s_in = early[tokens : tokens + Q_GRP, :Q_GRP] * inv_q[:, None] * inv_p[None, :] * inv_temp
    exp_in = jnp.exp(s_in)
    sum_in = jnp.sum(exp_in, axis=1)
    token_query = jnp.arange(tokens) // QLEN
    scaled_pos = early[:tokens, :Q_GRP]
    scaled_q = jnp.sum(
        jnp.where(
            token_query[:, None] == jnp.arange(CH_Q)[None, :],
            early[:tokens, Q_GRP : Q_GRP + CH_Q],
            0.0,
        ),
        axis=1,
    )
    replies, sum_in, scaled_q, attn_turned, hidden_back, inv_rms = lax.optimization_barrier(
        (replies, sum_in, scaled_q, attn_turned, hidden_back, inv_rms)
    )

    slot = owner_t.reshape(requests) * SLOTS + position
    slot_hot = (slot[:, None] == jnp.arange(slot_rows)[None, :]).astype(BF16)
    negs = dot(slot_hot, replies.reshape(slot_rows, cols), 1, 0).astype(BF16)
    negs = negs.reshape(NEG, Q_GRP, cols)
    negs_wide = negs.astype(F32)
    n_cos = jnp.sum(negs_wide * q_wide[None], axis=2)
    n_sq = jnp.sum(negs_wide * negs_wide, axis=2)
    first_negs = negs[:, :CH_Q].reshape(NEG * CH_Q, cols)
    scaled_negs = dot(scaled_hi, first_negs, 1, 1) + dot(scaled_lo, first_negs, 1, 1)
    scaled_negs = jnp.sum(
        jnp.where(
            token_query[:, None, None] == jnp.arange(CH_Q)[None, None, :],
            scaled_negs.reshape(tokens, NEG, CH_Q),
            0.0,
        ),
        axis=2,
    )
    late = feature_total(
        jnp.concatenate(
            [
                jnp.concatenate([n_cos, jnp.zeros((1, Q_GRP), F32)], axis=0),
                jnp.concatenate([n_sq, jnp.zeros((1, Q_GRP), F32)], axis=0),
                scaled_negs.T.reshape(NEG * tokens // Q_GRP, Q_GRP),
            ],
            axis=0,
        )
    )
    n_cos = late[:NEG]
    n_sq = late[NEG + 1 : 2 * NEG + 1]
    scaled_negs = late[2 * NEG + 2 :].reshape(NEG, tokens)
    inv_n = lax.rsqrt(n_sq + rep_epsilon)
    s_neg = n_cos * inv_q[None, :] * inv_n * inv_temp
    exp_neg = jnp.exp(s_neg)
    denominator = sum_in + jnp.sum(exp_neg, axis=0)
    coef_in = exp_in / denominator[:, None] - eye
    coef_neg = exp_neg / denominator[None, :]

    w_q = loss_scale * inv_temp * coef_neg * inv_q[None, :] * inv_n
    w_n = loss_scale * coef_neg * s_neg * inv_n * inv_n
    place = place_hot.astype(F32)
    sent = dot_exact(
        owner_hot.astype(F32),
        jnp.concatenate(
            [place * w_q.reshape(requests, 1), place * w_n.reshape(requests, 1)], axis=1
        ),
        0,
        0,
    )
    got = lax.all_to_all(sent, "dp", split_axis=0, concat_axis=0, tiled=True)

    self_dot = loss_scale * (jnp.sum(coef_in * s_in, axis=1) + jnp.sum(coef_neg * s_neg, axis=0))
    pos_part = (coef_in * inv_p[None, :])[:CH_Q]
    neg_part = (coef_neg * inv_n)[:, :CH_Q]
    direction = dot_exact(pos_part, pos_wide, 1, 0) + jnp.sum(
        neg_part[:, :, None] * negs_wide[:, :CH_Q], axis=0
    )
    inv_c = inv_q[:CH_Q]
    scale_dir = loss_scale * inv_temp * inv_c * (1.0 / QLEN)
    scale_own = inv_c * inv_c * self_dot[:CH_Q] * (1.0 / QLEN)
    pooled = scale_dir[:, None] * direction - scale_own[:, None] * q_wide[:CH_Q]
    gained = pooled * norm_gain[None, :]
    inner = jnp.repeat(scale_dir, QLEN) * (
        jnp.sum(jnp.repeat(pos_part, QLEN, axis=0) * scaled_pos, axis=1)
        + jnp.sum(jnp.repeat(neg_part, QLEN, axis=1) * scaled_negs, axis=0)
    ) - jnp.repeat(scale_own, QLEN) * scaled_q
    hidden_c = hidden.reshape(CH_Q, QLEN, cols)
    shrink = inv_rms * inv_rms * inv_rms * inner * (1.0 / D)
    g_hi, g_lo = split(gained)
    gained_back = dot(jnp.concatenate([g_hi, g_lo], axis=0), out_weight, 1, 1)
    gained_back = feature_scatter(gained_back[:CH_Q] + gained_back[CH_Q:])
    resid_grad = (
        inv_rms.reshape(CH_Q, QLEN, 1) * gained[:, None, :]
        - hidden_c * shrink.reshape(CH_Q, QLEN, 1)
    ).reshape(tokens, cols).astype(BF16)
    own = tokens // N_FS
    first = lax.axis_index("fsdp") * own
    own_rms = lax.dynamic_slice(inv_rms, (first,), (own,))
    own_shrink = lax.dynamic_slice(shrink, (first,), (own,))
    gained_rows = jnp.broadcast_to(
        gained_back[:, None, :], (CH_Q // N_FS, QLEN, gained_back.shape[1])
    ).reshape(own, gained_back.shape[1])
    attn_grad = (own_rms[:, None] * gained_rows - own_shrink[:, None] * hidden_back).astype(BF16)
    weight_grad = dot(attn_turned, resid_grad, 1, 0).astype(BF16)[None]

    back = dot_exact(coef_in * inv_q[:, None], q_wide, 0, 0)
    pos_grad = (loss_scale * inv_temp) * inv_p[:, None] * back - (
        inv_p * inv_p * loss_scale * jnp.sum(coef_in * s_in, axis=0)
    )[:, None] * pos_wide

    query_hot = (wanted_query[:, :, None] == jnp.arange(Q_GRP)[None, None, :]).astype(BF16)
    askers = lax.dot_general(
        query_hot,
        q_all.reshape(owners, Q_GRP, cols),
        (((2,), (1,)), ((0,), (0,))),
        preferred_element_type=F32,
    ).astype(BF16).reshape(slot_rows, cols)
    row_wide = row_hot.astype(F32)
    weighted = row_wide * got[:, :SLOTS].reshape(slot_rows, 1)
    row_hi, row_lo = split(weighted)
    row_weight = jnp.sum(row_wide * got[:, SLOTS:].reshape(slot_rows, 1), axis=0)
    pool_grad = (
        dot(row_hi, askers, 0, 0)
        + dot(row_lo, askers, 0, 0)
        - row_weight[:, None] * pool.astype(F32)
    )
    return (
        resid_grad,
        attn_grad,
        weight_grad,
        pos_grad.astype(BF16),
        pool_grad.astype(BF16),
    )


def solution(mesh):
    placed = (
        P("dp", "fsdp"),
        P("dp", "fsdp"),
        P("dp", "fsdp"),
        P("dp", None),
        P("dp", None),
        P("dp", "fsdp"),
        P("dp", None),
        P(None, "fsdp"),
        P("fsdp"),
    )
    return jax.shard_map(
        per_device,
        mesh=mesh,
        in_specs=placed,
        out_specs=(
            P("dp", "fsdp"),
            P(("dp", "fsdp"), None),
            P("dp", None, "fsdp"),
            P("dp", "fsdp"),
            P("dp", "fsdp"),
        ),
        check_vma=False,
    )
```

time: 259 us -> 165 us (0.64)
  waiting for transfers between devices: 116 us -> 56.3 us
  blocking collectives: 42.8 us -> 0 us
  local copies, waits for them, and re-layouts: 38.9 us -> 9.15 us
  starting transfers between devices: 15.5 us -> 42 us
  matrix products: 19.6 us -> 31.2 us
    all_to_all x2 -> x3, waiting for transfers between devices: 116 us -> 29.9 us  [the longest x1 21 us: per_device(): lax.all_to_all(fetched, 'dp', split_axis=0, concat_axis=0, tiled=True)]
    ppermute x0 -> x12, waiting for transfers between devices: none -> 25.7 us  [shifted(): lax.ppermute(value, 'fsdp', [(i, (i + step) % N_FS) for i in range(N_FS)])]
    all_to_all x1 -> x0, blocking collectives: 22.1 us -> none  [per_device(): lax.all_to_all(request_ids, 'dp', split_axis=0, concat_axis=0, tiled=True)]
    psum x2 -> x0, blocking collectives: 20.7 us -> none  [feature_sum(): return lax.psum(values, 'fsdp')]
    ppermute x0 -> x12, starting transfers between devices: none -> 15.1 us  [shifted(): lax.ppermute(value, 'fsdp', [(i, (i + step) % N_FS) for i in range(N_FS)])]
    dot_general x9 -> x20, matrix products: 19.6 us -> 31.2 us  [the longest x16 24.5 us: dot(): lax.dot_general(a, b, (((ca,), (cb,)), ((), ())), preferred_element_type=...]
    reshape x7 -> x4, local copies, waits for them, and re-layouts: 12.9 us -> 1.44 us  [the longest x1 0.65 us: per_device(): jnp.repeat(scale_dir, QLEN)]
    all_to_all x2 -> x3, starting transfers between devices: 15.5 us -> 26.8 us  [the longest x1 13 us: per_device(): wanted = lax.all_to_all(code, 'dp', split_axis=0, concat_axis=0, tiled=True)]
  transfers between devices with their start and end apart: 3 -> 16, of which waited for: 2 -> 8; matrix products, arithmetic and copies ran while one was open for 13% -> 26% of each run, Pallas kernels for 0% -> 0%
where the time goes in v1:
time: 165 us; the launch traced here: 163 us
  waiting for transfers between devices  56.3 us (34%)
  starting transfers between devices  42 us (25%)
  matrix products  31.2 us (19%)
  between operations  14.6 us (9%)
  other arithmetic  10.1 us (6%)
  local copies, waits for them, and re-layouts  9.15 us (6%)
    ppermute x12, waiting for transfers between devices, shifted(): lax.ppermute(value, 'fsdp', [(i, (i + step) % N_FS) for i in range(N_FS)])  25.7 us
    dot_general x16, matrix products, dot(): lax.dot_general(a, b, (((ca,), (cb,)), ((), ())), preferred_element_type=...  24.5 us
    all_to_all x1, waiting for transfers between devices, per_device(): lax.all_to_all(fetched, 'dp', split_axis=0, concat_axis=0, tiled=True)  21 us
    ppermute x12, starting transfers between devices, shifted(): lax.ppermute(value, 'fsdp', [(i, (i + step) % N_FS) for i in range(N_FS)])  15.1 us
    all_to_all x1, starting transfers between devices, per_device(): wanted = lax.all_to_all(code, 'dp', split_axis=0, concat_axis=0, tiled=True)  13 us
    all_to_all x1, waiting for transfers between devices, per_device(): wanted = lax.all_to_all(code, 'dp', split_axis=0, concat_axis=0, tiled=True)  8.95 us
    all_to_all x1, starting transfers between devices, per_device(): got = lax.all_to_all(sent, 'dp', split_axis=0, concat_axis=0, tiled=True)  8.09 us
    all_to_all x1, starting transfers between devices, per_device(): lax.all_to_all(fetched, 'dp', split_axis=0, concat_axis=0, tiled=True)  5.72 us
  transfers between devices with their start and end apart: 16, of which 8 were waited for; matrix products, arithmetic and copies ran while one was open for 26% of the time, Pallas kernels for 0%

profile of v1, /device:TPU:1, one launch (start us, length us, event | category | flops | bytes accessed | tf_op | source)
XLA Modules:
  0.0 163.4 jit_solution(12876683737083785161)
XLA Ops:
  7.2 0.7 all-gather.2.cloned.1.call-update
  8.0 0.8 eq.118
  9.0 0.7 fusion.76
  10.0 0.7 copy.26
  10.7 13.0 %all-to-all-start = ((s32[64,1,16]{2,1,0:T(1,128)}), s32[64,1,16]{2,1,0:T(1,128)S(1)}, u32[]{:S(2)}, u32[]{:S(2)}) async-start(s32[64,1,16]{2,1,0:T(1,128)} %copy.26), calls=%async_computation | async-start | bytes 65536 | tf_op jit(solution)/shard_map/all_to_all | solution.py:82
  23.9 8.9 %all-to-all-done = s32[64,1,16]{2,1,0:T(1,128)S(1)} async-done(((s32[64,1,16]{2,1,0:T(1,128)}), s32[64,1,16]{2,1,0:T(1,128)S(1)}, u32[]{:S(2)}, u32[]{:S(2)}) %all-to-all-start) | async-done | bytes 4128 | tf_op jit(solution)/shard_map/all_to_all | solution.py:82
  33.4 0.7 reduce.8
  34.2 3.0 %convolution_convert_fusion.1 = bf16[1024,1024]{1,0:T(8,128)(2,1)} fusion(bf16[128,1024]{1,0:T(8,128)(2,1)} %param.11, s32[1024]{0:T(1024)S(1)} %fusion.71), kind=kOutput, calls=%fused_computation.5 | convolution fusion | flops 269615104 | bytes 2363392 | tf_op jit(solution)/shard_map/dot_general | solution.py:25
  37.3 5.7 %all-to-all-start.1 = ((bf16[64,16,1024]{2,1,0:T(8,128)(2,1)}), bf16[64,16,1024]{2,1,0:T(8,128)(2,1)}, u32[]{:S(2)}, u32[]{:S(2)}) async-start(bf16[64,16,1024]{2,1,0:T(8,128)(2,1)} %bitcast.3), calls=%async_computation.1 | async-start | bytes 4194304 | tf_op jit(solution)/shard_map/all_to_all | solution.py:87
  43.5 3.7 %multiply_reduce_fusion = (f32[256]{0:T(256)S(1)}, f32[256,1024]{1,0:T(8,128)S(1)}) fusion(bf16[256,2048]{1,0:T(8,128)(2,1)S(1)} %copy-done, bf16[2048,1024]{1,0:T(8,128)(2,1)} %param.16, bf16[256,1024]{1,0:T(8,128)(2,1)S(1)} %copy-done.19), kind=kOutput, calls=%fused_computation.33 | convolution fusion | flops 1074790144 | bytes 6816768 | tf_op jit(solution)/shard_map/dot_general | solution.py:25
  47.8 2.8 %collective-permute-start.1 = (f32[328,128]{1,0:T(8,128)S(1)}, f32[328,128]{1,0:T(8,128)S(1)}, u32[]{:S(2)}, u32[]{:S(2)}) collective-permute-start(f32[328,128]{1,0:T(8,128)S(1)} %pad_maximum_fusion), channel_id=1, source_target_pairs={{0,3},{1,0},{2,1},{3,2},{4,7},{5,4},{6,5},{7,6},{8,11},{9,8},{10,9... | collective-permute-start | bytes 503816 | tf_op jit(solution)/shard_map/ppermute | solution.py:40
  51.0 0.7 collective-permute-start
  51.7 1.3 fusion.33
  53.0 1.3 convolution_add_fusion
  54.3 1.3 copy-done.2
  55.6 1.2 constant_dynamic-slice_fusion.5
  56.8 1.6 collective-permute-start.3
  58.4 1.6 collective-permute-start.5
  60.0 1.1 collective-permute-start.4
  61.1 1.0 collective-permute-done
  62.1 1.0 add_add_fusion.1
  63.2 0.6 multiply_bitcast_fusion
  64.2 0.8 fusion.42
  65.0 7.9 %collective-permute-done.3 = f32[64,2048]{1,0:T(8,128)} collective-permute-done((f32[64,2048]{1,0:T(8,128)}, f32[64,2048]{1,0:T(8,128)}, u32[]{:S(2)}, u32[]{:S(2)}) %collective-permute-start.3) | collective-permute-done | bytes 524320 | tf_op jit(solution)/shard_map/ppermute | solution.py:40
  73.0 10.4 %collective-permute-done.5 = f32[64,2048]{1,0:T(8,128)} collective-permute-done((f32[64,2048]{1,0:T(8,128)}, f32[64,2048]{1,0:T(8,128)}, u32[]{:S(2)}, u32[]{:S(2)}) %collective-permute-start.5) | collective-permute-done | bytes 524320 | tf_op jit(solution)/shard_map/ppermute | solution.py:40
  83.4 1.5 add_add_fusion
  84.9 21.0 %all-to-all-done.1 = bf16[64,16,1024]{2,1,0:T(8,128)(2,1)} async-done(((bf16[64,16,1024]{2,1,0:T(8,128)(2,1)}), bf16[64,16,1024]{2,1,0:T(8,128)(2,1)}, u32[]{:S(2)}, u32[]{:S(2)}) %all-to-all-start.1) | async-done | bytes 2097184 | tf_op jit(solution)/shard_map/all_to_all | solution.py:87
  106.0 3.8 %fusion.1 = (f32[448]{0:T(512)S(1)}, f32[448]{0:T(512)S(1)}, bf16[448,1024]{1,0:T(8,128)(2,1)}) fusion(f32[448,1024]{1,0:T(8,128)S(1)} %bitcast.72, bf16[1024,1024]{1,0:T(8,128)(2,1)} %bitcast.6, s32[448]{0:T(512)S(1)} %multiply_add_fusion), kind=kOutput, calls=%fused_computation.7 | convolution fusion | flops 942734464 | bytes 4855040 | tf_op jit(solution)/shard_map/dot_general | solution.py:25
  110.0 1.0 slice.96
  111.8 2.8 %collective-permute-start.8 = (f32[44,64]{1,0:T(8,128)S(1)}, f32[44,64]{1,0:T(8,128)S(1)}, u32[]{:S(2)}, u32[]{:S(2)}) collective-permute-start(f32[44,64]{1,0:T(8,128)S(1)} %concatenate.25), channel_id=1, source_target_pairs={{0,2},{1,3},{2,0},{3,1},{4,6},{5,7},{6,4},{7,5},{8,10},{9,11},{10,... | collective-permute-start | bytes 33800 | tf_op jit(solution)/shard_map/ppermute | solution.py:40
  114.6 0.9 collective-permute-start.7
  117.3 2.2 %collective-permute-done.6 = f32[44,64]{1,0:T(8,128)S(1)} collective-permute-done((f32[44,64]{1,0:T(8,128)S(1)}, f32[44,64]{1,0:T(8,128)S(1)}, u32[]{:S(2)}, u32[]{:S(2)}) %collective-permute-start.6) | collective-permute-done | bytes 11296 | tf_op jit(solution)/shard_map/ppermute | solution.py:40
  119.7 0.6 fusion.85
  120.3 0.6 fusion.38
  121.0 0.6 reshape.265
  121.7 0.6 reshape.268
  122.6 0.8 fusion.43
  123.5 8.1 %all-to-all-start.2 = ((f32[64,1,32]{2,1,0:T(1,128)}), f32[64,1,32]{2,1,0:T(1,128)S(1)}, u32[]{:S(2)}, u32[]{:S(2)}) async-start(f32[64,1,32]{2,1,0:T(1,128)} %bitcast.23), calls=%async_computation.2 | async-start | bytes 65536 | tf_op jit(solution)/shard_map/all_to_all | solution.py:184
  131.6 1.1 multiply_reduce_fusion.1
  132.9 3.5 %fusion.45 = f32[32,2048]{1,0:T(8,128)S(1)} fusion(bf16[2048,1024]{1,0:T(8,128)(2,1)} %param.16, bf16[16,1024]{1,0:T(8,128)(2,1)S(1)} %get-tuple-element.29, bf16[16,1024]{1,0:T(8,128)(2,1)S(1)} %get-tuple-element.30), kind=kOutput, calls=%fused_computation.83 | convolution fusion | flops 134348800 | bytes 4521984 | tf_op jit(solution)/shard_map/dot_general | solution.py:25
  136.6 2.7 %collective-permute-start.10 = (f32[4,2048]{1,0:T(4,128)S(1)}, f32[4,2048]{1,0:T(4,128)S(1)}, u32[]{:S(2)}, u32[]{:S(2)}) collective-permute-start(f32[4,2048]{1,0:T(4,128)S(1)} %get-tuple-element.41), channel_id=1, source_target_pairs={{0,3},{1,0},{2,1},{3,2},{4,7},{5,4},{6,5},{7,6},{8,11},{9,8},{10,9... | collective-permute-start | bytes 98312 | tf_op jit(solution)/shard_map/ppermute | solution.py:40
  139.6 3.3 %convert_bitcast_fusion = bf16[1,2048,1024]{2,1,0:T(8,128)(2,1)} fusion(bf16[2048,256]{0,1:T(8,128)(2,1)S(1)} %bitcast.66, bf16[256,1024]{1,0:T(8,128)(2,1)S(1)} %fusion.14), kind=kOutput, calls=%fused_computation | convolution fusion | flops 1075838976 | bytes 5767168 | tf_op jit(solution)/shard_map/dot_general | solution.py:25
  142.9 1.0 fusion.7
  144.7 3.7 %collective-permute-done.11 = f32[4,2048]{1,0:T(4,128)S(1)} collective-permute-done((f32[4,2048]{1,0:T(4,128)S(1)}, f32[4,2048]{1,0:T(4,128)S(1)}, u32[]{:S(2)}, u32[]{:S(2)}) %collective-permute-start.11) | collective-permute-done | bytes 32800 | tf_op jit(solution)/shard_map/ppermute | solution.py:40
  148.4 0.8 fusion.21
  149.2 4.6 %convolution_convert_fusion = bf16[64,16,1024]{2,1,0:T(8,128)(2,1)S(1)} fusion(bf16[64,64,1024]{2,1,0:T(8,128)(2,1)} %bitcast.69, s32[64,16]{1,0:T(8,128)S(1)} %copy.30), kind=kOutput, calls=%fused_computation.4 | convolution fusion | flops 135331840 | bytes 10489856 | tf_op jit(solution)/shard_map/dot_general | solution.py:226
  153.9 1.0 fusion.25
  154.9 1.7 %fusion.5 = bf16[128,1024]{1,0:T(8,128)(2,1)} fusion(f32[128,1024]{1,0:T(8,128)S(1)} %fusion.25, bf16[1024,1024]{1,0:T(8,128)(2,1)S(1)} %bitcast.68, bf16[128,1024]{1,0:T(8,128)(2,1)S(1)} %copy-done.5, f32[128]{0:T(128)S(1)} %fusion.19, f32[1024]{0:T(1024)S(1)} %mul.515, s32[1024]{0:T(1024)S(1)} %fusion.71), kind=kOutput, calls=%fused_computation.14 | convolution fusion | flops 270139392 | bytes 3154432 | tf_op jit(solution)/shard_map/dot_general | solution.py:25
  (124 shorter events, 8.3 us)
Async XLA Ops:
  7.2 36.2 %copy-start = (bf16[256,2048]{1,0:T(8,128)(2,1)S(1)}, bf16[256,2048]{1,0:T(8,128)(2,1)}, u32[]{:S(2)}) copy-start(bf16[256,2048]{1,0:T(8,128)(2,1)} %param.15) | copy-start | bytes 3145732
  7.2 142.0 %all-gather.2.cloned.1.call-start = ((), (), s32[]{:S(2)}) async-start(), calls=%async_computation.3 | async-start | bytes 8519680 | tf_op jit(solution)/shard_map/all_gather | solution.py:64
  10.7 22.2 %all-to-all-start = ((s32[64,1,16]{2,1,0:T(1,128)}), s32[64,1,16]{2,1,0:T(1,128)S(1)}, u32[]{:S(2)}, u32[]{:S(2)}) async-start(s32[64,1,16]{2,1,0:T(1,128)} %copy.26), calls=%async_computation | async-start | bytes 65536 | tf_op jit(solution)/shard_map/all_to_all | solution.py:82
  37.3 5.7 %copy-start.4 = (bf16[64,1024]{1,0:T(8,128)(2,1)S(1)}, bf16[64,1024]{1,0:T(8,128)(2,1)}, u32[]{:S(2)}) copy-start(bf16[64,1024]{1,0:T(8,128)(2,1)} %param.10) | copy-start | bytes 393220
  37.3 5.9 %copy-start.3 = (bf16[64,1024]{1,0:T(8,128)(2,1)S(1)}, bf16[64,1024]{1,0:T(8,128)(2,1)}, u32[]{:S(2)}) copy-start(bf16[64,1024]{1,0:T(8,128)(2,1)} %param.9) | copy-start | bytes 393220
  37.3 6.2 %copy-start.19 = (bf16[256,1024]{1,0:T(8,128)(2,1)S(1)}, bf16[256,1024]{1,0:T(8,128)(2,1)}, u32[]{:S(2)}) copy-start(bf16[256,1024]{1,0:T(8,128)(2,1)} %param.14) | copy-start | bytes 1572868
  37.3 68.6 %all-to-all-start.1 = ((bf16[64,16,1024]{2,1,0:T(8,128)(2,1)}), bf16[64,16,1024]{2,1,0:T(8,128)(2,1)}, u32[]{:S(2)}, u32[]{:S(2)}) async-start(bf16[64,16,1024]{2,1,0:T(8,128)(2,1)} %bitcast.3), calls=%async_computation.1 | async-start | bytes 4194304 | tf_op jit(solution)/shard_map/all_to_all | solution.py:87
  43.4 3.7 %copy-start.7 = (f32[1024]{0:T(1024)S(1)}, f32[1024]{0:T(1024)}, u32[]{:S(2)}) copy-start(f32[1024]{0:T(1024)} %param.17) | copy-start | bytes 12292
  43.4 8.3 %copy-start.1 = (bf16[2048,1024]{1,0:T(8,128)(2,1)S(1)}, bf16[2048,1024]{1,0:T(8,128)(2,1)}, u32[]{:S(2)}) copy-start(bf16[2048,1024]{1,0:T(8,128)(2,1)} %param.16) | copy-start | bytes 12582916
  47.8 12.2 %collective-permute-start.1 = (f32[328,128]{1,0:T(8,128)S(1)}, f32[328,128]{1,0:T(8,128)S(1)}, u32[]{:S(2)}, u32[]{:S(2)}) collective-permute-start(f32[328,128]{1,0:T(8,128)S(1)} %pad_maximum_fusion), channel_id=1, source_target_pairs={{0,3},{1,0},{2,1},{3,2},{4,7},{5,4},{6,5},{7,6},{8,11},{9,8},{10,9... | collective-permute-start | bytes 503816 | tf_op jit(solution)/shard_map/ppermute | solution.py:40
  50.7 10.4 %collective-permute-start.2 = (f32[328,128]{1,0:T(8,128)S(1)}, f32[328,128]{1,0:T(8,128)S(1)}, u32[]{:S(2)}, u32[]{:S(2)}) collective-permute-start(f32[328,128]{1,0:T(8,128)S(1)} %pad_maximum_fusion), channel_id=1, source_target_pairs={{0,2},{1,3},{2,0},{3,1},{4,6},{5,7},{6,4},{7,5},{8,10},{9,11},{10,... | collective-permute-start | bytes 503816 | tf_op jit(solution)/shard_map/ppermute | solution.py:40
  51.0 11.1 %collective-permute-start = (f32[328,128]{1,0:T(8,128)S(1)}, f32[328,128]{1,0:T(8,128)}, u32[]{:S(2)}, u32[]{:S(2)}) collective-permute-start(f32[328,128]{1,0:T(8,128)S(1)} %pad_maximum_fusion), channel_id=1, source_target_pairs={{0,1},{1,2},{2,3},{3,0},{4,5},{5,6},{6,7},{7,4},{8,9},{9,10},{10,1... | collective-permute-start | bytes 503816 | tf_op jit(solution)/shard_map/ppermute | solution.py:40
  54.3 1.3 copy-start.2
  56.8 16.2 %collective-permute-start.3 = (f32[64,2048]{1,0:T(8,128)}, f32[64,2048]{1,0:T(8,128)}, u32[]{:S(2)}, u32[]{:S(2)}) collective-permute-start(f32[64,2048]{1,0:T(8,128)} %get-tuple-element.34), channel_id=1, source_target_pairs={{0,1},{1,2},{2,3},{3,0},{4,5},{5,6},{6,7},{7,4},{8,9},{9,10},{10,1... | collective-permute-start | bytes 1572872 | tf_op jit(solution)/shard_map/ppermute | solution.py:40
  58.4 25.0 %collective-permute-start.5 = (f32[64,2048]{1,0:T(8,128)}, f32[64,2048]{1,0:T(8,128)}, u32[]{:S(2)}, u32[]{:S(2)}) collective-permute-start(f32[64,2048]{1,0:T(8,128)} %get-tuple-element.35), channel_id=1, source_target_pairs={{0,2},{1,3},{2,0},{3,1},{4,6},{5,7},{6,4},{7,5},{8,10},{9,11},{10,... | collective-permute-start | bytes 1572872 | tf_op jit(solution)/shard_map/ppermute | solution.py:40
  60.0 23.4 %collective-permute-start.4 = (f32[64,2048]{1,0:T(8,128)}, f32[64,2048]{1,0:T(8,128)S(1)}, u32[]{:S(2)}, u32[]{:S(2)}) collective-permute-start(f32[64,2048]{1,0:T(8,128)} %get-tuple-element.36), channel_id=1, source_target_pairs={{0,3},{1,0},{2,1},{3,2},{4,7},{5,4},{6,5},{7,6},{8,11},{9,8},{10,9... | collective-permute-start | bytes 1572872 | tf_op jit(solution)/shard_map/ppermute | solution.py:40
  63.8 57.1 %copy-start.8 = (f32[64]{0:T(128)}, f32[64]{0:T(128)S(1)}, u32[]{:S(2)}) copy-start(f32[64]{0:T(128)S(1)} %get-tuple-element.55) | copy-start | bytes 772
  64.2 51.9 %copy-start.10 = (f32[256]{0:T(256)}, f32[256]{0:T(256)S(1)}, u32[]{:S(2)}) copy-start(f32[256]{0:T(256)S(1)} %fusion.41) | copy-start | bytes 3076
  111.8 5.0 %collective-permute-start.8 = (f32[44,64]{1,0:T(8,128)S(1)}, f32[44,64]{1,0:T(8,128)S(1)}, u32[]{:S(2)}, u32[]{:S(2)}) collective-permute-start(f32[44,64]{1,0:T(8,128)S(1)} %concatenate.25), channel_id=1, source_target_pairs={{0,2},{1,3},{2,0},{3,1},{4,6},{5,7},{6,4},{7,5},{8,10},{9,11},{10,... | collective-permute-start | bytes 33800 | tf_op jit(solution)/shard_map/ppermute | solution.py:40
  114.6 2.7 %collective-permute-start.7 = (f32[44,64]{1,0:T(8,128)S(1)}, f32[44,64]{1,0:T(8,128)S(1)}, u32[]{:S(2)}, u32[]{:S(2)}) collective-permute-start(f32[44,64]{1,0:T(8,128)S(1)} %concatenate.25), channel_id=1, source_target_pairs={{0,3},{1,0},{2,1},{3,2},{4,7},{5,4},{6,5},{7,6},{8,11},{9,8},{10,9... | collective-permute-start | bytes 33800 | tf_op jit(solution)/shard_map/ppermute | solution.py:40
  115.5 3.9 %collective-permute-start.6 = (f32[44,64]{1,0:T(8,128)S(1)}, f32[44,64]{1,0:T(8,128)S(1)}, u32[]{:S(2)}, u32[]{:S(2)}) collective-permute-start(f32[44,64]{1,0:T(8,128)S(1)} %concatenate.25), channel_id=1, source_target_pairs={{0,1},{1,2},{2,3},{3,0},{4,5},{5,6},{6,7},{7,4},{8,9},{9,10},{10,1... | collective-permute-start | bytes 33800 | tf_op jit(solution)/shard_map/ppermute | solution.py:40
  123.5 20.6 %all-to-all-start.2 = ((f32[64,1,32]{2,1,0:T(1,128)}), f32[64,1,32]{2,1,0:T(1,128)S(1)}, u32[]{:S(2)}, u32[]{:S(2)}) async-start(f32[64,1,32]{2,1,0:T(1,128)} %bitcast.23), calls=%async_computation.2 | async-start | bytes 65536 | tf_op jit(solution)/shard_map/all_to_all | solution.py:184
  132.8 6.4 %copy-start.11 = (f32[256]{0:T(256)S(1)}, f32[256]{0:T(256)}, u32[]{:S(2)}) copy-start(f32[256]{0:T(256)} %copy-done.10) | copy-start | bytes 3076
  132.8 6.4 %copy-start.12 = (f32[256]{0:T(256)S(1)}, f32[256]{0:T(256)}, u32[]{:S(2)}) copy-start(f32[256]{0:T(256)} %fusion.42) | copy-start | bytes 3076
  132.9 6.4 %copy-start.13 = (f32[256]{0:T(256)S(1)}, f32[256]{0:T(256)}, u32[]{:S(2)}) copy-start(f32[256]{0:T(256)} %fusion.38) | copy-start | bytes 3076
  132.9 6.4 %copy-start.14 = (f32[256]{0:T(256)S(1)}, f32[256]{0:T(256)}, u32[]{:S(2)}) copy-start(f32[256]{0:T(256)} %reshape.265) | copy-start | bytes 3076
  132.9 6.4 %copy-start.15 = (f32[256]{0:T(256)S(1)}, f32[256]{0:T(256)}, u32[]{:S(2)}) copy-start(f32[256]{0:T(256)} %reshape.268) | copy-start | bytes 3076
  136.4 3.1 %copy-start.18 = (f32[64]{0:T(128)S(1)}, f32[64]{0:T(128)}, u32[]{:S(2)}) copy-start(f32[64]{0:T(128)} %get-tuple-element.27) | copy-start | bytes 772
  136.5 8.2 %collective-permute-start.9 = (f32[4,2048]{1,0:T(4,128)S(1)}, f32[4,2048]{1,0:T(4,128)S(1)}, u32[]{:S(2)}, u32[]{:S(2)}) collective-permute-start(f32[4,2048]{1,0:T(4,128)S(1)} %get-tuple-element.39), channel_id=1, source_target_pairs={{0,1},{1,2},{2,3},{3,0},{4,5},{5,6},{6,7},{7,4},{8,9},{9,10},{10,1... | collective-permute-start | bytes 98312 | tf_op jit(solution)/shard_map/ppermute | solution.py:40
  136.6 11.7 %collective-permute-start.10 = (f32[4,2048]{1,0:T(4,128)S(1)}, f32[4,2048]{1,0:T(4,128)S(1)}, u32[]{:S(2)}, u32[]{:S(2)}) collective-permute-start(f32[4,2048]{1,0:T(4,128)S(1)} %get-tuple-element.41), channel_id=1, source_target_pairs={{0,3},{1,0},{2,1},{3,2},{4,7},{5,4},{6,5},{7,6},{8,11},{9,8},{10,9... | collective-permute-start | bytes 98312 | tf_op jit(solution)/shard_map/ppermute | solution.py:40
  139.5 3.4 %copy-start.6 = (bf16[256,1024]{1,0:T(8,128)(2,1)}, bf16[256,1024]{1,0:T(8,128)(2,1)S(1)}, u32[]{:S(2)}) copy-start(bf16[256,1024]{1,0:T(8,128)(2,1)S(1)} %fusion.14) | copy-start | bytes 1572868
  139.5 3.3 %copy-start.9 = (f32[64]{0:T(128)S(1)}, f32[64]{0:T(128)}, u32[]{:S(2)}) copy-start(f32[64]{0:T(128)} %copy-done.8) | copy-start | bytes 772
  139.5 3.3 %copy-start.16 = (f32[64]{0:T(128)S(1)}, f32[64]{0:T(128)}, u32[]{:S(2)}) copy-start(f32[64]{0:T(128)} %get-tuple-element.37) | copy-start | bytes 772
  139.5 8.8 %copy-start.17 = (f32[64]{0:T(128)S(1)}, f32[64]{0:T(128)}, u32[]{:S(2)}) copy-start(f32[64]{0:T(128)} %dynamic_slice.34) | copy-start | bytes 772
  144.0 4.3 %collective-permute-start.11 = (f32[4,2048]{1,0:T(4,128)S(1)}, f32[4,2048]{1,0:T(4,128)S(1)}, u32[]{:S(2)}, u32[]{:S(2)}) collective-permute-start(f32[4,2048]{1,0:T(4,128)S(1)} %get-tuple-element.40), channel_id=1, source_target_pairs={{0,2},{1,3},{2,0},{3,1},{4,6},{5,7},{6,4},{7,5},{8,10},{9,11},{10,... | collective-permute-start | bytes 98312 | tf_op jit(solution)/shard_map/ppermute | solution.py:40
  153.8 1.0 copy-start.5
Sparse Core Ops, SparseCore 0:
  10.8 106.7 all-gather.1

commit v2 on v1

v2 whole, which is shorter than its diff:
```python
import jax
import jax.numpy as jnp
from jax import lax
from jax.experimental import pallas as pl
from jax.experimental.pallas import tpu as pltpu
from jax.sharding import PartitionSpec as P

D = 4096
NEG = 7
QLEN = 16
Q_GRP = 64
CH_Q = 16
POOL_GRP = 128
SLOTS = 14
WIDE = 16
SUB = 8
LANES = 128
VMEM_LIMIT = 24 * 1024 * 1024
N_FS = 4


inv_temp = 1.0 / 0.05
loss_scale = 32.0
rep_epsilon = 1e-06
norm_epsilon = 1e-05
F32 = jnp.float32
BF16 = jnp.bfloat16


def dot(a, b, ca, cb):
    return lax.dot_general(a, b, (((ca,), (cb,)), ((), ())), preferred_element_type=F32)


def dot_exact(a, b, ca, cb):
    return lax.dot_general(
        a, b, (((ca,), (cb,)), ((), ())), precision=lax.Precision.HIGHEST, preferred_element_type=F32
    )


def split(a):
    hi = a.astype(BF16)
    return hi, (a - hi.astype(F32)).astype(BF16)


def shifted(value, step):
    return lax.ppermute(value, "fsdp", [(i, (i + step) % N_FS) for i in range(N_FS)])


def swapped(value, mask):
    return lax.ppermute(value, "fsdp", [(i, i ^ mask) for i in range(N_FS)])


def feature_total(rows):
    return rows + shifted(rows, 1) + shifted(rows, 3) + shifted(rows, 2)


def feature_scatter_small(rows):
    own = rows.shape[0] // N_FS
    me = lax.axis_index("fsdp")
    half = me // 2
    mine = lax.dynamic_slice(rows, (half * 2 * own, 0), (2 * own, rows.shape[1]))
    other = lax.dynamic_slice(rows, ((1 - half) * 2 * own, 0), (2 * own, rows.shape[1]))
    mine = mine + swapped(other, 3)
    side = me % 2
    kept = lax.dynamic_slice(mine, (side * own, 0), (own, rows.shape[1]))
    given = lax.dynamic_slice(mine, ((1 - side) * own, 0), (own, rows.shape[1]))
    return kept + swapped(given, 1)


def feature_scatter(rows):
    own = rows.shape[0] // N_FS
    me = lax.axis_index("fsdp")
    total = lax.dynamic_slice(rows, (me * own, 0), (own, rows.shape[1]))
    for step in (1, 3, 2):
        there = lax.rem(me + step, N_FS)
        total += shifted(lax.dynamic_slice(rows, (there * own, 0), (own, rows.shape[1])), step)
    return total


def eye_of(rows, cols):
    down = lax.broadcasted_iota(jnp.int32, (rows, cols), 0)
    return (down == lax.broadcasted_iota(jnp.int32, (rows, cols), 1)).astype(F32)


def to_column(row):
    size = row.shape[1]
    return jnp.sum(eye_of(size, size) * row, axis=1, keepdims=True)


def tiled(values, period, times):
    width = period * times
    down = lax.broadcasted_iota(jnp.int32, (period, width), 0)
    along = lax.broadcasted_iota(jnp.int32, (period, width), 1)
    return dot_exact(values, (along % period == down).astype(F32), 1, 0)


def flat_row(values, times):
    rows, period = values.shape
    wide = tiled(values, period, times)
    down = lax.broadcasted_iota(jnp.int32, wide.shape, 0)
    along = lax.broadcasted_iota(jnp.int32, wide.shape, 1)
    return jnp.sum(jnp.where(along // period == down, wide, 0.0), axis=0, keepdims=True)


def request_kernel(name_ref, code_ref, slot_ref, turned_ref, place_ref):
    name = flat_row(name_ref[...].astype(F32), NEG).astype(jnp.int32)
    owner = lax.shift_right_logical(name, 7).astype(F32)
    row = jnp.bitwise_and(name, 127).astype(F32)
    requests = owner.shape[1]
    peers = turned_ref.shape[0]
    along = lax.broadcasted_iota(jnp.int32, (1, requests), 1)
    down = lax.broadcasted_iota(jnp.int32, (peers, requests), 0)
    hot = jnp.where(down == owner.astype(jnp.int32), 1.0, 0.0)
    turned = hot.astype(BF16)
    earlier = lax.broadcasted_iota(jnp.int32, (requests, requests), 0) < along
    before = dot(turned, jnp.where(earlier, 1.0, 0.0).astype(BF16), 1, 0)
    position = jnp.sum(hot * before, axis=0, keepdims=True)
    down = lax.broadcasted_iota(jnp.int32, (WIDE, requests), 0)
    place = jnp.where(down == position.astype(jnp.int32), 1.0, 0.0)
    query = (along % Q_GRP + 1).astype(F32)
    marks = jnp.concatenate([place * row, place * query], axis=0).astype(BF16)
    table = dot(turned, marks, 1, 1).astype(jnp.int32)
    code_ref[...] = table[:, :WIDE] * 128 + table[:, WIDE:]
    slot_ref[...] = (owner * SLOTS + position).astype(jnp.int32)
    turned_ref[...] = turned
    place_ref[...] = place.astype(BF16)


def request_tables(name, owners):
    requests = name.shape[0] * name.shape[1]
    vmem = pl.BlockSpec(memory_space=pltpu.VMEM)
    return pl.pallas_call(
        request_kernel,
        out_shape=(
            jax.ShapeDtypeStruct((owners, WIDE), jnp.int32),
            jax.ShapeDtypeStruct((1, requests), jnp.int32),
            jax.ShapeDtypeStruct((owners, requests), BF16),
            jax.ShapeDtypeStruct((WIDE, requests), BF16),
        ),
        in_specs=[vmem],
        out_specs=(vmem,) * 4,
        compiler_params=pltpu.CompilerParams(vmem_limit_bytes=VMEM_LIMIT),
        cost_estimate=pl.CostEstimate(flops=30000000, bytes_accessed=100000, transcendentals=0),
    )(name)


def fetch_kernel(code_ref, pool_ref, out_ref):
    @pl.loop(0, out_ref.shape[0])
    def _(peer):
        for place in range(SLOTS):
            out_ref[peer, place] = pool_ref[lax.shift_right_logical(code_ref[peer, place], 7)]


def fetch_rows(code, pool_tiles):
    peers = code.shape[0]
    return pl.pallas_call(
        fetch_kernel,
        out_shape=jax.ShapeDtypeStruct((peers, SLOTS, SUB, LANES), BF16),
        in_specs=[
            pl.BlockSpec(memory_space=pltpu.SMEM),
            pl.BlockSpec(memory_space=pltpu.VMEM),
        ],
        out_specs=pl.BlockSpec(memory_space=pltpu.VMEM),
        compiler_params=pltpu.CompilerParams(vmem_limit_bytes=VMEM_LIMIT),
        cost_estimate=pl.CostEstimate(flops=0, bytes_accessed=2 * 1835008, transcendentals=0),
    )(code, pool_tiles)


def row_sums_kernel(slot_ref, reply_ref, q_ref, sums_ref, first_ref, cos_ref, sq_ref):
    last = reply_ref.shape[0] - 1

    def one(query, keep):
        asked = q_ref[query].astype(F32)
        for k in range(NEG):
            row = reply_ref[jnp.clip(slot_ref[0, k * Q_GRP + query], 0, last)]
            if keep:
                first_ref[k * CH_Q + query] = row
            wide = row.astype(F32)
            at = pl.ds(k * Q_GRP + query, 1)
            cos_ref[at, :] = jnp.sum(wide * asked, axis=0, keepdims=True)
            sq_ref[at, :] = jnp.sum(wide * wide, axis=0, keepdims=True)

    pl.loop(0, CH_Q)(lambda query: one(query, True))
    pl.loop(CH_Q, Q_GRP)(lambda query: one(query, False))

    line = lax.broadcasted_iota(jnp.int32, (SUB, LANES), 0)
    for part, ref in ((0, cos_ref), (1, sq_ref)):
        total = jnp.zeros((SUB, Q_GRP), F32)
        for k in range(NEG):
            total += dot_exact((line == k).astype(F32), ref[k * Q_GRP : (k + 1) * Q_GRP, :], 1, 1)
        sums_ref[part * SUB : (part + 1) * SUB, :] = total


def row_sums(slot, replies, q_tiles):
    return pl.pallas_call(
        row_sums_kernel,
        out_shape=(
            jax.ShapeDtypeStruct((2 * SUB, Q_GRP), F32),
            jax.ShapeDtypeStruct((NEG * CH_Q, SUB, LANES), BF16),
        ),
        in_specs=[
            pl.BlockSpec(memory_space=pltpu.SMEM),
            pl.BlockSpec(memory_space=pltpu.VMEM),
            pl.BlockSpec(memory_space=pltpu.VMEM),
        ],
        out_specs=(
            pl.BlockSpec(memory_space=pltpu.VMEM),
            pl.BlockSpec(memory_space=pltpu.VMEM),
        ),
        scratch_shapes=[
            pltpu.VMEM((NEG * Q_GRP, LANES), F32),
            pltpu.VMEM((NEG * Q_GRP, LANES), F32),
        ],
        compiler_params=pltpu.CompilerParams(vmem_limit_bytes=VMEM_LIMIT),
        cost_estimate=pl.CostEstimate(flops=2000000, bytes_accessed=2200000, transcendentals=0),
    )(slot, replies, q_tiles)


def soft_kernel(
    late_ref, sum_ref, inv_q_ref, owner_ref, place_ref, sent_ref, coef_ref, logit_ref, inv_n_ref, den_ref
):
    late = late_ref[...]
    inv_q = inv_q_ref[...]
    inv_n = lax.rsqrt(late[:, Q_GRP : 2 * Q_GRP] + rep_epsilon)
    logit = late[:, :Q_GRP] * inv_q * inv_n * inv_temp
    used = lax.broadcasted_iota(jnp.int32, logit.shape, 0) < NEG
    raised = jnp.where(used, jnp.exp(logit), 0.0)
    total = sum_ref[...] + jnp.sum(raised, axis=0, keepdims=True)
    coef = raised / total
    coef_ref[...] = coef
    logit_ref[...] = logit
    inv_n_ref[...] = inv_n
    den_ref[...] = total
    w_q = flat_row(loss_scale * inv_temp * coef * inv_q * inv_n, NEG)
    w_n = flat_row(loss_scale * coef * logit * inv_n * inv_n, NEG)
    owner = owner_ref[...].astype(F32)
    parts = split(owner * w_q) + split(owner * w_n)
    placed = dot(jnp.concatenate(parts, axis=0), place_ref[...], 1, 1)
    peers = owner.shape[0]
    sent_ref[:, :WIDE] = placed[:peers] + placed[peers : 2 * peers]
    sent_ref[:, WIDE:] = placed[2 * peers : 3 * peers] + placed[3 * peers :]


def soft(late, sum_in, inv_q, owner_turned, place_hot):
    small = jax.ShapeDtypeStruct((SUB, Q_GRP), F32)
    vmem = pl.BlockSpec(memory_space=pltpu.VMEM)
    return pl.pallas_call(
        soft_kernel,
        out_shape=(
            jax.ShapeDtypeStruct((owner_turned.shape[0], 2 * WIDE), F32),
            small,
            small,
            small,
            jax.ShapeDtypeStruct((1, Q_GRP), F32),
        ),
        in_specs=[vmem] * 5,
        out_specs=(vmem,) * 5,
        compiler_params=pltpu.CompilerParams(vmem_limit_bytes=VMEM_LIMIT),
        cost_estimate=pl.CostEstimate(flops=8000000, bytes_accessed=100000, transcendentals=512),
    )(late, sum_in, inv_q, owner_turned, place_hot)


def grads_kernel(
    late_ref, coef_ref, logit_ref, inv_n_ref, den_ref, exp_ref, s_ref, inv_q_ref, inv_p_ref,
    rms_ref, scaled_pos_ref, scaled_q_ref, gain_ref, q_ref, pos_ref, negs_ref,
    gained_ref, halves_ref, shrink_ref, pos_grad_ref,
):
    eye = eye_of(Q_GRP, Q_GRP)
    inv_q_row = inv_q_ref[...]
    inv_p_row = inv_p_ref[...]
    inv_q = to_column(inv_q_row)
    coef_neg = coef_ref[...]
    coef_in = exp_ref[...] / to_column(den_ref[...]) - eye
    product = coef_in * s_ref[...]
    neg_dot = jnp.sum(coef_neg * logit_ref[...], axis=0, keepdims=True)
    self_dot = loss_scale * (jnp.sum(product, axis=1, keepdims=True) + to_column(neg_dot))
    scale_dir = loss_scale * inv_temp / QLEN * inv_q
    scale_own = inv_q * inv_q * self_dot * (1.0 / QLEN)
    of_pos = (coef_in * inv_p_row * scale_dir)[:CH_Q]
    neg_part = (coef_neg * inv_n_ref[...] * (loss_scale * inv_temp / QLEN) * inv_q_row)[:, :CH_Q]
    neg_row = flat_row(neg_part, NEG)
    down = lax.broadcasted_iota(jnp.int32, (CH_Q, NEG * CH_Q), 0)
    along = lax.broadcasted_iota(jnp.int32, (CH_Q, NEG * CH_Q), 1)
    of_neg = jnp.where(along % CH_Q == down, neg_row, 0.0)
    of_own = -eye[:CH_Q, :CH_Q] * scale_own[:CH_Q]
    both = (
        dot(jnp.concatenate(split(of_pos), axis=0), pos_ref[...], 1, 0)
        + dot(jnp.concatenate(split(of_neg), axis=0), negs_ref[...], 1, 0)
        + dot(jnp.concatenate(split(of_own), axis=0), q_ref[:CH_Q, :], 1, 0)
    )
    gained = (both[:CH_Q] + both[CH_Q:]) * gain_ref[...]
    gained_ref[...] = gained
    high, low = split(gained)
    halves_ref[:CH_Q, :] = high
    halves_ref[CH_Q:, :] = low
    tokens = CH_Q * QLEN
    down = lax.broadcasted_iota(jnp.int32, (CH_Q, tokens), 0)
    mine = lax.broadcasted_iota(jnp.int32, (CH_Q, tokens), 1) // QLEN == down
    inner = dot_exact(of_pos, scaled_pos_ref[...], 1, 0) - scale_own[:CH_Q] * scaled_q_ref[...]
    inner = jnp.sum(jnp.where(mine, inner, 0.0), axis=0, keepdims=True)
    spread = dot_exact(neg_part, mine.astype(F32), 1, 0)
    inner += jnp.sum(spread * late_ref[:, 2 * Q_GRP :], axis=0, keepdims=True)
    rms = rms_ref[...]
    shrink_ref[...] = rms * rms * rms * inner * (1.0 / D)
    back = coef_in * inv_q * (inv_p_row * (loss_scale * inv_temp))
    turned = dot(jnp.concatenate(split(back), axis=1), q_ref[...], 0, 0)
    less = to_column(inv_p_row * inv_p_row * loss_scale * jnp.sum(product, axis=0, keepdims=True))
    pos_grad_ref[...] = (
        turned[:Q_GRP] + turned[Q_GRP:] - less * pos_ref[...].astype(F32)
    ).astype(BF16)


def grads(*operands):
    vmem = pl.BlockSpec(memory_space=pltpu.VMEM)
    cols = operands[-1].shape[1]
    return pl.pallas_call(
        grads_kernel,
        out_shape=(
            jax.ShapeDtypeStruct((CH_Q, cols), F32),
            jax.ShapeDtypeStruct((2 * CH_Q, cols), BF16),
            jax.ShapeDtypeStruct((1, CH_Q * QLEN), F32),
            jax.ShapeDtypeStruct((Q_GRP, cols), BF16),
        ),
        in_specs=[vmem] * len(operands),
        out_specs=(vmem,) * 4,
        compiler_params=pltpu.CompilerParams(vmem_limit_bytes=VMEM_LIMIT),
        cost_estimate=pl.CostEstimate(flops=40000000, bytes_accessed=1000000, transcendentals=0),
    )(*operands)


def weight_kernel(
    hidden_ref, gained_ref, rms_ref, shrink_ref, attn_ref, resid_ref, out_ref, held_ref, tile_ref, sems
):
    rms = to_column(rms_ref[...])
    shrink = to_column(shrink_ref[...])
    for c in range(CH_Q):
        at = slice(c * QLEN, (c + 1) * QLEN)
        held_ref[at, :] = (
            rms[at] * gained_ref[c : c + 1, :] - shrink[at] * hidden_ref[at, :]
        ).astype(BF16)
    blocks, block = tile_ref.shape[0], tile_ref.shape[1]
    copies = [pltpu.make_async_copy(held_ref, resid_ref, sems.at[blocks])]
    copies[0].start()
    for b in range(blocks):
        at = slice(b * block, (b + 1) * block)
        tile_ref[b] = dot(attn_ref[at, :], held_ref[...], 1, 0).astype(BF16)
        copy = pltpu.make_async_copy(tile_ref.at[b], out_ref.at[pl.ds(b * block, block)], sems.at[b])
        copy.start()
        copies.append(copy)
    for copy in copies:
        copy.wait()


def weight_grads(hidden, gained, rms, shrink, attn_turned):
    tokens, cols = hidden.shape
    rows = attn_turned.shape[0]
    blocks = 8
    vmem = pl.BlockSpec(memory_space=pltpu.VMEM)
    anywhere = pl.BlockSpec(memory_space=pl.ANY)
    return pl.pallas_call(
        weight_kernel,
        out_shape=(
            jax.ShapeDtypeStruct((tokens, cols), BF16),
            jax.ShapeDtypeStruct((rows, cols), BF16),
        ),
        in_specs=[vmem] * 5,
        out_specs=(anywhere, anywhere),
        scratch_shapes=[
            pltpu.VMEM((tokens, cols), BF16),
            pltpu.VMEM((blocks, rows // blocks, cols), BF16),
            pltpu.SemaphoreType.DMA((blocks + 1,)),
        ],
        compiler_params=pltpu.CompilerParams(vmem_limit_bytes=VMEM_LIMIT),
        cost_estimate=pl.CostEstimate(
            flops=1100000000, bytes_accessed=7000000, transcendentals=0
        ),
    )(hidden, gained, rms, shrink, attn_turned)


def pool_sum_kernel(code_ref, weight_ref, q_ref, pool_ref, out_ref, spread_ref, held_ref, sems):
    blocks, block = held_ref.shape[0], held_ref.shape[2]
    copies = []
    for b in range(blocks):
        copy = pltpu.make_async_copy(
            q_ref.at[:, pl.ds(b * block, block)], held_ref.at[b], sems.at[b]
        )
        copy.start()
        copies.append(copy)
    group = LANES // WIDE
    steps = code_ref.shape[0] // group

    def lined(values):
        wide = tiled(values, WIDE, group)
        down = lax.broadcasted_iota(jnp.int32, wide.shape, 0)
        along = lax.broadcasted_iota(jnp.int32, wide.shape, 1)
        kept = jnp.where(along // WIDE == down % group, wide, 0.0)
        return jnp.sum(kept.reshape(wide.shape[0] // group, group, LANES), axis=1)

    code = code_ref[...]
    pool_row = lined(lax.shift_right_logical(code, 7).astype(F32)).astype(jnp.int32)
    query = lined(jnp.bitwise_and(code, 127).astype(F32)).astype(jnp.int32)
    peer = lax.broadcasted_iota(jnp.int32, (steps, LANES), 1) // WIDE
    query = jnp.where(query > 0, peer * Q_GRP + query - 1, -1)
    w_q = lined(weight_ref[:, :WIDE])
    w_n = lined(weight_ref[:, WIDE:])
    down = lax.broadcasted_iota(jnp.int32, (POOL_GRP, LANES), 0)
    across = lax.broadcasted_iota(jnp.int32, (group * Q_GRP, LANES), 0)
    own = jnp.zeros((POOL_GRP, LANES), F32)
    for step in range(steps):
        at = slice(step, step + 1)
        hot = down == pool_row[at]
        parts = split(jnp.where(hot, w_q[at], 0.0))
        pick = jnp.where(across == query[at], 1.0, 0.0).astype(BF16)
        spread_ref[:, step * group * Q_GRP : (step + 1) * group * Q_GRP] = dot(
            jnp.concatenate(parts, axis=0), pick, 1, 1
        ).astype(BF16)
        own += jnp.where(hot, w_n[at], 0.0)
    own = jnp.sum(own, axis=1, keepdims=True)
    for b in range(blocks):
        at = slice(b * block, (b + 1) * block)
        copies[b].wait()
        both = dot(spread_ref[...], held_ref[b], 1, 0)
        out_ref[:, at] = (
            both[:POOL_GRP] + both[POOL_GRP:] - own * pool_ref[:, at].astype(F32)
        ).astype(BF16)


def pool_sum(code, weights, q_all, pool):
    vmem = pl.BlockSpec(memory_space=pltpu.VMEM)
    return pl.pallas_call(
        pool_sum_kernel,
        out_shape=jax.ShapeDtypeStruct(pool.shape, BF16),
        in_specs=[vmem, vmem, pl.BlockSpec(memory_space=pl.ANY), vmem],
        out_specs=vmem,
        scratch_shapes=[
            pltpu.VMEM((2 * POOL_GRP, q_all.shape[0]), BF16),
            pltpu.VMEM((4, q_all.shape[0], pool.shape[1] // 4), BF16),
            pltpu.SemaphoreType.DMA((4,)),
        ],
        compiler_params=pltpu.CompilerParams(vmem_limit_bytes=60 * 1024 * 1024),
        cost_estimate=pl.CostEstimate(
            flops=2500000000, bytes_accessed=9000000, transcendentals=0
        ),
    )(code, weights, q_all, pool)


def per_device(q, pos, pool, neg_owner, neg_row, resid_in, attn_out, out_weight, norm_gain):
    owners = lax.axis_size("dp")
    cols = q.shape[1]
    tokens = resid_in.shape[0]

    q_all = lax.all_gather(q, "dp", tiled=True)

    code, slot, owner_turned, place_hot = request_tables(
        neg_owner.T * POOL_GRP + neg_row.T, owners
    )
    wanted = lax.all_to_all(code, "dp", split_axis=0, concat_axis=0, tiled=True)
    pool_tiles = pool.reshape(POOL_GRP, SUB, LANES)
    fetched = fetch_rows(wanted, pool_tiles).reshape(owners, SLOTS * SUB, LANES)
    replies = lax.all_to_all(fetched, "dp", split_axis=0, concat_axis=0, tiled=True)

    fetched, q, pos, resid_in, attn_out = lax.optimization_barrier(
        (fetched, q, pos, resid_in, attn_out)
    )
    attn_turned = attn_out.T
    hidden = resid_in.astype(F32) + dot(attn_out, out_weight, 1, 0)
    hid_hi, hid_lo = split(hidden)
    scaled = jnp.concatenate(split(hidden * norm_gain[None, :]), axis=0)
    both = jnp.concatenate([pos, q], axis=0)
    scaled_dots = dot(jnp.concatenate([pos, q[:CH_Q]], axis=0), scaled, 1, 1)
    early = feature_total(
        jnp.concatenate(
            [
                scaled_dots[:, :tokens] + scaled_dots[:, tokens:],
                jnp.concatenate([dot(q, both, 1, 1), dot(pos, both, 1, 1)], axis=1),
                jnp.broadcast_to(jnp.sum(hidden * hidden, axis=1)[None, :], (8, tokens)),
            ],
            axis=0,
        )
    )
    hidden_back = feature_scatter(dot(hid_hi, out_weight, 1, 1) + dot(hid_lo, out_weight, 1, 1))
    eye = jnp.eye(Q_GRP, dtype=F32)
    scaled_pos = early[:Q_GRP]
    mine = jnp.arange(CH_Q)[:, None] == (jnp.arange(tokens) // QLEN)[None, :]
    scaled_q = jnp.sum(jnp.where(mine, early[Q_GRP : Q_GRP + CH_Q], 0.0), axis=0)[None, :]
    pairs = early[Q_GRP + CH_Q : 2 * Q_GRP + CH_Q]
    q_sq = jnp.sum(pairs[:, Q_GRP : 2 * Q_GRP] * eye, axis=0)
    p_sq = jnp.sum(pairs[:, 2 * Q_GRP : 3 * Q_GRP] * eye, axis=0)
    h_sq = early[2 * Q_GRP + CH_Q]
    inv_q = lax.rsqrt(q_sq + rep_epsilon)
    inv_p = lax.rsqrt(p_sq + rep_epsilon)
    inv_rms = lax.rsqrt(h_sq / D + norm_epsilon)
    s_in = pairs[:, :Q_GRP] * inv_q[:, None] * inv_p[None, :] * inv_temp
    exp_in = jnp.exp(s_in)
    sum_in = jnp.sum(exp_in, axis=1)[None, :]
    inv_q_row = inv_q[None, :]
    inv_p_row = inv_p[None, :]
    rms_row = inv_rms[None, :]
    (
        replies, sum_in, inv_q_row, inv_p_row, rms_row, scaled, scaled_pos, scaled_q,
        attn_turned, hidden_back, exp_in, s_in, hidden,
    ) = lax.optimization_barrier(
        (
            replies, sum_in, inv_q_row, inv_p_row, rms_row, scaled, scaled_pos,
            scaled_q, attn_turned, hidden_back, exp_in, s_in, hidden,
        )
    )

    sums, first_negs = row_sums(
        slot, replies.reshape(owners * SLOTS, SUB, LANES), q.reshape(Q_GRP, SUB, LANES)
    )
    first_negs = first_negs.reshape(NEG * CH_Q, cols)
    scaled_negs = dot(first_negs, scaled, 1, 1)
    scaled_negs = (scaled_negs[:, :tokens] + scaled_negs[:, tokens:]).reshape(NEG, CH_Q, tokens)
    scaled_negs = jnp.sum(jnp.where(mine[None], scaled_negs, 0.0), axis=1)
    late = feature_total(
        jnp.concatenate(
            [sums[:SUB], sums[SUB:], jnp.concatenate([scaled_negs, jnp.zeros((1, tokens), F32)])],
            axis=1,
        )
    )
    sent, coef_neg, s_neg, inv_n, denominator = soft(
        late, sum_in, inv_q_row, owner_turned, place_hot
    )
    got = lax.all_to_all(sent, "dp", split_axis=0, concat_axis=0, tiled=True)

    gained, halves, shrink, pos_grad = grads(
        late, coef_neg, s_neg, inv_n, denominator, exp_in, s_in, inv_q_row, inv_p_row, rms_row,
        scaled_pos, scaled_q, norm_gain[None, :], q, pos, first_negs,
    )
    gained_back = dot(halves, out_weight, 1, 1)
    gained_back = feature_scatter_small(gained_back[:CH_Q] + gained_back[CH_Q:])
    resid_grad, weight_grad = weight_grads(hidden, gained, rms_row, shrink, attn_turned)
    own = tokens // N_FS
    first = lax.axis_index("fsdp") * own
    own_rms = lax.dynamic_slice(rms_row[0], (first,), (own,))
    own_shrink = lax.dynamic_slice(shrink[0], (first,), (own,))
    gained_rows = jnp.broadcast_to(
        gained_back[:, None, :], (CH_Q // N_FS, QLEN, gained_back.shape[1])
    ).reshape(own, gained_back.shape[1])
    attn_grad = (own_rms[:, None] * gained_rows - own_shrink[:, None] * hidden_back).astype(BF16)
    pool_grad = pool_sum(wanted, got, q_all, pool)
    return (
        resid_grad,
        attn_grad,
        weight_grad[None],
        pos_grad,
        pool_grad,
    )


def solution(mesh):
    placed = (
        P("dp", "fsdp"),
        P("dp", "fsdp"),
        P("dp", "fsdp"),
        P("dp", None),
        P("dp", None),
        P("dp", "fsdp"),
        P("dp", None),
        P(None, "fsdp"),
        P("fsdp"),
    )
    return jax.shard_map(
        per_device,
        mesh=mesh,
        in_specs=placed,
        out_specs=(
            P("dp", "fsdp"),
            P(("dp", "fsdp"), None),
            P("dp", None, "fsdp"),
            P("dp", "fsdp"),
            P("dp", "fsdp"),
        ),
        check_vma=False,
    )
```

time: 165 us -> 145 us (0.88)
  matrix products: 31.2 us -> 9.55 us
  Pallas kernels: 0 us -> 20.2 us
  waiting for transfers between devices: 56.3 us -> 44.4 us
  starting transfers between devices: 42 us -> 39.4 us
  other arithmetic: 10.1 us -> 8.22 us
    pallas_call x0 -> x7, Pallas kernels: none -> 20.2 us  [the longest x1 8.24 us: pool_sum(): pl.pallas_call(pool_sum_kernel, out_shape=jax.ShapeDtypeStruct(pool.shape...]
    dot_general x16 -> x8, matrix products: 24.5 us -> 9.55 us  [dot(): lax.dot_general(a, b, (((ca,), (cb,)), ((), ())), preferred_element_type=...]
    all_to_all x1, waiting for transfers between devices: 21 us -> 10 us  [per_device(): lax.all_to_all(fetched, 'dp', split_axis=0, concat_axis=0, tiled=True)]
    dot_general x4 -> x0, matrix products: 6.69 us -> none  [the longest x1 4.64 us: per_device(): lax.dot_general(query_hot, q_all.reshape(owners, Q_GRP, cols), (((2,), (1...]
    ppermute x12 -> x9, waiting for transfers between devices: 25.7 us -> 20.1 us  [shifted(): lax.ppermute(value, 'fsdp', [(i, (i + step) % N_FS) for i in range(N_FS)])]
    all_to_all x1, waiting for transfers between devices: 0.01 us -> 5.07 us  [per_device(): got = lax.all_to_all(sent, 'dp', split_axis=0, concat_axis=0, tiled=True)]
    reduce_sum x11 -> x4, other arithmetic: 4.11 us -> 0.26 us  [the longest x1 0.11 us: per_device(): sum_in = jnp.sum(exp_in, axis=1)[None, :]]
    ppermute x12 -> x9, starting transfers between devices: 15.1 us -> 11.8 us  [shifted(): lax.ppermute(value, 'fsdp', [(i, (i + step) % N_FS) for i in range(N_FS)])]
  transfers between devices with their start and end apart: 16 -> 15, of which waited for: 8 -> 7; matrix products, arithmetic and copies ran while one was open for 26% -> 16% of each run, Pallas kernels for 0% -> 8%
where the time goes in v2:
time: 145 us; the launch traced here: 144 us
  waiting for transfers between devices  44.4 us (31%)
  starting transfers between devices  39.4 us (27%)
  Pallas kernels  20.2 us (14%)
  between operations  14.5 us (10%)
  matrix products  9.55 us (7%)
  other arithmetic  8.22 us (6%)
  local copies, waits for them, and re-layouts  7.95 us (5%)
    ppermute x9, waiting for transfers between devices, shifted(): lax.ppermute(value, 'fsdp', [(i, (i + step) % N_FS) for i in range(N_FS)])  20.1 us
    all_to_all x1, starting transfers between devices, per_device(): wanted = lax.all_to_all(code, 'dp', split_axis=0, concat_axis=0, tiled=True)  13 us
    ppermute x9, starting transfers between devices, shifted(): lax.ppermute(value, 'fsdp', [(i, (i + step) % N_FS) for i in range(N_FS)])  11.8 us
    all_to_all x1, waiting for transfers between devices, per_device(): lax.all_to_all(fetched, 'dp', split_axis=0, concat_axis=0, tiled=True)  10 us
    dot_general x8, matrix products, dot(): lax.dot_general(a, b, (((ca,), (cb,)), ((), ())), preferred_element_type=...  9.55 us
    pallas_call x1, Pallas kernels, pool_sum(): pl.pallas_call(pool_sum_kernel, out_shape=jax.ShapeDtypeStruct(pool.shape...  8.24 us
    all_to_all x1, starting transfers between devices, per_device(): got = lax.all_to_all(sent, 'dp', split_axis=0, concat_axis=0, tiled=True)  8.2 us
    all_to_all x1, waiting for transfers between devices, per_device(): wanted = lax.all_to_all(code, 'dp', split_axis=0, concat_axis=0, tiled=True)  8.1 us
  transfers between devices with their start and end apart: 15, of which 7 were waited for; matrix products, arithmetic and copies ran while one was open for 16% of the time, Pallas kernels for 8%

profile of v2, /device:TPU:1, one launch (start us, length us, event | category | flops | bytes accessed | tf_op | source)
XLA Modules:
  0.0 144.2 jit_solution(4256280824126396640)
XLA Ops:
  7.2 0.7 all-gather.2.cloned.1.call-update
  7.9 0.7 add_bitcast_fusion.name_ref
  8.6 1.2 shard_map.128
  9.8 13.0 %all-to-all-start = ((s32[64,1,16]{2,1,0:T(1,128)}), s32[64,1,16]{2,1,0:T(1,128)S(1)}, u32[]{:S(2)}, u32[]{:S(2)}) async-start(s32[64,1,16]{2,1,0:T(1,128)} %bitcast.2), calls=%async_computation | async-start | bytes 65536 | tf_op jit(solution)/shard_map/all_to_all | solution.py:457
  22.9 1.0 copy.18
  24.0 8.1 %all-to-all-done = s32[64,1,16]{2,1,0:T(1,128)S(1)} async-done(((s32[64,1,16]{2,1,0:T(1,128)}), s32[64,1,16]{2,1,0:T(1,128)S(1)}, u32[]{:S(2)}, u32[]{:S(2)}) %all-to-all-start) | async-done | bytes 4128 | tf_op jit(solution)/shard_map/all_to_all | solution.py:457
  32.1 2.6 %shard_map.129 = bf16[64,14,8,128]{3,2,1,0:T(8,128)(2,1)S(1)} custom-call(s32[64,16]{1,0:T(8,128)S(1)} %bitcast.61, bf16[128,8,128]{2,1,0:T(8,128)(2,1)S(1)} %bitcast.56), custom_call_target="tpu_custom_call" | custom-call | bytes 3670016 | tf_op jit(solution)/shard_map/pallas_call | solution.py:156
  34.7 1.3 copy-done
  35.9 4.9 %all-to-all-start.1 = ((bf16[64,112,128]{2,1,0:T(8,128)(2,1)}), bf16[64,112,128]{2,1,0:T(8,128)(2,1)S(1)}, u32[]{:S(2)}, u32[]{:S(2)}) async-start(bf16[64,112,128]{2,1,0:T(8,128)(2,1)} %bitcast.53), calls=%async_computation.1 | async-start | bytes 3670016 | tf_op jit(solution)/shard_map/all_to_all | solution.py:460
  41.0 4.3 %multiply_convert_fusion = (bf16[256,1024]{1,0:T(8,128)(2,1)S(1)}, bf16[256,1024]{1,0:T(8,128)(2,1)S(1)}, f32[256]{0:T(256)S(1)}, f32[256,1024]{1,0:T(8,128)S(1)}) fusion(f32[1024]{0:T(1024)S(1)} %copy-done.5, bf16[256,2048]{1,0:T(8,128)(2,1)} %param.15, bf16[2048,1024]{1,0:T(8,128)(2,1)} %param.16, bf16[256,1024]{1,0:T(8,128)(2,1)} %param.14), kind=kOutput, calls=%fused_computation.6 | convolution fusion | flops 1076100864 | bytes 7869440 | tf_op jit(solution)/shard_map/dot_general | solution.py:31
  45.3 0.5 fusion.5
  45.7 0.2 fusion.25
  45.9 0.2 fusion.26
  46.2 0.7 pad_maximum_fusion.1
  46.9 1.3 collective-permute-start
  48.1 1.4 collective-permute-start.1
  49.6 1.6 %collective-permute-start.2 = (f32[152,256]{1,0:T(8,128)}, f32[152,256]{1,0:T(8,128)}, u32[]{:S(2)}, u32[]{:S(2)}) collective-permute-start(f32[152,256]{1,0:T(8,128)} %pad_maximum_fusion.1), channel_id=1, source_target_pairs={{0,2},{1,3},{2,0},{3,1},{4,6},{5,7},{6,4},{7,5},{8,10},{9,11},{10,... | collective-permute-start | bytes 466952 | tf_op jit(solution)/shard_map/ppermute | solution.py:46
  51.2 1.3 fusion.3
  52.5 1.3 convolution_add_fusion
  53.9 1.3 copy-done.8
  55.2 1.2 constant_dynamic-slice_fusion.6
  56.4 2.3 %copy.16 = bf16[256,2048]{0,1:T(8,128)(2,1)} copy(bf16[256,2048]{1,0:T(8,128)(2,1)} %param.15) | data formatting | bytes 2097152 | tf_op jit(solution)/shard_map/optimization_barrier | solution.py:462
  58.6 0.4 collective-permute-start.3
  59.0 2.3 %collective-permute-start.4 = (f32[64,2048]{1,0:T(8,128)}, f32[64,2048]{1,0:T(8,128)S(1)}, u32[]{:S(2)}, u32[]{:S(2)}) collective-permute-start(f32[64,2048]{1,0:T(8,128)} %get-tuple-element.79), channel_id=1, source_target_pairs={{0,3},{1,0},{2,1},{3,2},{4,7},{5,4},{6,5},{7,6},{8,11},{9,8},{10,9... | collective-permute-start | bytes 1572872 | tf_op jit(solution)/shard_map/ppermute | solution.py:46
  61.3 2.3 %pad_maximum_fusion = bf16[512,1024]{1,0:T(8,128)(2,1)} fusion(bf16[256,1024]{1,0:T(8,128)(2,1)} %copy-done.13, bf16[256,1024]{1,0:T(8,128)(2,1)} %copy-done.12), kind=kLoop, calls=%fused_computation.2 | loop fusion | flops 2097152 | bytes 2097152 | tf_op jit(solution)/shard_map/concatenate | solution.py:468
  63.7 1.1 add_add_fusion.1
  65.1 0.1 exponential_reduce_fusion
  65.2 7.7 %collective-permute-done.3 = f32[64,2048]{1,0:T(8,128)S(1)} collective-permute-done((f32[64,2048]{1,0:T(8,128)}, f32[64,2048]{1,0:T(8,128)S(1)}, u32[]{:S(2)}, u32[]{:S(2)}) %collective-permute-start.3) | collective-permute-done | bytes 524320 | tf_op jit(solution)/shard_map/ppermute | solution.py:46
  72.8 9.8 %collective-permute-done.5 = f32[64,2048]{1,0:T(8,128)S(1)} collective-permute-done((f32[64,2048]{1,0:T(8,128)S(1)}, f32[64,2048]{1,0:T(8,128)S(1)}, u32[]{:S(2)}, u32[]{:S(2)}) %collective-permute-start.5) | collective-permute-done | bytes 524320 | tf_op jit(solution)/shard_map/ppermute | solution.py:46
  82.6 2.0 %add_add_fusion = f32[64,2048]{1,0:T(8,128)} fusion(f32[64,2048]{1,0:T(8,128)S(1)} %collective-permute-done.5, f32[64,2048]{1,0:T(8,128)S(1)} %collective-permute-done.4, f32[64,2048]{1,0:T(8,128)S(1)} %collective-permute-done.3, f32[256,2048]{1,0:T(8,128)} %copy-done.8, s32[]{:T(128)S(6)} %select_n.58), kind=kLoop, calls=%fused_computation.10 | loop fusion | flops 393216 | bytes 2621444 | tf_op jit(solution)/shard_map/add | solution.py:76
  84.7 10.0 %all-to-all-done.1 = bf16[64,112,128]{2,1,0:T(8,128)(2,1)S(1)} async-done(((bf16[64,112,128]{2,1,0:T(8,128)(2,1)}), bf16[64,112,128]{2,1,0:T(8,128)(2,1)S(1)}, u32[]{:S(2)}, u32[]{:S(2)}) %all-to-all-start.1) | async-done | bytes 1835040 | tf_op jit(solution)/shard_map/all_to_all | solution.py:460
  94.7 3.2 %shard_map.130 = (f32[16,64]{1,0:T(8,128)S(1)}, bf16[112,8,128]{2,1,0:T(8,128)(2,1)S(1)}) custom-call(s32[1,448]{1,0:T(1,128)S(1)} %get-tuple-element.45.slot_ref, bf16[896,8,128]{2,1,0:T(8,128)(2,1)S(1)} %bitcast.52, bf16[64,8,128]{2,1,0:T(8,128)(2,1)S(1)} %bitcast.60), custom_call_target="tpu_custom_call" | custom-call | flops 2000000 | bytes 2200000 | tf_op jit(solution)/shard_map/pallas_call | solution.py:195
  97.9 0.5 fusion.21
  98.5 1.5 %collective-permute-start.6 = (f32[8,384]{1,0:T(8,128)S(1)}, f32[8,384]{1,0:T(8,128)S(1)}, u32[]{:S(2)}, u32[]{:S(2)}) collective-permute-start(f32[8,384]{1,0:T(8,128)S(1)} %select_maximum_fusion), channel_id=1, source_target_pairs={{0,1},{1,2},{2,3},{3,0},{4,5},{5,6},{6,7},{7,4},{8,9},{9,10},{10,1... | collective-permute-start | bytes 36872 | tf_op jit(solution)/shard_map/ppermute | solution.py:46
  100.0 1.7 %collective-permute-start.7 = (f32[8,384]{1,0:T(8,128)S(1)}, f32[8,384]{1,0:T(8,128)S(1)}, u32[]{:S(2)}, u32[]{:S(2)}) collective-permute-start(f32[8,384]{1,0:T(8,128)S(1)} %select_maximum_fusion), channel_id=1, source_target_pairs={{0,3},{1,0},{2,1},{3,2},{4,7},{5,4},{6,5},{7,6},{8,11},{9,8},{10,9... | collective-permute-start | bytes 36872 | tf_op jit(solution)/shard_map/ppermute | solution.py:46
  101.8 1.3 collective-permute-start.8
  103.2 2.6 %collective-permute-done.8 = f32[8,384]{1,0:T(8,128)S(1)} collective-permute-done((f32[8,384]{1,0:T(8,128)S(1)}, f32[8,384]{1,0:T(8,128)S(1)}, u32[]{:S(2)}, u32[]{:S(2)}) %collective-permute-start.8) | collective-permute-done | bytes 12320 | tf_op jit(solution)/shard_map/ppermute | solution.py:46
  105.9 1.2 shard_map.131
  107.1 1.2 shard_map.132
  108.3 1.3 fusion.27
  109.7 1.4 collective-permute-start.9
  111.1 8.2 %all-to-all-start.2 = ((f32[64,1,32]{2,1,0:T(1,128)}), f32[64,1,32]{2,1,0:T(1,128)S(1)}, u32[]{:S(2)}, u32[]{:S(2)}) async-start(f32[64,1,32]{2,1,0:T(1,128)} %bitcast.18), calls=%async_computation.2 | async-start | bytes 65536 | tf_op jit(solution)/shard_map/all_to_all | solution.py:525
  119.5 2.6 %shard_map.133 = (bf16[256,1024]{1,0:T(8,128)(2,1)}, bf16[2048,1024]{1,0:T(8,128)(2,1)}) custom-call(f32[256,1024]{1,0:T(8,128)S(1)} %get-tuple-element.44.hidden_ref, f32[16,1024]{1,0:T(8,128)S(1)} %get-tuple-element.64.gained_ref, f32[1,256]{1,0:T(1,128)S(1)} %fusion.15.rms_ref, f32[1,256]{1,0:T(1,128)S(1)} %get-tuple-element.65.shrink_ref, ...), custom_call_target="tpu_custom_call" | custom-call | flops 1100000000 | bytes 7000000 | tf_op jit(solution)/shard_map/pallas_call | solution.py:360
  122.1 0.4 collective-permute-done.10
  122.6 0.8 fusion.1
  123.4 5.1 %all-to-all-done.2 = f32[64,1,32]{2,1,0:T(1,128)S(1)} async-done(((f32[64,1,32]{2,1,0:T(1,128)}), f32[64,1,32]{2,1,0:T(1,128)S(1)}, u32[]{:S(2)}, u32[]{:S(2)}) %all-to-all-start.2) | async-done | bytes 8224 | tf_op jit(solution)/shard_map/all_to_all | solution.py:525
  128.5 0.6 copy-done.14
  129.1 8.2 %shard_map.134 = bf16[128,1024]{1,0:T(8,128)(2,1)} custom-call(s32[64,16]{1,0:T(8,128)} %bitcast.62, f32[64,32]{1,0:T(8,128)} %bitcast.68, bf16[4096,1024]{1,0:T(8,128)(2,1)} %all-gather.2.cloned.1.call-done.q_ref, bf16[128,1024]{1,0:T(8,128)(2,1)} %pool_ref.1), custom_call_target="tpu_custom_call" | custom-call | flops 2500000000 | bytes 9000000 | tf_op jit(solution)/shard_map/pallas_call | solution.py:430
  (65 shorter events, 1.1 us)
Async XLA Ops:
  7.2 121.4 %all-gather.2.cloned.1.call-start = ((), (), s32[]{:S(2)}) async-start(), calls=%async_computation.3 | async-start | bytes 8519680 | tf_op jit(solution)/shard_map/all_gather | solution.py:452
  9.8 22.2 %all-to-all-start = ((s32[64,1,16]{2,1,0:T(1,128)}), s32[64,1,16]{2,1,0:T(1,128)S(1)}, u32[]{:S(2)}, u32[]{:S(2)}) async-start(s32[64,1,16]{2,1,0:T(1,128)} %bitcast.2), calls=%async_computation | async-start | bytes 65536 | tf_op jit(solution)/shard_map/all_to_all | solution.py:457
  32.1 3.9 %copy-start.4 = (s32[64,1,16]{2,1,0:T(1,128)}, s32[64,1,16]{2,1,0:T(1,128)S(1)}, u32[]{:S(2)}) copy-start(s32[64,1,16]{2,1,0:T(1,128)S(1)} %all-to-all-done) | copy-start | bytes 12292
  34.6 1.3 copy-start
  35.9 4.9 %copy-start.1 = (bf16[64,1024]{1,0:T(8,128)(2,1)S(1)}, bf16[64,1024]{1,0:T(8,128)(2,1)}, u32[]{:S(2)}) copy-start(bf16[64,1024]{1,0:T(8,128)(2,1)} %q_ref) | copy-start | bytes 393220
  35.9 5.0 %copy-start.2 = (bf16[64,1024]{1,0:T(8,128)(2,1)S(1)}, bf16[64,1024]{1,0:T(8,128)(2,1)}, u32[]{:S(2)}) copy-start(bf16[64,1024]{1,0:T(8,128)(2,1)} %pos_ref) | copy-start | bytes 393220
  35.9 5.0 %copy-start.5 = (f32[1024]{0:T(1024)S(1)}, f32[1024]{0:T(1024)}, u32[]{:S(2)}) copy-start(f32[1024]{0:T(1024)} %param.17) | copy-start | bytes 12292
  35.9 58.7 %all-to-all-start.1 = ((bf16[64,112,128]{2,1,0:T(8,128)(2,1)}), bf16[64,112,128]{2,1,0:T(8,128)(2,1)S(1)}, u32[]{:S(2)}, u32[]{:S(2)}) async-start(bf16[64,112,128]{2,1,0:T(8,128)(2,1)} %bitcast.53), calls=%async_computation.1 | async-start | bytes 3670016 | tf_op jit(solution)/shard_map/all_to_all | solution.py:460
  41.0 10.3 %copy-start.6 = (bf16[2048,1024]{1,0:T(8,128)(2,1)S(1)}, bf16[2048,1024]{1,0:T(8,128)(2,1)}, u32[]{:S(2)}) copy-start(bf16[2048,1024]{1,0:T(8,128)(2,1)} %param.16) | copy-start | bytes 12582916
  45.2 6.0 %copy-start.12 = (bf16[256,1024]{1,0:T(8,128)(2,1)}, bf16[256,1024]{1,0:T(8,128)(2,1)S(1)}, u32[]{:S(2)}) copy-start(bf16[256,1024]{1,0:T(8,128)(2,1)S(1)} %get-tuple-element.80) | copy-start | bytes 1572868
  45.2 6.0 %copy-start.13 = (bf16[256,1024]{1,0:T(8,128)(2,1)}, bf16[256,1024]{1,0:T(8,128)(2,1)S(1)}, u32[]{:S(2)}) copy-start(bf16[256,1024]{1,0:T(8,128)(2,1)S(1)} %get-tuple-element.81) | copy-start | bytes 1572868
  46.9 16.7 %collective-permute-start = (f32[152,256]{1,0:T(8,128)}, f32[152,256]{1,0:T(8,128)}, u32[]{:S(2)}, u32[]{:S(2)}) collective-permute-start(f32[152,256]{1,0:T(8,128)} %pad_maximum_fusion.1), channel_id=1, source_target_pairs={{0,1},{1,2},{2,3},{3,0},{4,5},{5,6},{6,7},{7,4},{8,9},{9,10},{10,1... | collective-permute-start | bytes 466952 | tf_op jit(solution)/shard_map/ppermute | solution.py:46
  48.1 15.6 %collective-permute-start.1 = (f32[152,256]{1,0:T(8,128)}, f32[152,256]{1,0:T(8,128)}, u32[]{:S(2)}, u32[]{:S(2)}) collective-permute-start(f32[152,256]{1,0:T(8,128)} %pad_maximum_fusion.1), channel_id=1, source_target_pairs={{0,3},{1,0},{2,1},{3,2},{4,7},{5,4},{6,5},{7,6},{8,11},{9,8},{10,9... | collective-permute-start | bytes 466952 | tf_op jit(solution)/shard_map/ppermute | solution.py:46
  49.6 14.1 %collective-permute-start.2 = (f32[152,256]{1,0:T(8,128)}, f32[152,256]{1,0:T(8,128)}, u32[]{:S(2)}, u32[]{:S(2)}) collective-permute-start(f32[152,256]{1,0:T(8,128)} %pad_maximum_fusion.1), channel_id=1, source_target_pairs={{0,2},{1,3},{2,0},{3,1},{4,6},{5,7},{6,4},{7,5},{8,10},{9,11},{10,... | collective-permute-start | bytes 466952 | tf_op jit(solution)/shard_map/ppermute | solution.py:46
  53.8 1.3 copy-start.8
  58.6 5.0 %copy-start.11 = (f32[64,2048]{1,0:T(8,128)S(1)}, f32[64,2048]{1,0:T(8,128)}, u32[]{:S(2)}) copy-start(f32[64,2048]{1,0:T(8,128)} %get-tuple-element.78) | copy-start | bytes 1572868
  58.6 14.2 %collective-permute-start.3 = (f32[64,2048]{1,0:T(8,128)}, f32[64,2048]{1,0:T(8,128)S(1)}, u32[]{:S(2)}, u32[]{:S(2)}) collective-permute-start(f32[64,2048]{1,0:T(8,128)} %get-tuple-element.77), channel_id=1, source_target_pairs={{0,1},{1,2},{2,3},{3,0},{4,5},{5,6},{6,7},{7,4},{8,9},{9,10},{10,1... | collective-permute-start | bytes 1572872 | tf_op jit(solution)/shard_map/ppermute | solution.py:46
  59.0 13.8 %collective-permute-start.4 = (f32[64,2048]{1,0:T(8,128)}, f32[64,2048]{1,0:T(8,128)S(1)}, u32[]{:S(2)}, u32[]{:S(2)}) collective-permute-start(f32[64,2048]{1,0:T(8,128)} %get-tuple-element.79), channel_id=1, source_target_pairs={{0,3},{1,0},{2,1},{3,2},{4,7},{5,4},{6,5},{7,6},{8,11},{9,8},{10,9... | collective-permute-start | bytes 1572872 | tf_op jit(solution)/shard_map/ppermute | solution.py:46
  63.6 19.0 %collective-permute-start.5 = (f32[64,2048]{1,0:T(8,128)S(1)}, f32[64,2048]{1,0:T(8,128)S(1)}, u32[]{:S(2)}, u32[]{:S(2)}) collective-permute-start(f32[64,2048]{1,0:T(8,128)S(1)} %copy-done.11), channel_id=1, source_target_pairs={{0,2},{1,3},{2,0},{3,1},{4,6},{5,7},{6,4},{7,5},{8,10},{9,11},{10,... | collective-permute-start | bytes 1572872 | tf_op jit(solution)/shard_map/ppermute | solution.py:46
  94.7 3.2 %copy-start.9 = (bf16[512,1024]{1,0:T(8,128)(2,1)S(1)}, bf16[512,1024]{1,0:T(8,128)(2,1)}, u32[]{:S(2)}) copy-start(bf16[512,1024]{1,0:T(8,128)(2,1)} %pad_maximum_fusion) | copy-start | bytes 3145732
  94.7 13.6 %copy-start.7 = (bf16[2048,1024]{1,0:T(8,128)(2,1)S(1)}, bf16[2048,1024]{1,0:T(8,128)(2,1)}, u32[]{:S(2)}) copy-start(bf16[2048,1024]{1,0:T(8,128)(2,1)} %param.16) | copy-start | bytes 12582916
  98.5 4.7 %collective-permute-start.6 = (f32[8,384]{1,0:T(8,128)S(1)}, f32[8,384]{1,0:T(8,128)S(1)}, u32[]{:S(2)}, u32[]{:S(2)}) collective-permute-start(f32[8,384]{1,0:T(8,128)S(1)} %select_maximum_fusion), channel_id=1, source_target_pairs={{0,1},{1,2},{2,3},{3,0},{4,5},{5,6},{6,7},{7,4},{8,9},{9,10},{10,1... | collective-permute-start | bytes 36872 | tf_op jit(solution)/shard_map/ppermute | solution.py:46
  100.0 3.2 %collective-permute-start.7 = (f32[8,384]{1,0:T(8,128)S(1)}, f32[8,384]{1,0:T(8,128)S(1)}, u32[]{:S(2)}, u32[]{:S(2)}) collective-permute-start(f32[8,384]{1,0:T(8,128)S(1)} %select_maximum_fusion), channel_id=1, source_target_pairs={{0,3},{1,0},{2,1},{3,2},{4,7},{5,4},{6,5},{7,6},{8,11},{9,8},{10,9... | collective-permute-start | bytes 36872 | tf_op jit(solution)/shard_map/ppermute | solution.py:46
  101.8 4.1 %collective-permute-start.8 = (f32[8,384]{1,0:T(8,128)S(1)}, f32[8,384]{1,0:T(8,128)S(1)}, u32[]{:S(2)}, u32[]{:S(2)}) collective-permute-start(f32[8,384]{1,0:T(8,128)S(1)} %select_maximum_fusion), channel_id=1, source_target_pairs={{0,2},{1,3},{2,0},{3,1},{4,6},{5,7},{6,4},{7,5},{8,10},{9,11},{10,... | collective-permute-start | bytes 36872 | tf_op jit(solution)/shard_map/ppermute | solution.py:46
  108.3 11.2 %copy-start.3 = (bf16[256,2048]{0,1:T(8,128)(2,1)S(1)}, bf16[256,2048]{0,1:T(8,128)(2,1)}, u32[]{:S(2)}) copy-start(bf16[256,2048]{0,1:T(8,128)(2,1)} %copy.16) | copy-start | bytes 3145732
  109.7 9.7 %collective-permute-start.9 = (f32[8,2048]{1,0:T(8,128)S(1)}, f32[8,2048]{1,0:T(8,128)S(1)}, u32[]{:S(2)}, u32[]{:S(2)}) collective-permute-start(f32[8,2048]{1,0:T(8,128)S(1)} %constant_dynamic-slice_fusion.2), channel_id=1, source_target_pairs={{0,3},{1,2},{2,1},{3,0},{4,7},{5,6},{6,5},{7,4},{8,11},{9,10},{10,... | collective-permute-start | bytes 196616 | tf_op jit(solution)/shard_map/ppermute | solution.py:50
  111.1 17.4 %all-to-all-start.2 = ((f32[64,1,32]{2,1,0:T(1,128)}), f32[64,1,32]{2,1,0:T(1,128)S(1)}, u32[]{:S(2)}, u32[]{:S(2)}) async-start(f32[64,1,32]{2,1,0:T(1,128)} %bitcast.18), calls=%async_computation.2 | async-start | bytes 65536 | tf_op jit(solution)/shard_map/all_to_all | solution.py:525
  119.4 3.2 %copy-start.10 = (f32[64,2048]{1,0:T(8,128)S(1)}, f32[64,2048]{1,0:T(8,128)}, u32[]{:S(2)}) copy-start(f32[64,2048]{1,0:T(8,128)} %add_add_fusion) | copy-start | bytes 1572868
  119.4 3.1 %collective-permute-start.10 = (f32[4,2048]{1,0:T(4,128)S(1)}, f32[4,2048]{1,0:T(4,128)S(1)}, u32[]{:S(2)}, u32[]{:S(2)}) collective-permute-start(f32[4,2048]{1,0:T(4,128)S(1)} %constant_dynamic-slice_fusion.1), channel_id=1, source_target_pairs={{0,1},{1,0},{2,3},{3,2},{4,5},{5,4},{6,7},{7,6},{8,9},{9,8},{10,11... | collective-permute-start | bytes 98312 | tf_op jit(solution)/shard_map/ppermute | solution.py:50
  128.5 0.6 copy-start.14
Sparse Core Ops, SparseCore 0:
  10.8 99.8 all-gather.1

commit v3 on v2

--- a/solution.py
+++ b/solution.py
@@ -73,7 +73,8 @@
     total = lax.dynamic_slice(rows, (me * own, 0), (own, rows.shape[1]))
     for step in (1, 3, 2):
         there = lax.rem(me + step, N_FS)
-        total += shifted(lax.dynamic_slice(rows, (there * own, 0), (own, rows.shape[1])), step)
+        part = lax.dynamic_slice(rows, (there * own, 0), (own, rows.shape[1]))
+        total += shifted(part.astype(BF16), step).astype(F32)
     return total
 
 
@@ -145,7 +146,7 @@
 
 
 def fetch_kernel(code_ref, pool_ref, out_ref):
-    @pl.loop(0, out_ref.shape[0])
+    @pl.loop(0, out_ref.shape[0], unroll=2)
     def _(peer):
         for place in range(SLOTS):
             out_ref[peer, place] = pool_ref[lax.shift_right_logical(code_ref[peer, place], 7)]
@@ -180,8 +181,8 @@
             cos_ref[at, :] = jnp.sum(wide * asked, axis=0, keepdims=True)
             sq_ref[at, :] = jnp.sum(wide * wide, axis=0, keepdims=True)
 
-    pl.loop(0, CH_Q)(lambda query: one(query, True))
-    pl.loop(CH_Q, Q_GRP)(lambda query: one(query, False))
+    pl.loop(0, CH_Q, unroll=2)(lambda query: one(query, True))
+    pl.loop(CH_Q, Q_GRP, unroll=4)(lambda query: one(query, False))
 
     line = lax.broadcasted_iota(jnp.int32, (SUB, LANES), 0)
     for part, ref in ((0, cos_ref), (1, sq_ref)):
@@ -377,15 +378,7 @@
     )(hidden, gained, rms, shrink, attn_turned)
 
 
-def pool_sum_kernel(code_ref, weight_ref, q_ref, pool_ref, out_ref, spread_ref, held_ref, sems):
-    blocks, block = held_ref.shape[0], held_ref.shape[2]
-    copies = []
-    for b in range(blocks):
-        copy = pltpu.make_async_copy(
-            q_ref.at[:, pl.ds(b * block, block)], held_ref.at[b], sems.at[b]
-        )
-        copy.start()
-        copies.append(copy)
+def pool_sum_kernel(code_ref, weight_ref, q_ref, pool_ref, out_ref, spread_ref):
     group = LANES // WIDE
     steps = code_ref.shape[0] // group
 
@@ -416,10 +409,10 @@
         ).astype(BF16)
         own += jnp.where(hot, w_n[at], 0.0)
     own = jnp.sum(own, axis=1, keepdims=True)
-    for b in range(blocks):
-        at = slice(b * block, (b + 1) * block)
-        copies[b].wait()
-        both = dot(spread_ref[...], held_ref[b], 1, 0)
+    width = 256
+    for first in range(0, out_ref.shape[1], width):
+        at = slice(first, first + width)
+        both = dot(spread_ref[...], q_ref[:, at], 1, 0)
         out_ref[:, at] = (
             both[:POOL_GRP] + both[POOL_GRP:] - own * pool_ref[:, at].astype(F32)
         ).astype(BF16)
@@ -430,14 +423,10 @@
     return pl.pallas_call(
         pool_sum_kernel,
         out_shape=jax.ShapeDtypeStruct(pool.shape, BF16),
-        in_specs=[vmem, vmem, pl.BlockSpec(memory_space=pl.ANY), vmem],
+        in_specs=[vmem] * 4,
         out_specs=vmem,
-        scratch_shapes=[
-            pltpu.VMEM((2 * POOL_GRP, q_all.shape[0]), BF16),
-            pltpu.VMEM((4, q_all.shape[0], pool.shape[1] // 4), BF16),
-            pltpu.SemaphoreType.DMA((4,)),
-        ],
-        compiler_params=pltpu.CompilerParams(vmem_limit_bytes=60 * 1024 * 1024),
+        scratch_shapes=[pltpu.VMEM((2 * POOL_GRP, q_all.shape[0]), BF16)],
+        compiler_params=pltpu.CompilerParams(vmem_limit_bytes=VMEM_LIMIT),
         cost_estimate=pl.CostEstimate(
             flops=2500000000, bytes_accessed=9000000, transcendentals=0
         ),

time: 145 us -> 142 us (0.979)
  Pallas kernels: 20.2 us -> 15.3 us
  local copies, waits for them, and re-layouts: 7.95 us -> 10.5 us
    ppermute x9, waiting for transfers between devices: 20.1 us -> 8.29 us  [shifted(): lax.ppermute(value, 'fsdp', [(i, (i + step) % N_FS) for i in range(N_FS)])]
    all_to_all x1, waiting for transfers between devices: 10 us -> 21.7 us  [per_device(): lax.all_to_all(fetched, 'dp', split_axis=0, concat_axis=0, tiled=True)]
    pallas_call x1, Pallas kernels: 8.24 us -> 3.97 us  [pool_sum(): pl.pallas_call(pool_sum_kernel, out_shape=jax.ShapeDtypeStruct(pool.shape...]
    unnamed x34 -> x38, local copies, waits for them, and re-layouts: 4.3 us -> 7.08 us
where the time goes in v3:
time: 142 us
  waiting for transfers between devices  44.2 us (31%)
  starting transfers between devices  39.7 us (28%)
  Pallas kernels  15.3 us (11%)
  between operations  14.5 us (10%)
  local copies, waits for them, and re-layouts  10.5 us (7%)
  matrix products  9.54 us (7%)
  other arithmetic  8.19 us (6%)
    all_to_all x1, waiting for transfers between devices, per_device(): lax.all_to_all(fetched, 'dp', split_axis=0, concat_axis=0, tiled=True)  21.7 us
    all_to_all x1, starting transfers between devices, per_device(): wanted = lax.all_to_all(code, 'dp', split_axis=0, concat_axis=0, tiled=True)  13 us
    ppermute x9, starting transfers between devices, shifted(): lax.ppermute(value, 'fsdp', [(i, (i + step) % N_FS) for i in range(N_FS)])  11.7 us
    dot_general x8, matrix products, dot(): lax.dot_general(a, b, (((ca,), (cb,)), ((), ())), preferred_element_type=...  9.54 us
    all_to_all x1, starting transfers between devices, per_device(): got = lax.all_to_all(sent, 'dp', split_axis=0, concat_axis=0, tiled=True)  8.43 us
    ppermute x9, waiting for transfers between devices, shifted(): lax.ppermute(value, 'fsdp', [(i, (i + step) % N_FS) for i in range(N_FS)])  8.29 us
    all_to_all x1, waiting for transfers between devices, per_device(): wanted = lax.all_to_all(code, 'dp', split_axis=0, concat_axis=0, tiled=True)  8.1 us
    unnamed x38, local copies, waits for them, and re-layouts  7.08 us
  transfers between devices with their start and end apart: 15, of which 7 were waited for; matrix products, arithmetic and copies ran while one was open for 16% of the time, Pallas kernels for 8%

profile of v3, /device:TPU:1, one launch (start us, length us, event | category | flops | bytes accessed | tf_op | source)
XLA Modules:
  0.0 142.0 jit_solution(12320719939542563384)
XLA Ops:
  7.2 0.7 all-gather.2.cloned.1.call-update
  7.9 0.7 add_bitcast_fusion.name_ref
  8.6 1.2 shard_map.128
  9.8 13.0 %all-to-all-start = ((s32[64,1,16]{2,1,0:T(1,128)}), s32[64,1,16]{2,1,0:T(1,128)S(1)}, u32[]{:S(2)}, u32[]{:S(2)}) async-start(s32[64,1,16]{2,1,0:T(1,128)} %bitcast.2), calls=%async_computation | async-start | bytes 65536 | tf_op jit(solution)/shard_map/all_to_all | solution.py:446
  22.9 1.0 copy.18
  24.0 8.1 %all-to-all-done = s32[64,1,16]{2,1,0:T(1,128)S(1)} async-done(((s32[64,1,16]{2,1,0:T(1,128)}), s32[64,1,16]{2,1,0:T(1,128)S(1)}, u32[]{:S(2)}, u32[]{:S(2)}) %all-to-all-start) | async-done | bytes 4128 | tf_op jit(solution)/shard_map/all_to_all | solution.py:446
  32.1 2.4 %shard_map.129 = bf16[64,14,8,128]{3,2,1,0:T(8,128)(2,1)S(1)} custom-call(s32[64,16]{1,0:T(8,128)S(1)} %bitcast.62, bf16[128,8,128]{2,1,0:T(8,128)(2,1)S(1)} %bitcast.56), custom_call_target="tpu_custom_call" | custom-call | bytes 3670016 | tf_op jit(solution)/shard_map/pallas_call | solution.py:157
  34.5 1.3 copy-done
  35.8 4.9 %all-to-all-start.1 = ((bf16[64,112,128]{2,1,0:T(8,128)(2,1)}), bf16[64,112,128]{2,1,0:T(8,128)(2,1)S(1)}, u32[]{:S(2)}, u32[]{:S(2)}) async-start(bf16[64,112,128]{2,1,0:T(8,128)(2,1)} %bitcast.53), calls=%async_computation.1 | async-start | bytes 3670016 | tf_op jit(solution)/shard_map/all_to_all | solution.py:449
  40.8 4.3 %multiply_convert_fusion = (bf16[256,1024]{1,0:T(8,128)(2,1)S(1)}, bf16[256,1024]{1,0:T(8,128)(2,1)S(1)}, f32[256]{0:T(256)S(1)}, f32[256,1024]{1,0:T(8,128)S(1)}) fusion(f32[1024]{0:T(1024)S(1)} %copy-done.5, bf16[256,2048]{1,0:T(8,128)(2,1)} %param.15, bf16[2048,1024]{1,0:T(8,128)(2,1)} %param.16, bf16[256,1024]{1,0:T(8,128)(2,1)} %param.14), kind=kOutput, calls=%fused_computation.6 | convolution fusion | flops 1076100864 | bytes 7869440 | tf_op jit(solution)/shard_map/dot_general | solution.py:31
  45.0 0.5 fusion.5
  45.5 0.2 fusion.25
  45.7 0.2 fusion.26
  46.0 0.7 pad_maximum_fusion.1
  46.7 1.3 collective-permute-start
  48.0 1.4 %collective-permute-start.1 = (f32[152,256]{1,0:T(8,128)}, f32[152,256]{1,0:T(8,128)}, u32[]{:S(2)}, u32[]{:S(2)}) collective-permute-start(f32[152,256]{1,0:T(8,128)} %pad_maximum_fusion.1), channel_id=1, source_target_pairs={{0,3},{1,0},{2,1},{3,2},{4,7},{5,4},{6,5},{7,6},{8,11},{9,8},{10,9... | collective-permute-start | bytes 466952 | tf_op jit(solution)/shard_map/ppermute | solution.py:46
  49.4 1.6 %collective-permute-start.2 = (f32[152,256]{1,0:T(8,128)}, f32[152,256]{1,0:T(8,128)}, u32[]{:S(2)}, u32[]{:S(2)}) collective-permute-start(f32[152,256]{1,0:T(8,128)} %pad_maximum_fusion.1), channel_id=1, source_target_pairs={{0,2},{1,3},{2,0},{3,1},{4,6},{5,7},{6,4},{7,5},{8,10},{9,11},{10,... | collective-permute-start | bytes 466952 | tf_op jit(solution)/shard_map/ppermute | solution.py:46
  51.0 1.3 fusion.3
  52.3 1.3 convolution_add_fusion
  53.7 1.3 copy-done.9
  55.0 0.9 dynamic-slice_convert_fusion.2
  55.9 2.3 %copy.16 = bf16[256,2048]{0,1:T(8,128)(2,1)} copy(bf16[256,2048]{1,0:T(8,128)(2,1)} %param.15) | data formatting | bytes 2097152 | tf_op jit(solution)/shard_map/optimization_barrier | solution.py:451
  58.2 0.4 collective-permute-start.3
  58.6 2.3 %collective-permute-start.4 = (bf16[64,2048]{1,0:T(8,128)(2,1)}, bf16[64,2048]{1,0:T(8,128)(2,1)S(1)}, u32[]{:S(2)}, u32[]{:S(2)}) collective-permute-start(bf16[64,2048]{1,0:T(8,128)(2,1)} %get-tuple-element.79), channel_id=1, source_target_pairs={{0,3},{1,0},{2,1},{3,2},{4,7},{5,4},{6,5},{7,6},{8,11},{9,8},{10,9... | collective-permute-start | bytes 786440 | tf_op jit(solution)/shard_map/ppermute | solution.py:46
  60.9 2.3 %pad_maximum_fusion = bf16[512,1024]{1,0:T(8,128)(2,1)} fusion(bf16[256,1024]{1,0:T(8,128)(2,1)} %copy-done.13, bf16[256,1024]{1,0:T(8,128)(2,1)} %copy-done.12), kind=kLoop, calls=%fused_computation.2 | loop fusion | flops 2097152 | bytes 2097152 | tf_op jit(solution)/shard_map/concatenate | solution.py:457
  63.1 0.1 collective-permute-start.5
  63.3 1.1 add_add_fusion
  64.8 1.2 collective-permute-done.3
  66.0 4.6 %collective-permute-done.5 = bf16[64,2048]{1,0:T(8,128)(2,1)S(1)} collective-permute-done((bf16[64,2048]{1,0:T(8,128)(2,1)S(1)}, bf16[64,2048]{1,0:T(8,128)(2,1)S(1)}, u32[]{:S(2)}, u32[]{:S(2)}) %collective-permute-start.5) | collective-permute-done | bytes 262176 | tf_op jit(solution)/shard_map/ppermute | solution.py:46
  70.6 2.0 %convert_add_fusion = f32[64,2048]{1,0:T(8,128)} fusion(bf16[64,2048]{1,0:T(8,128)(2,1)S(1)} %collective-permute-done.5, bf16[64,2048]{1,0:T(8,128)(2,1)S(1)} %collective-permute-done.4, bf16[64,2048]{1,0:T(8,128)(2,1)S(1)} %collective-permute-done.3, f32[256,2048]{1,0:T(8,128)} %copy-done.9, s32[]{:T(128)S(6)} %select_n.58), kind=kLoop, calls=%fused_computation.10 | loop fusion | flops 786432 | bytes 1835012 | tf_op jit(solution)/shard_map/add | solution.py:77
  72.5 21.7 %all-to-all-done.1 = bf16[64,112,128]{2,1,0:T(8,128)(2,1)S(1)} async-done(((bf16[64,112,128]{2,1,0:T(8,128)(2,1)}), bf16[64,112,128]{2,1,0:T(8,128)(2,1)S(1)}, u32[]{:S(2)}, u32[]{:S(2)}) %all-to-all-start.1) | async-done | bytes 1835040 | tf_op jit(solution)/shard_map/all_to_all | solution.py:449
  94.2 2.8 %shard_map.130 = (f32[16,64]{1,0:T(8,128)S(1)}, bf16[112,8,128]{2,1,0:T(8,128)(2,1)S(1)}) custom-call(s32[1,448]{1,0:T(1,128)S(1)} %get-tuple-element.45.slot_ref, bf16[896,8,128]{2,1,0:T(8,128)(2,1)S(1)} %bitcast.52, bf16[64,8,128]{2,1,0:T(8,128)(2,1)S(1)} %bitcast.60), custom_call_target="tpu_custom_call" | custom-call | flops 2000000 | bytes 2200000 | tf_op jit(solution)/shard_map/pallas_call | solution.py:196
  97.0 0.5 fusion.21
  97.6 1.5 %collective-permute-start.6 = (f32[8,384]{1,0:T(8,128)S(1)}, f32[8,384]{1,0:T(8,128)S(1)}, u32[]{:S(2)}, u32[]{:S(2)}) collective-permute-start(f32[8,384]{1,0:T(8,128)S(1)} %select_maximum_fusion), channel_id=1, source_target_pairs={{0,1},{1,2},{2,3},{3,0},{4,5},{5,6},{6,7},{7,4},{8,9},{9,10},{10,1... | collective-permute-start | bytes 36872 | tf_op jit(solution)/shard_map/ppermute | solution.py:46
  99.2 1.6 %collective-permute-start.7 = (f32[8,384]{1,0:T(8,128)S(1)}, f32[8,384]{1,0:T(8,128)S(1)}, u32[]{:S(2)}, u32[]{:S(2)}) collective-permute-start(f32[8,384]{1,0:T(8,128)S(1)} %select_maximum_fusion), channel_id=1, source_target_pairs={{0,3},{1,0},{2,1},{3,2},{4,7},{5,4},{6,5},{7,6},{8,11},{9,8},{10,9... | collective-permute-start | bytes 36872 | tf_op jit(solution)/shard_map/ppermute | solution.py:46
  100.7 1.5 %collective-permute-start.8 = (f32[8,384]{1,0:T(8,128)S(1)}, f32[8,384]{1,0:T(8,128)S(1)}, u32[]{:S(2)}, u32[]{:S(2)}) collective-permute-start(f32[8,384]{1,0:T(8,128)S(1)} %select_maximum_fusion), channel_id=1, source_target_pairs={{0,2},{1,3},{2,0},{3,1},{4,6},{5,7},{6,4},{7,5},{8,10},{9,11},{10,... | collective-permute-start | bytes 36872 | tf_op jit(solution)/shard_map/ppermute | solution.py:46
  102.3 2.5 %collective-permute-done.8 = f32[8,384]{1,0:T(8,128)S(1)} collective-permute-done((f32[8,384]{1,0:T(8,128)S(1)}, f32[8,384]{1,0:T(8,128)S(1)}, u32[]{:S(2)}, u32[]{:S(2)}) %collective-permute-start.8) | collective-permute-done | bytes 12320 | tf_op jit(solution)/shard_map/ppermute | solution.py:46
  104.9 1.2 shard_map.131
  106.0 1.2 shard_map.132
  107.2 1.3 fusion.27
  108.6 1.5 %collective-permute-start.9 = (f32[8,2048]{1,0:T(8,128)S(1)}, f32[8,2048]{1,0:T(8,128)S(1)}, u32[]{:S(2)}, u32[]{:S(2)}) collective-permute-start(f32[8,2048]{1,0:T(8,128)S(1)} %constant_dynamic-slice_fusion.2), channel_id=1, source_target_pairs={{0,3},{1,2},{2,1},{3,0},{4,7},{5,6},{6,5},{7,4},{8,11},{9,10},{10,... | collective-permute-start | bytes 196616 | tf_op jit(solution)/shard_map/ppermute | solution.py:50
  110.1 8.4 %all-to-all-start.2 = ((f32[64,1,32]{2,1,0:T(1,128)}), f32[64,1,32]{2,1,0:T(1,128)S(1)}, u32[]{:S(2)}, u32[]{:S(2)}) async-start(f32[64,1,32]{2,1,0:T(1,128)} %bitcast.18), calls=%async_computation.2 | async-start | bytes 65536 | tf_op jit(solution)/shard_map/all_to_all | solution.py:514
  118.8 2.6 %shard_map.133 = (bf16[256,1024]{1,0:T(8,128)(2,1)}, bf16[2048,1024]{1,0:T(8,128)(2,1)}) custom-call(f32[256,1024]{1,0:T(8,128)S(1)} %get-tuple-element.44.hidden_ref, f32[16,1024]{1,0:T(8,128)S(1)} %get-tuple-element.64.gained_ref, f32[1,256]{1,0:T(1,128)S(1)} %fusion.15.rms_ref, f32[1,256]{1,0:T(1,128)S(1)} %get-tuple-element.65.shrink_ref, ...), custom_call_target="tpu_custom_call" | custom-call | flops 1100000000 | bytes 7000000 | tf_op jit(solution)/shard_map/pallas_call | solution.py:361
  121.4 0.4 collective-permute-done.10
  121.9 0.8 fusion.1
  122.7 5.1 %all-to-all-done.2 = f32[64,1,32]{2,1,0:T(1,128)S(1)} async-done(((f32[64,1,32]{2,1,0:T(1,128)}), f32[64,1,32]{2,1,0:T(1,128)S(1)}, u32[]{:S(2)}, u32[]{:S(2)}) %all-to-all-start.2) | async-done | bytes 8224 | tf_op jit(solution)/shard_map/all_to_all | solution.py:514
  127.8 3.4 %copy-done.6 = bf16[4096,1024]{1,0:T(8,128)(2,1)S(1)} copy-done((bf16[4096,1024]{1,0:T(8,128)(2,1)S(1)}, bf16[4096,1024]{1,0:T(8,128)(2,1)}, u32[]{:S(2)}) %copy-start.6) | copy-done | bytes 8388632
  131.2 4.0 %shard_map.134 = bf16[128,1024]{1,0:T(8,128)(2,1)} custom-call(s32[64,16]{1,0:T(8,128)S(1)} %bitcast.63, f32[64,32]{1,0:T(8,128)S(1)} %bitcast.64, bf16[4096,1024]{1,0:T(8,128)(2,1)S(1)} %copy-done.6, bf16[128,1024]{1,0:T(8,128)(2,1)S(1)} %copy-done.4), custom_call_target="tpu_custom_call" | custom-call | flops 2500000000 | bytes 9000000 | tf_op jit(solution)/shard_map/pallas_call | solution.py:423
  (69 shorter events, 1.1 us)
Async XLA Ops:
  7.2 120.6 %all-gather.2.cloned.1.call-start = ((), (), s32[]{:S(2)}) async-start(), calls=%async_computation.3 | async-start | bytes 8519680 | tf_op jit(solution)/shard_map/all_gather | solution.py:441
  9.8 22.2 %all-to-all-start = ((s32[64,1,16]{2,1,0:T(1,128)}), s32[64,1,16]{2,1,0:T(1,128)S(1)}, u32[]{:S(2)}, u32[]{:S(2)}) async-start(s32[64,1,16]{2,1,0:T(1,128)} %bitcast.2), calls=%async_computation | async-start | bytes 65536 | tf_op jit(solution)/shard_map/all_to_all | solution.py:446
  34.5 1.3 copy-start
  35.7 4.9 %copy-start.1 = (bf16[64,1024]{1,0:T(8,128)(2,1)S(1)}, bf16[64,1024]{1,0:T(8,128)(2,1)}, u32[]{:S(2)}) copy-start(bf16[64,1024]{1,0:T(8,128)(2,1)} %q_ref) | copy-start | bytes 393220
  35.8 5.0 %copy-start.2 = (bf16[64,1024]{1,0:T(8,128)(2,1)S(1)}, bf16[64,1024]{1,0:T(8,128)(2,1)}, u32[]{:S(2)}) copy-start(bf16[64,1024]{1,0:T(8,128)(2,1)} %pos_ref) | copy-start | bytes 393220
  35.8 5.0 %copy-start.5 = (f32[1024]{0:T(1024)S(1)}, f32[1024]{0:T(1024)}, u32[]{:S(2)}) copy-start(f32[1024]{0:T(1024)} %param.17) | copy-start | bytes 12292
  35.8 58.5 %all-to-all-start.1 = ((bf16[64,112,128]{2,1,0:T(8,128)(2,1)}), bf16[64,112,128]{2,1,0:T(8,128)(2,1)S(1)}, u32[]{:S(2)}, u32[]{:S(2)}) async-start(bf16[64,112,128]{2,1,0:T(8,128)(2,1)} %bitcast.53), calls=%async_computation.1 | async-start | bytes 3670016 | tf_op jit(solution)/shard_map/all_to_all | solution.py:449
  40.8 10.3 %copy-start.7 = (bf16[2048,1024]{1,0:T(8,128)(2,1)S(1)}, bf16[2048,1024]{1,0:T(8,128)(2,1)}, u32[]{:S(2)}) copy-start(bf16[2048,1024]{1,0:T(8,128)(2,1)} %param.16) | copy-start | bytes 12582916
  45.0 6.0 %copy-start.12 = (bf16[256,1024]{1,0:T(8,128)(2,1)}, bf16[256,1024]{1,0:T(8,128)(2,1)S(1)}, u32[]{:S(2)}) copy-start(bf16[256,1024]{1,0:T(8,128)(2,1)S(1)} %get-tuple-element.80) | copy-start | bytes 1572868
  45.0 6.0 %copy-start.13 = (bf16[256,1024]{1,0:T(8,128)(2,1)}, bf16[256,1024]{1,0:T(8,128)(2,1)S(1)}, u32[]{:S(2)}) copy-start(bf16[256,1024]{1,0:T(8,128)(2,1)S(1)} %get-tuple-element.81) | copy-start | bytes 1572868
  46.0 5.1 %copy-start.15 = (f32[8,256]{1,0:T(8,128)}, f32[8,256]{1,0:T(8,128)S(1)}, u32[]{:S(2)}) copy-start(f32[8,256]{1,0:T(8,128)S(1)} %broadcast_in_dim.28) | copy-start | bytes 24580
  46.7 16.5 %collective-permute-start = (f32[152,256]{1,0:T(8,128)}, f32[152,256]{1,0:T(8,128)}, u32[]{:S(2)}, u32[]{:S(2)}) collective-permute-start(f32[152,256]{1,0:T(8,128)} %pad_maximum_fusion.1), channel_id=1, source_target_pairs={{0,1},{1,2},{2,3},{3,0},{4,5},{5,6},{6,7},{7,4},{8,9},{9,10},{10,1... | collective-permute-start | bytes 466952 | tf_op jit(solution)/shard_map/ppermute | solution.py:46
  48.0 15.3 %collective-permute-start.1 = (f32[152,256]{1,0:T(8,128)}, f32[152,256]{1,0:T(8,128)}, u32[]{:S(2)}, u32[]{:S(2)}) collective-permute-start(f32[152,256]{1,0:T(8,128)} %pad_maximum_fusion.1), channel_id=1, source_target_pairs={{0,3},{1,0},{2,1},{3,2},{4,7},{5,4},{6,5},{7,6},{8,11},{9,8},{10,9... | collective-permute-start | bytes 466952 | tf_op jit(solution)/shard_map/ppermute | solution.py:46
  49.4 13.9 %collective-permute-start.2 = (f32[152,256]{1,0:T(8,128)}, f32[152,256]{1,0:T(8,128)}, u32[]{:S(2)}, u32[]{:S(2)}) collective-permute-start(f32[152,256]{1,0:T(8,128)} %pad_maximum_fusion.1), channel_id=1, source_target_pairs={{0,2},{1,3},{2,0},{3,1},{4,6},{5,7},{6,4},{7,5},{8,10},{9,11},{10,... | collective-permute-start | bytes 466952 | tf_op jit(solution)/shard_map/ppermute | solution.py:46
  53.6 1.3 copy-start.9
  58.2 5.0 %copy-start.14 = (bf16[64,2048]{1,0:T(8,128)(2,1)S(1)}, bf16[64,2048]{1,0:T(8,128)(2,1)}, u32[]{:S(2)}) copy-start(bf16[64,2048]{1,0:T(8,128)(2,1)} %get-tuple-element.78) | copy-start | bytes 786436
  58.2 5.1 %copy-start.16 = (f32[8,256]{1,0:T(8,128)S(1)}, f32[8,256]{1,0:T(8,128)}, u32[]{:S(2)}) copy-start(f32[8,256]{1,0:T(8,128)} %copy-done.15) | copy-start | bytes 24580
  58.2 7.8 %collective-permute-start.3 = (bf16[64,2048]{1,0:T(8,128)(2,1)}, bf16[64,2048]{1,0:T(8,128)(2,1)S(1)}, u32[]{:S(2)}, u32[]{:S(2)}) collective-permute-start(bf16[64,2048]{1,0:T(8,128)(2,1)} %get-tuple-element.77), channel_id=1, source_target_pairs={{0,1},{1,2},{2,3},{3,0},{4,5},{5,6},{6,7},{7,4},{8,9},{9,10},{10,1... | collective-permute-start | bytes 786440 | tf_op jit(solution)/shard_map/ppermute | solution.py:46
  58.6 7.4 %collective-permute-start.4 = (bf16[64,2048]{1,0:T(8,128)(2,1)}, bf16[64,2048]{1,0:T(8,128)(2,1)S(1)}, u32[]{:S(2)}, u32[]{:S(2)}) collective-permute-start(bf16[64,2048]{1,0:T(8,128)(2,1)} %get-tuple-element.79), channel_id=1, source_target_pairs={{0,3},{1,0},{2,1},{3,2},{4,7},{5,4},{6,5},{7,6},{8,11},{9,8},{10,9... | collective-permute-start | bytes 786440 | tf_op jit(solution)/shard_map/ppermute | solution.py:46
  63.1 7.4 %collective-permute-start.5 = (bf16[64,2048]{1,0:T(8,128)(2,1)S(1)}, bf16[64,2048]{1,0:T(8,128)(2,1)S(1)}, u32[]{:S(2)}, u32[]{:S(2)}) collective-permute-start(bf16[64,2048]{1,0:T(8,128)(2,1)S(1)} %copy-done.14), channel_id=1, source_target_pairs={{0,2},{1,3},{2,0},{3,1},{4,6},{5,7},{6,4},{7,5},{8,10},{9,11},{10,... | collective-permute-start | bytes 786440 | tf_op jit(solution)/shard_map/ppermute | solution.py:46
  94.2 2.8 %copy-start.10 = (bf16[512,1024]{1,0:T(8,128)(2,1)S(1)}, bf16[512,1024]{1,0:T(8,128)(2,1)}, u32[]{:S(2)}) copy-start(bf16[512,1024]{1,0:T(8,128)(2,1)} %pad_maximum_fusion) | copy-start | bytes 3145732
  94.2 13.0 %copy-start.8 = (bf16[2048,1024]{1,0:T(8,128)(2,1)S(1)}, bf16[2048,1024]{1,0:T(8,128)(2,1)}, u32[]{:S(2)}) copy-start(bf16[2048,1024]{1,0:T(8,128)(2,1)} %param.16) | copy-start | bytes 12582916
  97.6 4.7 %collective-permute-start.6 = (f32[8,384]{1,0:T(8,128)S(1)}, f32[8,384]{1,0:T(8,128)S(1)}, u32[]{:S(2)}, u32[]{:S(2)}) collective-permute-start(f32[8,384]{1,0:T(8,128)S(1)} %select_maximum_fusion), channel_id=1, source_target_pairs={{0,1},{1,2},{2,3},{3,0},{4,5},{5,6},{6,7},{7,4},{8,9},{9,10},{10,1... | collective-permute-start | bytes 36872 | tf_op jit(solution)/shard_map/ppermute | solution.py:46
  99.2 3.2 %collective-permute-start.7 = (f32[8,384]{1,0:T(8,128)S(1)}, f32[8,384]{1,0:T(8,128)S(1)}, u32[]{:S(2)}, u32[]{:S(2)}) collective-permute-start(f32[8,384]{1,0:T(8,128)S(1)} %select_maximum_fusion), channel_id=1, source_target_pairs={{0,3},{1,0},{2,1},{3,2},{4,7},{5,4},{6,5},{7,6},{8,11},{9,8},{10,9... | collective-permute-start | bytes 36872 | tf_op jit(solution)/shard_map/ppermute | solution.py:46
  100.7 4.0 %collective-permute-start.8 = (f32[8,384]{1,0:T(8,128)S(1)}, f32[8,384]{1,0:T(8,128)S(1)}, u32[]{:S(2)}, u32[]{:S(2)}) collective-permute-start(f32[8,384]{1,0:T(8,128)S(1)} %select_maximum_fusion), channel_id=1, source_target_pairs={{0,2},{1,3},{2,0},{3,1},{4,6},{5,7},{6,4},{7,5},{8,10},{9,11},{10,... | collective-permute-start | bytes 36872 | tf_op jit(solution)/shard_map/ppermute | solution.py:46
  107.2 11.6 %copy-start.3 = (bf16[256,2048]{0,1:T(8,128)(2,1)S(1)}, bf16[256,2048]{0,1:T(8,128)(2,1)}, u32[]{:S(2)}) copy-start(bf16[256,2048]{0,1:T(8,128)(2,1)} %copy.16) | copy-start | bytes 3145732
  108.6 10.0 %collective-permute-start.9 = (f32[8,2048]{1,0:T(8,128)S(1)}, f32[8,2048]{1,0:T(8,128)S(1)}, u32[]{:S(2)}, u32[]{:S(2)}) collective-permute-start(f32[8,2048]{1,0:T(8,128)S(1)} %constant_dynamic-slice_fusion.2), channel_id=1, source_target_pairs={{0,3},{1,2},{2,1},{3,0},{4,7},{5,6},{6,5},{7,4},{8,11},{9,10},{10,... | collective-permute-start | bytes 196616 | tf_op jit(solution)/shard_map/ppermute | solution.py:50
  110.1 17.7 %all-to-all-start.2 = ((f32[64,1,32]{2,1,0:T(1,128)}), f32[64,1,32]{2,1,0:T(1,128)S(1)}, u32[]{:S(2)}, u32[]{:S(2)}) async-start(f32[64,1,32]{2,1,0:T(1,128)} %bitcast.18), calls=%async_computation.2 | async-start | bytes 65536 | tf_op jit(solution)/shard_map/all_to_all | solution.py:514
  118.7 3.2 %copy-start.11 = (f32[64,2048]{1,0:T(8,128)S(1)}, f32[64,2048]{1,0:T(8,128)}, u32[]{:S(2)}) copy-start(f32[64,2048]{1,0:T(8,128)} %convert_add_fusion) | copy-start | bytes 1572868
  118.7 3.1 %collective-permute-start.10 = (f32[4,2048]{1,0:T(4,128)S(1)}, f32[4,2048]{1,0:T(4,128)S(1)}, u32[]{:S(2)}, u32[]{:S(2)}) collective-permute-start(f32[4,2048]{1,0:T(4,128)S(1)} %constant_dynamic-slice_fusion.1), channel_id=1, source_target_pairs={{0,1},{1,0},{2,3},{3,2},{4,5},{5,4},{6,7},{7,6},{8,9},{9,8},{10,11... | collective-permute-start | bytes 98312 | tf_op jit(solution)/shard_map/ppermute | solution.py:50
  118.8 9.0 %copy-start.4 = (bf16[128,1024]{1,0:T(8,128)(2,1)S(1)}, bf16[128,1024]{1,0:T(8,128)(2,1)}, u32[]{:S(2)}) copy-start(bf16[128,1024]{1,0:T(8,128)(2,1)} %pool_ref.1) | copy-start | bytes 786436
  127.8 3.4 %copy-start.6 = (bf16[4096,1024]{1,0:T(8,128)(2,1)S(1)}, bf16[4096,1024]{1,0:T(8,128)(2,1)}, u32[]{:S(2)}) copy-start(bf16[4096,1024]{1,0:T(8,128)(2,1)} %all-gather.2.cloned.1.call-done.q_ref) | copy-start | bytes 25165828
Sparse Core Ops, SparseCore 0:
  10.8 100.1 all-gather.1

commit v4 on v3

--- a/solution.py
+++ b/solution.py
@@ -330,7 +330,8 @@
 
 
 def weight_kernel(
-    hidden_ref, gained_ref, rms_ref, shrink_ref, attn_ref, resid_ref, out_ref, held_ref, tile_ref, sems
+    hidden_ref, gained_ref, rms_ref, shrink_ref, attn_ref, q_ref,
+    resid_ref, out_ref, held_ref, tile_ref, sems,
 ):
     rms = to_column(rms_ref[...])
     shrink = to_column(shrink_ref[...])
@@ -352,7 +353,7 @@
         copy.wait()
 
 
-def weight_grads(hidden, gained, rms, shrink, attn_turned):
+def weight_grads(hidden, gained, rms, shrink, attn_turned, q_all):
     tokens, cols = hidden.shape
     rows = attn_turned.shape[0]
     blocks = 8
@@ -364,7 +365,7 @@
             jax.ShapeDtypeStruct((tokens, cols), BF16),
             jax.ShapeDtypeStruct((rows, cols), BF16),
         ),
-        in_specs=[vmem] * 5,
+        in_specs=[vmem] * 6,
         out_specs=(anywhere, anywhere),
         scratch_shapes=[
             pltpu.VMEM((tokens, cols), BF16),
@@ -375,7 +376,7 @@
         cost_estimate=pl.CostEstimate(
             flops=1100000000, bytes_accessed=7000000, transcendentals=0
         ),
-    )(hidden, gained, rms, shrink, attn_turned)
+    )(hidden, gained, rms, shrink, attn_turned, q_all)
 
 
 def pool_sum_kernel(code_ref, weight_ref, q_ref, pool_ref, out_ref, spread_ref):
@@ -519,7 +520,9 @@
     )
     gained_back = dot(halves, out_weight, 1, 1)
     gained_back = feature_scatter_small(gained_back[:CH_Q] + gained_back[CH_Q:])
-    resid_grad, weight_grad = weight_grads(hidden, gained, rms_row, shrink, attn_turned)
+    resid_grad, weight_grad = weight_grads(
+        hidden, gained, rms_row, shrink, attn_turned, q_all
+    )
     own = tokens // N_FS
     first = lax.axis_index("fsdp") * own
     own_rms = lax.dynamic_slice(rms_row[0], (first,), (own,))
@@ -528,6 +531,7 @@
         gained_back[:, None, :], (CH_Q // N_FS, QLEN, gained_back.shape[1])
     ).reshape(own, gained_back.shape[1])
     attn_grad = (own_rms[:, None] * gained_rows - own_shrink[:, None] * hidden_back).astype(BF16)
+    resid_grad, got = lax.optimization_barrier((resid_grad, got))
     pool_grad = pool_sum(wanted, got, q_all, pool)
     return (
         resid_grad,

time: 142 us -> 150 us (1.056)
  local copies, waits for them, and re-layouts: 10.5 us -> 15.2 us
  waiting for transfers between devices: 44.2 us -> 40 us
  other arithmetic: 8.19 us -> 11.7 us
  matrix products: 9.54 us -> 11.8 us
    unnamed x38 -> x76, local copies, waits for them, and re-layouts: 7.08 us -> 11.2 us
    ppermute x9, waiting for transfers between devices: 8.29 us -> 4.82 us  [shifted(): lax.ppermute(value, 'fsdp', [(i, (i + step) % N_FS) for i in range(N_FS)])]
    all_to_all x1, waiting for transfers between devices: 5.07 us -> 2.35 us  [per_device(): got = lax.all_to_all(sent, 'dp', split_axis=0, concat_axis=0, tiled=True)]
    ppermute x2, waiting for transfers between devices: 0.43 us -> 2.86 us  [swapped(): return lax.ppermute(value, 'fsdp', [(i, i ^ mask) for i in range(N_FS)])]
    dot_general x8, matrix products: 9.54 us -> 11.8 us  [dot(): lax.dot_general(a, b, (((ca,), (cb,)), ((), ())), preferred_element_type=...]
  transfers between devices with their start and end apart: 15 -> 15, of which waited for: 7 -> 6; matrix products, arithmetic and copies ran while one was open for 16% -> 19% of each run, Pallas kernels for 8% -> 8%
where the time goes in v4:
time: 150 us; the launch traced here: 149 us
  starting transfers between devices  40.4 us (27%)
  waiting for transfers between devices  40 us (27%)
  Pallas kernels  15.3 us (10%)
  local copies, waits for them, and re-layouts  15.2 us (10%)
  between operations  14.5 us (10%)
  matrix products  11.8 us (8%)
  other arithmetic  11.7 us (8%)
    all_to_all x1, waiting for transfers between devices, per_device(): lax.all_to_all(fetched, 'dp', split_axis=0, concat_axis=0, tiled=True)  21.7 us
    all_to_all x1, starting transfers between devices, per_device(): wanted = lax.all_to_all(code, 'dp', split_axis=0, concat_axis=0, tiled=True)  13 us
    dot_general x8, matrix products, dot(): lax.dot_general(a, b, (((ca,), (cb,)), ((), ())), preferred_element_type=...  11.8 us
    ppermute x9, starting transfers between devices, shifted(): lax.ppermute(value, 'fsdp', [(i, (i + step) % N_FS) for i in range(N_FS)])  11.8 us
    unnamed x76, local copies, waits for them, and re-layouts  11.2 us
    all_to_all x1, starting transfers between devices, per_device(): got = lax.all_to_all(sent, 'dp', split_axis=0, concat_axis=0, tiled=True)  9.15 us
    all_to_all x1, waiting for transfers between devices, per_device(): wanted = lax.all_to_all(code, 'dp', split_axis=0, concat_axis=0, tiled=True)  7.57 us
    all_to_all x1, starting transfers between devices, per_device(): lax.all_to_all(fetched, 'dp', split_axis=0, concat_axis=0, tiled=True)  4.93 us
  transfers between devices with their start and end apart: 15, of which 6 were waited for; matrix products, arithmetic and copies ran while one was open for 19% of the time, Pallas kernels for 8%

profile of v4, /device:TPU:1, one launch (start us, length us, event | category | flops | bytes accessed | tf_op | source)
XLA Modules:
  0.0 149.0 jit_solution(2164768446733191749)
XLA Ops:
  7.2 0.7 all-gather.2.cloned.1.call-update
  7.9 0.7 add_bitcast_fusion.name_ref
  8.6 1.2 shard_map.128
  9.9 13.0 %all-to-all-start = ((s32[64,1,16]{2,1,0:T(1,128)}), s32[64,1,16]{2,1,0:T(1,128)S(1)}, u32[]{:S(2)}, u32[]{:S(2)}) async-start(s32[64,1,16]{2,1,0:T(1,128)} %bitcast.2), calls=%async_computation | async-start | bytes 65536 | tf_op jit(solution)/shard_map/all_to_all | solution.py:447
  22.9 0.6 iota_compare_fusion.1
  23.5 1.0 copy.18
  24.5 7.6 %all-to-all-done = s32[64,1,16]{2,1,0:T(1,128)S(1)} async-done(((s32[64,1,16]{2,1,0:T(1,128)}), s32[64,1,16]{2,1,0:T(1,128)S(1)}, u32[]{:S(2)}, u32[]{:S(2)}) %all-to-all-start) | async-done | bytes 4128 | tf_op jit(solution)/shard_map/all_to_all | solution.py:447
  32.1 2.4 %shard_map.129 = bf16[64,14,8,128]{3,2,1,0:T(8,128)(2,1)S(1)} custom-call(s32[64,16]{1,0:T(8,128)S(1)} %bitcast.62, bf16[128,8,128]{2,1,0:T(8,128)(2,1)S(1)} %bitcast.56), custom_call_target="tpu_custom_call" | custom-call | bytes 3670016 | tf_op jit(solution)/shard_map/pallas_call | solution.py:157
  34.5 1.2 copy-done.2
  35.8 4.9 %all-to-all-start.1 = ((bf16[64,112,128]{2,1,0:T(8,128)(2,1)}), bf16[64,112,128]{2,1,0:T(8,128)(2,1)S(1)}, u32[]{:S(2)}, u32[]{:S(2)}) async-start(bf16[64,112,128]{2,1,0:T(8,128)(2,1)} %bitcast.53), calls=%async_computation.1 | async-start | bytes 3670016 | tf_op jit(solution)/shard_map/all_to_all | solution.py:450
  40.8 4.3 %multiply_convert_fusion = (bf16[256,1024]{1,0:T(8,128)(2,1)S(1)}, bf16[256,1024]{1,0:T(8,128)(2,1)S(1)}, f32[256]{0:T(256)S(1)}, f32[256,1024]{1,0:T(8,128)S(1)}) fusion(f32[1024]{0:T(1024)S(1)} %copy-done.15, bf16[256,2048]{1,0:T(8,128)(2,1)} %param.15, bf16[2048,1024]{1,0:T(8,128)(2,1)} %param.16, bf16[256,1024]{1,0:T(8,128)(2,1)} %param.14), kind=kOutput, calls=%fused_computation.6 | convolution fusion | flops 1076100864 | bytes 7869440 | tf_op jit(solution)/shard_map/dot_general | solution.py:31
  46.0 0.7 pad_maximum_fusion.1
  46.7 1.3 collective-permute-start
  48.0 1.4 collective-permute-start.1
  49.4 1.6 %collective-permute-start.2 = (f32[152,256]{1,0:T(8,128)}, f32[152,256]{1,0:T(8,128)}, u32[]{:S(2)}, u32[]{:S(2)}) collective-permute-start(f32[152,256]{1,0:T(8,128)} %pad_maximum_fusion.1), channel_id=1, source_target_pairs={{0,2},{1,3},{2,0},{3,1},{4,6},{5,7},{6,4},{7,5},{8,10},{9,11},{10,... | collective-permute-start | bytes 466952 | tf_op jit(solution)/shard_map/ppermute | solution.py:46
  51.1 1.3 fusion.3
  52.4 1.3 convolution_add_fusion
  53.7 1.3 copy-done.23
  55.0 0.9 dynamic-slice_convert_fusion.2
  55.9 2.3 %copy.16 = bf16[256,2048]{0,1:T(8,128)(2,1)} copy(bf16[256,2048]{1,0:T(8,128)(2,1)} %param.15) | data formatting | bytes 2097152 | tf_op jit(solution)/shard_map/optimization_barrier | solution.py:452
  58.6 2.3 %collective-permute-start.4 = (bf16[64,2048]{1,0:T(8,128)(2,1)}, bf16[64,2048]{1,0:T(8,128)(2,1)S(1)}, u32[]{:S(2)}, u32[]{:S(2)}) collective-permute-start(bf16[64,2048]{1,0:T(8,128)(2,1)} %get-tuple-element.83), channel_id=1, source_target_pairs={{0,3},{1,0},{2,1},{3,2},{4,7},{5,4},{6,5},{7,6},{8,11},{9,8},{10,9... | collective-permute-start | bytes 786440 | tf_op jit(solution)/shard_map/ppermute | solution.py:46
  60.9 2.3 %pad_maximum_fusion = bf16[512,1024]{1,0:T(8,128)(2,1)} fusion(bf16[256,1024]{1,0:T(8,128)(2,1)} %copy-done.29, bf16[256,1024]{1,0:T(8,128)(2,1)} %copy-done.28), kind=kLoop, calls=%fused_computation.2 | loop fusion | flops 2097152 | bytes 2097152 | tf_op jit(solution)/shard_map/concatenate | solution.py:458
  63.3 1.1 add_add_fusion
  65.1 0.7 fusion.22
  65.8 0.7 exponential_reduce_fusion
  67.1 0.6 slice.70.scaled_pos_ref
  67.7 0.6 fusion.15.rms_ref
  68.3 2.3 %collective-permute-done.5 = bf16[64,2048]{1,0:T(8,128)(2,1)S(1)} collective-permute-done((bf16[64,2048]{1,0:T(8,128)(2,1)S(1)}, bf16[64,2048]{1,0:T(8,128)(2,1)S(1)}, u32[]{:S(2)}, u32[]{:S(2)}) %collective-permute-start.5) | collective-permute-done | bytes 262176 | tf_op jit(solution)/shard_map/ppermute | solution.py:46
  70.6 2.0 %convert_add_fusion = f32[64,2048]{1,0:T(8,128)} fusion(bf16[64,2048]{1,0:T(8,128)(2,1)S(1)} %collective-permute-done.5, bf16[64,2048]{1,0:T(8,128)(2,1)S(1)} %collective-permute-done.4, bf16[64,2048]{1,0:T(8,128)(2,1)S(1)} %collective-permute-done.3, f32[256,2048]{1,0:T(8,128)} %copy-done.23, s32[]{:T(128)S(6)} %select_n.58), kind=kLoop, calls=%fused_computation.10 | loop fusion | flops 786432 | bytes 1835012 | tf_op jit(solution)/shard_map/add | solution.py:77
  72.6 21.7 %all-to-all-done.1 = bf16[64,112,128]{2,1,0:T(8,128)(2,1)S(1)} async-done(((bf16[64,112,128]{2,1,0:T(8,128)(2,1)}), bf16[64,112,128]{2,1,0:T(8,128)(2,1)S(1)}, u32[]{:S(2)}, u32[]{:S(2)}) %all-to-all-start.1) | async-done | bytes 1835040 | tf_op jit(solution)/shard_map/all_to_all | solution.py:450
  94.3 0.7 copy-done.19
  95.0 2.8 %shard_map.130 = (f32[16,64]{1,0:T(8,128)S(1)}, bf16[112,8,128]{2,1,0:T(8,128)(2,1)S(1)}) custom-call(s32[1,448]{1,0:T(1,128)S(1)} %copy-done.19, bf16[896,8,128]{2,1,0:T(8,128)(2,1)S(1)} %bitcast.52, bf16[64,8,128]{2,1,0:T(8,128)(2,1)S(1)} %bitcast.60), custom_call_target="tpu_custom_call" | custom-call | flops 2000000 | bytes 2200000 | tf_op jit(solution)/shard_map/pallas_call | solution.py:196
  98.4 1.5 %collective-permute-start.6 = (f32[8,384]{1,0:T(8,128)S(1)}, f32[8,384]{1,0:T(8,128)S(1)}, u32[]{:S(2)}, u32[]{:S(2)}) collective-permute-start(f32[8,384]{1,0:T(8,128)S(1)} %select_maximum_fusion), channel_id=1, source_target_pairs={{0,1},{1,2},{2,3},{3,0},{4,5},{5,6},{6,7},{7,4},{8,9},{9,10},{10,1... | collective-permute-start | bytes 36872 | tf_op jit(solution)/shard_map/ppermute | solution.py:46
  100.0 1.6 %collective-permute-start.7 = (f32[8,384]{1,0:T(8,128)S(1)}, f32[8,384]{1,0:T(8,128)S(1)}, u32[]{:S(2)}, u32[]{:S(2)}) collective-permute-start(f32[8,384]{1,0:T(8,128)S(1)} %select_maximum_fusion), channel_id=1, source_target_pairs={{0,3},{1,0},{2,1},{3,2},{4,7},{5,4},{6,5},{7,6},{8,11},{9,8},{10,9... | collective-permute-start | bytes 36872 | tf_op jit(solution)/shard_map/ppermute | solution.py:46
  101.5 1.5 %collective-permute-start.8 = (f32[8,384]{1,0:T(8,128)S(1)}, f32[8,384]{1,0:T(8,128)S(1)}, u32[]{:S(2)}, u32[]{:S(2)}) collective-permute-start(f32[8,384]{1,0:T(8,128)S(1)} %select_maximum_fusion), channel_id=1, source_target_pairs={{0,2},{1,3},{2,0},{3,1},{4,6},{5,7},{6,4},{7,5},{8,10},{9,11},{10,... | collective-permute-start | bytes 36872 | tf_op jit(solution)/shard_map/ppermute | solution.py:46
  103.1 2.5 %collective-permute-done.8 = f32[8,384]{1,0:T(8,128)S(1)} collective-permute-done((f32[8,384]{1,0:T(8,128)S(1)}, f32[8,384]{1,0:T(8,128)S(1)}, u32[]{:S(2)}, u32[]{:S(2)}) %collective-permute-start.8) | collective-permute-done | bytes 12320 | tf_op jit(solution)/shard_map/ppermute | solution.py:46
  105.7 1.2 shard_map.131
  106.9 1.2 shard_map.132
  108.1 3.6 %fusion.27 = f32[32,2048]{1,0:T(8,128)S(1)} fusion(bf16[32,1024]{1,0:T(8,128)(2,1)S(1)} %get-tuple-element.72, bf16[2048,1024]{1,0:T(8,128)(2,1)} %param.16), kind=kOutput, calls=%fused_computation.71 | convolution fusion | flops 134217728 | bytes 4521984 | tf_op jit(solution)/shard_map/dot_general | solution.py:31
  111.8 1.5 collective-permute-start.9
  113.4 2.9 %collective-permute-done.9 = f32[8,2048]{1,0:T(8,128)S(1)} collective-permute-done((f32[8,2048]{1,0:T(8,128)S(1)}, f32[8,2048]{1,0:T(8,128)S(1)}, u32[]{:S(2)}, u32[]{:S(2)}) %collective-permute-start.9) | collective-permute-done | bytes 65568 | tf_op jit(solution)/shard_map/ppermute | solution.py:50
  116.4 9.2 %all-to-all-start.2 = ((f32[64,1,32]{2,1,0:T(1,128)}), f32[64,1,32]{2,1,0:T(1,128)S(1)}, u32[]{:S(2)}, u32[]{:S(2)}) async-start(f32[64,1,32]{2,1,0:T(1,128)} %bitcast.14), calls=%async_computation.2 | async-start | bytes 65536 | tf_op jit(solution)/shard_map/all_to_all | solution.py:515
  125.6 0.8 fusion.1
  126.5 3.4 %copy-done = bf16[4096,1024]{1,0:T(8,128)(2,1)S(1)} copy-done((bf16[4096,1024]{1,0:T(8,128)(2,1)S(1)}, bf16[4096,1024]{1,0:T(8,128)(2,1)}, u32[]{:S(2)}) %copy-start) | copy-done | bytes 8388632
  129.9 2.6 %shard_map.133 = (bf16[256,1024]{1,0:T(8,128)(2,1)}, bf16[2048,1024]{1,0:T(8,128)(2,1)}) custom-call(f32[256,1024]{1,0:T(8,128)S(1)} %get-tuple-element.46.hidden_ref, f32[16,1024]{1,0:T(8,128)S(1)} %get-tuple-element.66.gained_ref, f32[1,256]{1,0:T(1,128)S(1)} %copy-done.13, f32[1,256]{1,0:T(1,128)S(1)} %get-tuple-element.67.shrink_ref, ...), custom_call_target="tpu_custom_call" | custom-call | flops 1100000000 | bytes 7000000 | tf_op jit(solution)/shard_map/pallas_call | solution.py:362
  132.5 2.3 %all-to-all-done.2 = f32[64,1,32]{2,1,0:T(1,128)S(1)} async-done(((f32[64,1,32]{2,1,0:T(1,128)}), f32[64,1,32]{2,1,0:T(1,128)S(1)}, u32[]{:S(2)}, u32[]{:S(2)}) %all-to-all-start.2) | async-done | bytes 8224 | tf_op jit(solution)/shard_map/all_to_all | solution.py:515
  134.8 3.4 %copy-done.1 = bf16[4096,1024]{1,0:T(8,128)(2,1)S(1)} copy-done((bf16[4096,1024]{1,0:T(8,128)(2,1)S(1)}, bf16[4096,1024]{1,0:T(8,128)(2,1)}, u32[]{:S(2)}) %copy-start.1) | copy-done | bytes 8388632
  138.2 3.9 %shard_map.134 = bf16[128,1024]{1,0:T(8,128)(2,1)} custom-call(s32[64,16]{1,0:T(8,128)S(1)} %bitcast.63, f32[64,32]{1,0:T(8,128)S(1)} %bitcast.64, bf16[4096,1024]{1,0:T(8,128)(2,1)S(1)} %copy-done.1, bf16[128,1024]{1,0:T(8,128)(2,1)S(1)} %copy-done.7), custom_call_target="tpu_custom_call" | custom-call | flops 2500000000 | bytes 9000000 | tf_op jit(solution)/shard_map/pallas_call | solution.py:424
  (107 shorter events, 4.0 us)
Async XLA Ops:
  7.2 119.3 %all-gather.2.cloned.1.call-start = ((), (), s32[]{:S(2)}) async-start(), calls=%async_computation.3 | async-start | bytes 8519680 | tf_op jit(solution)/shard_map/all_gather | solution.py:442
  9.8 13.6 %copy-start.11 = (bf16[64,448]{1,0:T(8,128)(2,1)}, bf16[64,448]{1,0:T(8,128)(2,1)S(1)}, u32[]{:S(2)}) copy-start(bf16[64,448]{1,0:T(8,128)(2,1)S(1)} %get-tuple-element.54.owner_ref) | copy-start | bytes 172036
  9.8 13.6 %copy-start.18 = (s32[1,448]{1,0:T(1,128)}, s32[1,448]{1,0:T(1,128)S(1)}, u32[]{:S(2)}) copy-start(s32[1,448]{1,0:T(1,128)S(1)} %get-tuple-element.47.slot_ref) | copy-start | bytes 5380
  9.9 22.2 %all-to-all-start = ((s32[64,1,16]{2,1,0:T(1,128)}), s32[64,1,16]{2,1,0:T(1,128)S(1)}, u32[]{:S(2)}, u32[]{:S(2)}) async-start(s32[64,1,16]{2,1,0:T(1,128)} %bitcast.2), calls=%async_computation | async-start | bytes 65536 | tf_op jit(solution)/shard_map/all_to_all | solution.py:447
  32.1 3.7 %copy-start.8 = (s32[64,1,16]{2,1,0:T(1,128)}, s32[64,1,16]{2,1,0:T(1,128)S(1)}, u32[]{:S(2)}) copy-start(s32[64,1,16]{2,1,0:T(1,128)S(1)} %all-to-all-done) | copy-start | bytes 12292
  35.7 4.9 %copy-start.4 = (bf16[64,1024]{1,0:T(8,128)(2,1)S(1)}, bf16[64,1024]{1,0:T(8,128)(2,1)}, u32[]{:S(2)}) copy-start(bf16[64,1024]{1,0:T(8,128)(2,1)} %q_ref) | copy-start | bytes 393220
  35.7 5.0 %copy-start.5 = (bf16[64,1024]{1,0:T(8,128)(2,1)S(1)}, bf16[64,1024]{1,0:T(8,128)(2,1)}, u32[]{:S(2)}) copy-start(bf16[64,1024]{1,0:T(8,128)(2,1)} %pos_ref) | copy-start | bytes 393220
  35.7 5.0 %copy-start.15 = (f32[1024]{0:T(1024)S(1)}, f32[1024]{0:T(1024)}, u32[]{:S(2)}) copy-start(f32[1024]{0:T(1024)} %param.17) | copy-start | bytes 12292
  35.8 58.5 %all-to-all-start.1 = ((bf16[64,112,128]{2,1,0:T(8,128)(2,1)}), bf16[64,112,128]{2,1,0:T(8,128)(2,1)S(1)}, u32[]{:S(2)}, u32[]{:S(2)}) async-start(bf16[64,112,128]{2,1,0:T(8,128)(2,1)} %bitcast.53), calls=%async_computation.1 | async-start | bytes 3670016 | tf_op jit(solution)/shard_map/all_to_all | solution.py:450
  40.8 10.3 %copy-start.22 = (bf16[2048,1024]{1,0:T(8,128)(2,1)S(1)}, bf16[2048,1024]{1,0:T(8,128)(2,1)}, u32[]{:S(2)}) copy-start(bf16[2048,1024]{1,0:T(8,128)(2,1)} %param.16) | copy-start | bytes 12582916
  45.0 6.0 %copy-start.28 = (bf16[256,1024]{1,0:T(8,128)(2,1)}, bf16[256,1024]{1,0:T(8,128)(2,1)S(1)}, u32[]{:S(2)}) copy-start(bf16[256,1024]{1,0:T(8,128)(2,1)S(1)} %get-tuple-element.84) | copy-start | bytes 1572868
  45.0 6.0 %copy-start.29 = (bf16[256,1024]{1,0:T(8,128)(2,1)}, bf16[256,1024]{1,0:T(8,128)(2,1)S(1)}, u32[]{:S(2)}) copy-start(bf16[256,1024]{1,0:T(8,128)(2,1)S(1)} %get-tuple-element.85) | copy-start | bytes 1572868
  45.8 6.6 %copy-start.26 = (f32[80,256]{1,0:T(8,128)}, f32[80,256]{1,0:T(8,128)S(1)}, u32[]{:S(2)}) copy-start(f32[80,256]{1,0:T(8,128)S(1)} %slice_add_fusion.2) | copy-start | bytes 245764
  46.0 5.1 %copy-start.30 = (f32[64,128]{1,0:T(8,128)}, f32[64,128]{1,0:T(8,128)S(1)}, u32[]{:S(2)}) copy-start(f32[64,128]{1,0:T(8,128)S(1)} %fusion.26) | copy-start | bytes 98308
  46.7 16.5 %collective-permute-start = (f32[152,256]{1,0:T(8,128)}, f32[152,256]{1,0:T(8,128)}, u32[]{:S(2)}, u32[]{:S(2)}) collective-permute-start(f32[152,256]{1,0:T(8,128)} %pad_maximum_fusion.1), channel_id=1, source_target_pairs={{0,1},{1,2},{2,3},{3,0},{4,5},{5,6},{6,7},{7,4},{8,9},{9,10},{10,1... | collective-permute-start | bytes 466952 | tf_op jit(solution)/shard_map/ppermute | solution.py:46
  48.0 15.3 %collective-permute-start.1 = (f32[152,256]{1,0:T(8,128)}, f32[152,256]{1,0:T(8,128)}, u32[]{:S(2)}, u32[]{:S(2)}) collective-permute-start(f32[152,256]{1,0:T(8,128)} %pad_maximum_fusion.1), channel_id=1, source_target_pairs={{0,3},{1,0},{2,1},{3,2},{4,7},{5,4},{6,5},{7,6},{8,11},{9,8},{10,9... | collective-permute-start | bytes 466952 | tf_op jit(solution)/shard_map/ppermute | solution.py:46
  49.4 13.9 %collective-permute-start.2 = (f32[152,256]{1,0:T(8,128)}, f32[152,256]{1,0:T(8,128)}, u32[]{:S(2)}, u32[]{:S(2)}) collective-permute-start(f32[152,256]{1,0:T(8,128)} %pad_maximum_fusion.1), channel_id=1, source_target_pairs={{0,2},{1,3},{2,0},{3,1},{4,6},{5,7},{6,4},{7,5},{8,10},{9,11},{10,... | collective-permute-start | bytes 466952 | tf_op jit(solution)/shard_map/ppermute | solution.py:46
  53.7 1.3 copy-start.23
  55.9 7.4 %copy-start.27 = (f32[80,256]{1,0:T(8,128)S(1)}, f32[80,256]{1,0:T(8,128)}, u32[]{:S(2)}) copy-start(f32[80,256]{1,0:T(8,128)} %copy-done.26) | copy-start | bytes 245764
  55.9 7.4 %copy-start.31 = (f32[64,128]{1,0:T(8,128)S(1)}, f32[64,128]{1,0:T(8,128)}, u32[]{:S(2)}) copy-start(f32[64,128]{1,0:T(8,128)} %copy-done.30) | copy-start | bytes 98308
  58.2 5.0 %copy-start.32 = (bf16[64,2048]{1,0:T(8,128)(2,1)S(1)}, bf16[64,2048]{1,0:T(8,128)(2,1)}, u32[]{:S(2)}) copy-start(bf16[64,2048]{1,0:T(8,128)(2,1)} %get-tuple-element.82) | copy-start | bytes 786436
  58.2 8.3 %copy-start.35 = (s32[256]{0:T(256)S(1)}, s32[256]{0:T(256)}, u32[]{:S(2)}) copy-start(s32[256]{0:T(256)} %copy-done.34) | copy-start | bytes 3076
  58.2 10.1 %collective-permute-start.3 = (bf16[64,2048]{1,0:T(8,128)(2,1)}, bf16[64,2048]{1,0:T(8,128)(2,1)S(1)}, u32[]{:S(2)}, u32[]{:S(2)}) collective-permute-start(bf16[64,2048]{1,0:T(8,128)(2,1)} %get-tuple-element.81), channel_id=1, source_target_pairs={{0,1},{1,2},{2,3},{3,0},{4,5},{5,6},{6,7},{7,4},{8,9},{9,10},{10,1... | collective-permute-start | bytes 786440 | tf_op jit(solution)/shard_map/ppermute | solution.py:46
  58.6 9.8 %collective-permute-start.4 = (bf16[64,2048]{1,0:T(8,128)(2,1)}, bf16[64,2048]{1,0:T(8,128)(2,1)S(1)}, u32[]{:S(2)}, u32[]{:S(2)}) collective-permute-start(bf16[64,2048]{1,0:T(8,128)(2,1)} %get-tuple-element.83), channel_id=1, source_target_pairs={{0,3},{1,0},{2,1},{3,2},{4,7},{5,4},{6,5},{7,6},{8,11},{9,8},{10,9... | collective-permute-start | bytes 786440 | tf_op jit(solution)/shard_map/ppermute | solution.py:46
  63.2 7.4 %collective-permute-start.5 = (bf16[64,2048]{1,0:T(8,128)(2,1)S(1)}, bf16[64,2048]{1,0:T(8,128)(2,1)S(1)}, u32[]{:S(2)}, u32[]{:S(2)}) collective-permute-start(bf16[64,2048]{1,0:T(8,128)(2,1)S(1)} %copy-done.32), channel_id=1, source_target_pairs={{0,2},{1,3},{2,0},{3,1},{4,6},{5,7},{6,4},{7,5},{8,10},{9,11},{10,... | collective-permute-start | bytes 786440 | tf_op jit(solution)/shard_map/ppermute | solution.py:46
  94.3 4.1 %copy-start.33 = (pred[16,256]{1,0:T(8,128)(4,1)S(1)}, pred[16,256]{1,0:T(8,128)(4,1)}, u32[]{:S(2)}) copy-start(pred[16,256]{1,0:T(8,128)(4,1)} %iota_compare_fusion.1) | copy-start | bytes 12292
  95.0 2.9 %copy-start.24 = (bf16[512,1024]{1,0:T(8,128)(2,1)S(1)}, bf16[512,1024]{1,0:T(8,128)(2,1)}, u32[]{:S(2)}) copy-start(bf16[512,1024]{1,0:T(8,128)(2,1)} %pad_maximum_fusion) | copy-start | bytes 3145732
  97.7 8.0 %copy-start.12 = (bf16[64,448]{1,0:T(8,128)(2,1)S(1)}, bf16[64,448]{1,0:T(8,128)(2,1)}, u32[]{:S(2)}) copy-start(bf16[64,448]{1,0:T(8,128)(2,1)} %copy-done.11) | copy-start | bytes 172036
  97.7 8.0 %copy-start.14 = (f32[1,64]{1,0:T(1,128)S(1)}, f32[1,64]{1,0:T(1,128)}, u32[]{:S(2)}) copy-start(f32[1,64]{1,0:T(1,128)} %get-tuple-element.53.inv_q_ref) | copy-start | bytes 772
  97.7 8.0 %copy-start.20 = (f32[64]{0:T(128)S(1)}, f32[64]{0:T(128)}, u32[]{:S(2)}) copy-start(f32[64]{0:T(128)} %exponential_reduce_fusion) | copy-start | bytes 772
  97.7 9.2 %copy-start.6 = (f32[64,256]{1,0:T(8,128)S(1)}, f32[64,256]{1,0:T(8,128)}, u32[]{:S(2)}) copy-start(f32[64,256]{1,0:T(8,128)} %slice.70.scaled_pos_ref) | copy-start | bytes 196612
  97.7 9.2 %copy-start.10 = (f32[64,64]{1,0:T(8,128)S(1)}, f32[64,64]{1,0:T(8,128)}, u32[]{:S(2)}) copy-start(f32[64,64]{1,0:T(8,128)} %get-tuple-element.60.exp_ref) | copy-start | bytes 49156
  97.8 9.1 %copy-start.13 = (f32[1,256]{1,0:T(1,128)S(1)}, f32[1,256]{1,0:T(1,128)}, u32[]{:S(2)}) copy-start(f32[1,256]{1,0:T(1,128)} %fusion.15.rms_ref) | copy-start | bytes 3076
  97.8 9.1 %copy-start.16 = (f32[1024]{0:T(1024)S(1)}, f32[1024]{0:T(1024)}, u32[]{:S(2)}) copy-start(f32[1024]{0:T(1024)} %param.17) | copy-start | bytes 12292
  97.8 9.1 %copy-start.17 = (f32[256]{0:T(256)S(1)}, f32[256]{0:T(256)}, u32[]{:S(2)}) copy-start(f32[256]{0:T(256)} %fusion.13) | copy-start | bytes 3076
  97.8 9.1 %copy-start.21 = (f32[1,64]{1,0:T(1,128)S(1)}, f32[1,64]{1,0:T(1,128)}, u32[]{:S(2)}) copy-start(f32[1,64]{1,0:T(1,128)} %get-tuple-element.62.inv_p_ref) | copy-start | bytes 772
  98.4 4.6 %collective-permute-start.6 = (f32[8,384]{1,0:T(8,128)S(1)}, f32[8,384]{1,0:T(8,128)S(1)}, u32[]{:S(2)}, u32[]{:S(2)}) collective-permute-start(f32[8,384]{1,0:T(8,128)S(1)} %select_maximum_fusion), channel_id=1, source_target_pairs={{0,1},{1,2},{2,3},{3,0},{4,5},{5,6},{6,7},{7,4},{8,9},{9,10},{10,1... | collective-permute-start | bytes 36872 | tf_op jit(solution)/shard_map/ppermute | solution.py:46
  100.0 3.1 %collective-permute-start.7 = (f32[8,384]{1,0:T(8,128)S(1)}, f32[8,384]{1,0:T(8,128)S(1)}, u32[]{:S(2)}, u32[]{:S(2)}) collective-permute-start(f32[8,384]{1,0:T(8,128)S(1)} %select_maximum_fusion), channel_id=1, source_target_pairs={{0,3},{1,0},{2,1},{3,2},{4,7},{5,4},{6,5},{7,6},{8,11},{9,8},{10,9... | collective-permute-start | bytes 36872 | tf_op jit(solution)/shard_map/ppermute | solution.py:46
  101.5 4.1 %collective-permute-start.8 = (f32[8,384]{1,0:T(8,128)S(1)}, f32[8,384]{1,0:T(8,128)S(1)}, u32[]{:S(2)}, u32[]{:S(2)}) collective-permute-start(f32[8,384]{1,0:T(8,128)S(1)} %select_maximum_fusion), channel_id=1, source_target_pairs={{0,2},{1,3},{2,0},{3,1},{4,6},{5,7},{6,4},{7,5},{8,10},{9,11},{10,... | collective-permute-start | bytes 36872 | tf_op jit(solution)/shard_map/ppermute | solution.py:46
  108.1 17.5 %copy-start.25 = (f32[64,2048]{1,0:T(8,128)S(1)}, f32[64,2048]{1,0:T(8,128)}, u32[]{:S(2)}) copy-start(f32[64,2048]{1,0:T(8,128)} %convert_add_fusion) | copy-start | bytes 1572868
  108.1 18.4 %copy-start.3 = (bf16[256,2048]{0,1:T(8,128)(2,1)S(1)}, bf16[256,2048]{0,1:T(8,128)(2,1)}, u32[]{:S(2)}) copy-start(bf16[256,2048]{0,1:T(8,128)(2,1)} %copy.16) | copy-start | bytes 3145732
  111.8 4.4 %collective-permute-start.9 = (f32[8,2048]{1,0:T(8,128)S(1)}, f32[8,2048]{1,0:T(8,128)S(1)}, u32[]{:S(2)}, u32[]{:S(2)}) collective-permute-start(f32[8,2048]{1,0:T(8,128)S(1)} %constant_dynamic-slice_fusion.2), channel_id=1, source_target_pairs={{0,3},{1,2},{2,1},{3,0},{4,7},{5,6},{6,5},{7,4},{8,11},{9,10},{10,... | collective-permute-start | bytes 196616 | tf_op jit(solution)/shard_map/ppermute | solution.py:50
  116.3 9.3 %collective-permute-start.10 = (f32[4,2048]{1,0:T(4,128)S(1)}, f32[4,2048]{1,0:T(4,128)S(1)}, u32[]{:S(2)}, u32[]{:S(2)}) collective-permute-start(f32[4,2048]{1,0:T(4,128)S(1)} %constant_dynamic-slice_fusion.1), channel_id=1, source_target_pairs={{0,1},{1,0},{2,3},{3,2},{4,5},{5,4},{6,7},{7,6},{8,9},{9,8},{10,11... | collective-permute-start | bytes 98312 | tf_op jit(solution)/shard_map/ppermute | solution.py:50
  116.4 18.4 %all-to-all-start.2 = ((f32[64,1,32]{2,1,0:T(1,128)}), f32[64,1,32]{2,1,0:T(1,128)S(1)}, u32[]{:S(2)}, u32[]{:S(2)}) async-start(f32[64,1,32]{2,1,0:T(1,128)} %bitcast.14), calls=%async_computation.2 | async-start | bytes 65536 | tf_op jit(solution)/shard_map/all_to_all | solution.py:515
  126.5 3.4 %copy-start = (bf16[4096,1024]{1,0:T(8,128)(2,1)S(1)}, bf16[4096,1024]{1,0:T(8,128)(2,1)}, u32[]{:S(2)}) copy-start(bf16[4096,1024]{1,0:T(8,128)(2,1)} %all-gather.2.cloned.1.call-done.q_ref) | copy-start | bytes 25165828
  129.9 4.9 %copy-start.7 = (bf16[128,1024]{1,0:T(8,128)(2,1)S(1)}, bf16[128,1024]{1,0:T(8,128)(2,1)}, u32[]{:S(2)}) copy-start(bf16[128,1024]{1,0:T(8,128)(2,1)} %pool_ref.1) | copy-start | bytes 786436
  129.9 4.9 %copy-start.9 = (s32[64,1,16]{2,1,0:T(1,128)S(1)}, s32[64,1,16]{2,1,0:T(1,128)}, u32[]{:S(2)}) copy-start(s32[64,1,16]{2,1,0:T(1,128)} %copy-done.8) | copy-start | bytes 12292
  134.8 3.4 %copy-start.1 = (bf16[4096,1024]{1,0:T(8,128)(2,1)S(1)}, bf16[4096,1024]{1,0:T(8,128)(2,1)}, u32[]{:S(2)}) copy-start(bf16[4096,1024]{1,0:T(8,128)(2,1)} %all-gather.2.cloned.1.call-done.q_ref) | copy-start | bytes 25165828
  (3 other events, 2.6 us)
Sparse Core Ops, SparseCore 0:
  10.8 100.1 all-gather.1

commit v5 on v3

--- a/solution.py
+++ b/solution.py
@@ -42,6 +42,13 @@
     return hi, (a - hi.astype(F32)).astype(BF16)
 
 
+def thirds(a):
+    hi = a.astype(BF16)
+    rest = a - hi.astype(F32)
+    mid = rest.astype(BF16)
+    return hi, mid, (rest - mid.astype(F32)).astype(BF16)
+
+
 def shifted(value, step):
     return lax.ppermute(value, "fsdp", [(i, (i + step) % N_FS) for i in range(N_FS)])
 
@@ -92,7 +99,8 @@
     width = period * times
     down = lax.broadcasted_iota(jnp.int32, (period, width), 0)
     along = lax.broadcasted_iota(jnp.int32, (period, width), 1)
-    return dot_exact(values, (along % period == down).astype(F32), 1, 0)
+    mask = (along % period == down).astype(F32).astype(BF16)
+    return sum(dot(part, mask, 1, 0) for part in thirds(values))
 
 
 def flat_row(values, times):
@@ -188,7 +196,9 @@
     for part, ref in ((0, cos_ref), (1, sq_ref)):
         total = jnp.zeros((SUB, Q_GRP), F32)
         for k in range(NEG):
-            total += dot_exact((line == k).astype(F32), ref[k * Q_GRP : (k + 1) * Q_GRP, :], 1, 1)
+            mask = (line == k).astype(F32).astype(BF16)
+            for piece in thirds(ref[k * Q_GRP : (k + 1) * Q_GRP, :]):
+                total += dot(mask, piece, 1, 1)
         sums_ref[part * SUB : (part + 1) * SUB, :] = total
 
 
@@ -299,7 +309,8 @@
     mine = lax.broadcasted_iota(jnp.int32, (CH_Q, tokens), 1) // QLEN == down
     inner = dot_exact(of_pos, scaled_pos_ref[...], 1, 0) - scale_own[:CH_Q] * scaled_q_ref[...]
     inner = jnp.sum(jnp.where(mine, inner, 0.0), axis=0, keepdims=True)
-    spread = dot_exact(neg_part, mine.astype(F32), 1, 0)
+    mask = mine.astype(F32).astype(BF16)
+    spread = sum(dot(part, mask, 1, 0) for part in thirds(neg_part))
     inner += jnp.sum(spread * late_ref[:, 2 * Q_GRP :], axis=0, keepdims=True)
     rms = rms_ref[...]
     shrink_ref[...] = rms * rms * rms * inner * (1.0 / D)

time: 142 us -> 142 us (level)
  no operation moved by 1% of the time
where the time goes in v5:
time: 142 us; the launch traced here: 141 us
  waiting for transfers between devices  44.2 us (31%)
  starting transfers between devices  39.5 us (28%)
  Pallas kernels  14.9 us (10%)
  between operations  14.5 us (10%)
  local copies, waits for them, and re-layouts  10.5 us (7%)
  matrix products  9.55 us (7%)
  other arithmetic  8.18 us (6%)
    all_to_all x1, waiting for transfers between devices, per_device(): lax.all_to_all(fetched, 'dp', split_axis=0, concat_axis=0, tiled=True)  21.6 us
    all_to_all x1, starting transfers between devices, per_device(): wanted = lax.all_to_all(code, 'dp', split_axis=0, concat_axis=0, tiled=True)  13 us
    ppermute x9, starting transfers between devices, shifted(): lax.ppermute(value, 'fsdp', [(i, (i + step) % N_FS) for i in range(N_FS)])  11.8 us
    dot_general x8, matrix products, dot(): lax.dot_general(a, b, (((ca,), (cb,)), ((), ())), preferred_element_type=...  9.55 us
    ppermute x9, waiting for transfers between devices, shifted(): lax.ppermute(value, 'fsdp', [(i, (i + step) % N_FS) for i in range(N_FS)])  8.33 us
    all_to_all x1, starting transfers between devices, per_device(): got = lax.all_to_all(sent, 'dp', split_axis=0, concat_axis=0, tiled=True)  8.25 us
    all_to_all x1, waiting for transfers between devices, per_device(): wanted = lax.all_to_all(code, 'dp', split_axis=0, concat_axis=0, tiled=True)  8.1 us
    unnamed x38, local copies, waits for them, and re-layouts  7.08 us
  transfers between devices with their start and end apart: 15, of which 7 were waited for; matrix products, arithmetic and copies ran while one was open for 16% of the time, Pallas kernels for 8%

profile of v5, /device:TPU:1, one launch (start us, length us, event | category | flops | bytes accessed | tf_op | source)
XLA Modules:
  0.0 141.3 jit_solution(8036967209149316074)
XLA Ops:
  7.2 0.7 all-gather.2.cloned.1.call-update
  7.9 0.7 add_bitcast_fusion.name_ref
  8.6 1.2 shard_map.128
  9.8 13.0 %all-to-all-start = ((s32[64,1,16]{2,1,0:T(1,128)}), s32[64,1,16]{2,1,0:T(1,128)S(1)}, u32[]{:S(2)}, u32[]{:S(2)}) async-start(s32[64,1,16]{2,1,0:T(1,128)} %bitcast.2), calls=%async_computation | async-start | bytes 65536 | tf_op jit(solution)/shard_map/all_to_all | solution.py:457
  22.9 1.0 copy.18
  23.9 8.1 %all-to-all-done = s32[64,1,16]{2,1,0:T(1,128)S(1)} async-done(((s32[64,1,16]{2,1,0:T(1,128)}), s32[64,1,16]{2,1,0:T(1,128)S(1)}, u32[]{:S(2)}, u32[]{:S(2)}) %all-to-all-start) | async-done | bytes 4128 | tf_op jit(solution)/shard_map/all_to_all | solution.py:457
  32.0 2.4 %shard_map.129 = bf16[64,14,8,128]{3,2,1,0:T(8,128)(2,1)S(1)} custom-call(s32[64,16]{1,0:T(8,128)S(1)} %bitcast.62, bf16[128,8,128]{2,1,0:T(8,128)(2,1)S(1)} %bitcast.56), custom_call_target="tpu_custom_call" | custom-call | bytes 3670016 | tf_op jit(solution)/shard_map/pallas_call | solution.py:165
  34.5 1.3 copy-done
  35.7 4.9 %all-to-all-start.1 = ((bf16[64,112,128]{2,1,0:T(8,128)(2,1)}), bf16[64,112,128]{2,1,0:T(8,128)(2,1)S(1)}, u32[]{:S(2)}, u32[]{:S(2)}) async-start(bf16[64,112,128]{2,1,0:T(8,128)(2,1)} %bitcast.53), calls=%async_computation.1 | async-start | bytes 3670016 | tf_op jit(solution)/shard_map/all_to_all | solution.py:460
  40.7 4.3 %multiply_convert_fusion = (bf16[256,1024]{1,0:T(8,128)(2,1)S(1)}, bf16[256,1024]{1,0:T(8,128)(2,1)S(1)}, f32[256]{0:T(256)S(1)}, f32[256,1024]{1,0:T(8,128)S(1)}) fusion(f32[1024]{0:T(1024)S(1)} %copy-done.5, bf16[256,2048]{1,0:T(8,128)(2,1)} %param.15, bf16[2048,1024]{1,0:T(8,128)(2,1)} %param.16, bf16[256,1024]{1,0:T(8,128)(2,1)} %param.14), kind=kOutput, calls=%fused_computation.6 | convolution fusion | flops 1076100864 | bytes 7869440 | tf_op jit(solution)/shard_map/dot_general | solution.py:31
  45.0 0.5 fusion.5
  45.5 0.2 fusion.25
  45.7 0.2 fusion.26
  46.0 0.7 pad_maximum_fusion.1
  46.6 1.3 collective-permute-start
  47.9 1.4 %collective-permute-start.1 = (f32[152,256]{1,0:T(8,128)}, f32[152,256]{1,0:T(8,128)}, u32[]{:S(2)}, u32[]{:S(2)}) collective-permute-start(f32[152,256]{1,0:T(8,128)} %pad_maximum_fusion.1), channel_id=1, source_target_pairs={{0,3},{1,0},{2,1},{3,2},{4,7},{5,4},{6,5},{7,6},{8,11},{9,8},{10,9... | collective-permute-start | bytes 466952 | tf_op jit(solution)/shard_map/ppermute | solution.py:53
  49.4 1.7 %collective-permute-start.2 = (f32[152,256]{1,0:T(8,128)}, f32[152,256]{1,0:T(8,128)}, u32[]{:S(2)}, u32[]{:S(2)}) collective-permute-start(f32[152,256]{1,0:T(8,128)} %pad_maximum_fusion.1), channel_id=1, source_target_pairs={{0,2},{1,3},{2,0},{3,1},{4,6},{5,7},{6,4},{7,5},{8,10},{9,11},{10,... | collective-permute-start | bytes 466952 | tf_op jit(solution)/shard_map/ppermute | solution.py:53
  51.0 1.3 fusion.3
  52.3 1.3 convolution_add_fusion
  53.6 1.3 copy-done.9
  55.0 0.9 dynamic-slice_convert_fusion.2
  55.9 2.3 %copy.16 = bf16[256,2048]{0,1:T(8,128)(2,1)} copy(bf16[256,2048]{1,0:T(8,128)(2,1)} %param.15) | data formatting | bytes 2097152 | tf_op jit(solution)/shard_map/optimization_barrier | solution.py:462
  58.1 0.4 collective-permute-start.3
  58.5 2.3 %collective-permute-start.4 = (bf16[64,2048]{1,0:T(8,128)(2,1)}, bf16[64,2048]{1,0:T(8,128)(2,1)S(1)}, u32[]{:S(2)}, u32[]{:S(2)}) collective-permute-start(bf16[64,2048]{1,0:T(8,128)(2,1)} %get-tuple-element.79), channel_id=1, source_target_pairs={{0,3},{1,0},{2,1},{3,2},{4,7},{5,4},{6,5},{7,6},{8,11},{9,8},{10,9... | collective-permute-start | bytes 786440 | tf_op jit(solution)/shard_map/ppermute | solution.py:53
  60.8 2.3 %pad_maximum_fusion = bf16[512,1024]{1,0:T(8,128)(2,1)} fusion(bf16[256,1024]{1,0:T(8,128)(2,1)} %copy-done.13, bf16[256,1024]{1,0:T(8,128)(2,1)} %copy-done.12), kind=kLoop, calls=%fused_computation.2 | loop fusion | flops 2097152 | bytes 2097152 | tf_op jit(solution)/shard_map/concatenate | solution.py:468
  63.2 1.1 add_add_fusion
  64.5 0.1 exponential_reduce_fusion
  64.7 1.2 collective-permute-done.3
  66.0 4.6 %collective-permute-done.5 = bf16[64,2048]{1,0:T(8,128)(2,1)S(1)} collective-permute-done((bf16[64,2048]{1,0:T(8,128)(2,1)S(1)}, bf16[64,2048]{1,0:T(8,128)(2,1)S(1)}, u32[]{:S(2)}, u32[]{:S(2)}) %collective-permute-start.5) | collective-permute-done | bytes 262176 | tf_op jit(solution)/shard_map/ppermute | solution.py:53
  70.6 2.0 %convert_add_fusion = f32[64,2048]{1,0:T(8,128)} fusion(bf16[64,2048]{1,0:T(8,128)(2,1)S(1)} %collective-permute-done.5, bf16[64,2048]{1,0:T(8,128)(2,1)S(1)} %collective-permute-done.4, bf16[64,2048]{1,0:T(8,128)(2,1)S(1)} %collective-permute-done.3, f32[256,2048]{1,0:T(8,128)} %copy-done.9, s32[]{:T(128)S(6)} %select_n.58), kind=kLoop, calls=%fused_computation.10 | loop fusion | flops 786432 | bytes 1835012 | tf_op jit(solution)/shard_map/add | solution.py:84
  72.5 21.6 %all-to-all-done.1 = bf16[64,112,128]{2,1,0:T(8,128)(2,1)S(1)} async-done(((bf16[64,112,128]{2,1,0:T(8,128)(2,1)}), bf16[64,112,128]{2,1,0:T(8,128)(2,1)S(1)}, u32[]{:S(2)}, u32[]{:S(2)}) %all-to-all-start.1) | async-done | bytes 1835040 | tf_op jit(solution)/shard_map/all_to_all | solution.py:460
  94.2 2.4 %shard_map.130 = (f32[16,64]{1,0:T(8,128)S(1)}, bf16[112,8,128]{2,1,0:T(8,128)(2,1)S(1)}) custom-call(s32[1,448]{1,0:T(1,128)S(1)} %get-tuple-element.45.slot_ref, bf16[896,8,128]{2,1,0:T(8,128)(2,1)S(1)} %bitcast.52, bf16[64,8,128]{2,1,0:T(8,128)(2,1)S(1)} %bitcast.60), custom_call_target="tpu_custom_call" | custom-call | flops 2000000 | bytes 2200000 | tf_op jit(solution)/shard_map/pallas_call | solution.py:206
  96.6 0.5 fusion.21
  97.2 1.5 %collective-permute-start.6 = (f32[8,384]{1,0:T(8,128)S(1)}, f32[8,384]{1,0:T(8,128)S(1)}, u32[]{:S(2)}, u32[]{:S(2)}) collective-permute-start(f32[8,384]{1,0:T(8,128)S(1)} %select_maximum_fusion), channel_id=1, source_target_pairs={{0,1},{1,2},{2,3},{3,0},{4,5},{5,6},{6,7},{7,4},{8,9},{9,10},{10,1... | collective-permute-start | bytes 36872 | tf_op jit(solution)/shard_map/ppermute | solution.py:53
  98.7 1.7 %collective-permute-start.7 = (f32[8,384]{1,0:T(8,128)S(1)}, f32[8,384]{1,0:T(8,128)S(1)}, u32[]{:S(2)}, u32[]{:S(2)}) collective-permute-start(f32[8,384]{1,0:T(8,128)S(1)} %select_maximum_fusion), channel_id=1, source_target_pairs={{0,3},{1,0},{2,1},{3,2},{4,7},{5,4},{6,5},{7,6},{8,11},{9,8},{10,9... | collective-permute-start | bytes 36872 | tf_op jit(solution)/shard_map/ppermute | solution.py:53
  100.3 1.5 %collective-permute-start.8 = (f32[8,384]{1,0:T(8,128)S(1)}, f32[8,384]{1,0:T(8,128)S(1)}, u32[]{:S(2)}, u32[]{:S(2)}) collective-permute-start(f32[8,384]{1,0:T(8,128)S(1)} %select_maximum_fusion), channel_id=1, source_target_pairs={{0,2},{1,3},{2,0},{3,1},{4,6},{5,7},{6,4},{7,5},{8,10},{9,11},{10,... | collective-permute-start | bytes 36872 | tf_op jit(solution)/shard_map/ppermute | solution.py:53
  102.0 2.5 %collective-permute-done.8 = f32[8,384]{1,0:T(8,128)S(1)} collective-permute-done((f32[8,384]{1,0:T(8,128)S(1)}, f32[8,384]{1,0:T(8,128)S(1)}, u32[]{:S(2)}, u32[]{:S(2)}) %collective-permute-start.8) | collective-permute-done | bytes 12320 | tf_op jit(solution)/shard_map/ppermute | solution.py:53
  104.5 1.1 shard_map.131
  105.7 1.2 shard_map.132
  106.8 1.3 fusion.27
  108.2 1.4 %collective-permute-start.9 = (f32[8,2048]{1,0:T(8,128)S(1)}, f32[8,2048]{1,0:T(8,128)S(1)}, u32[]{:S(2)}, u32[]{:S(2)}) collective-permute-start(f32[8,2048]{1,0:T(8,128)S(1)} %constant_dynamic-slice_fusion.2), channel_id=1, source_target_pairs={{0,3},{1,2},{2,1},{3,0},{4,7},{5,6},{6,5},{7,4},{8,11},{9,10},{10,... | collective-permute-start | bytes 196616 | tf_op jit(solution)/shard_map/ppermute | solution.py:57
  109.6 8.2 %all-to-all-start.2 = ((f32[64,1,32]{2,1,0:T(1,128)}), f32[64,1,32]{2,1,0:T(1,128)S(1)}, u32[]{:S(2)}, u32[]{:S(2)}) async-start(f32[64,1,32]{2,1,0:T(1,128)} %bitcast.18), calls=%async_computation.2 | async-start | bytes 65536 | tf_op jit(solution)/shard_map/all_to_all | solution.py:525
  118.2 2.6 %shard_map.133 = (bf16[256,1024]{1,0:T(8,128)(2,1)}, bf16[2048,1024]{1,0:T(8,128)(2,1)}) custom-call(f32[256,1024]{1,0:T(8,128)S(1)} %get-tuple-element.44.hidden_ref, f32[16,1024]{1,0:T(8,128)S(1)} %get-tuple-element.64.gained_ref, f32[1,256]{1,0:T(1,128)S(1)} %fusion.15.rms_ref, f32[1,256]{1,0:T(1,128)S(1)} %get-tuple-element.65.shrink_ref, ...), custom_call_target="tpu_custom_call" | custom-call | flops 1100000000 | bytes 7000000 | tf_op jit(solution)/shard_map/pallas_call | solution.py:372
  120.8 0.4 collective-permute-done.10
  121.2 0.8 fusion.1
  122.0 5.1 %all-to-all-done.2 = f32[64,1,32]{2,1,0:T(1,128)S(1)} async-done(((f32[64,1,32]{2,1,0:T(1,128)}), f32[64,1,32]{2,1,0:T(1,128)S(1)}, u32[]{:S(2)}, u32[]{:S(2)}) %all-to-all-start.2) | async-done | bytes 8224 | tf_op jit(solution)/shard_map/all_to_all | solution.py:525
  127.1 3.4 %copy-done.6 = bf16[4096,1024]{1,0:T(8,128)(2,1)S(1)} copy-done((bf16[4096,1024]{1,0:T(8,128)(2,1)S(1)}, bf16[4096,1024]{1,0:T(8,128)(2,1)}, u32[]{:S(2)}) %copy-start.6) | copy-done | bytes 8388632
  130.5 3.9 %shard_map.134 = bf16[128,1024]{1,0:T(8,128)(2,1)} custom-call(s32[64,16]{1,0:T(8,128)S(1)} %bitcast.63, f32[64,32]{1,0:T(8,128)S(1)} %bitcast.64, bf16[4096,1024]{1,0:T(8,128)(2,1)S(1)} %copy-done.6, bf16[128,1024]{1,0:T(8,128)(2,1)S(1)} %copy-done.4), custom_call_target="tpu_custom_call" | custom-call | flops 2500000000 | bytes 9000000 | tf_op jit(solution)/shard_map/pallas_call | solution.py:434
  (69 shorter events, 1.1 us)
Async XLA Ops:
  7.2 120.0 %all-gather.2.cloned.1.call-start = ((), (), s32[]{:S(2)}) async-start(), calls=%async_computation.3 | async-start | bytes 8519680 | tf_op jit(solution)/shard_map/all_gather | solution.py:452
  9.8 22.2 %all-to-all-start = ((s32[64,1,16]{2,1,0:T(1,128)}), s32[64,1,16]{2,1,0:T(1,128)S(1)}, u32[]{:S(2)}, u32[]{:S(2)}) async-start(s32[64,1,16]{2,1,0:T(1,128)} %bitcast.2), calls=%async_computation | async-start | bytes 65536 | tf_op jit(solution)/shard_map/all_to_all | solution.py:457
  34.4 1.3 copy-start
  35.7 4.9 %copy-start.1 = (bf16[64,1024]{1,0:T(8,128)(2,1)S(1)}, bf16[64,1024]{1,0:T(8,128)(2,1)}, u32[]{:S(2)}) copy-start(bf16[64,1024]{1,0:T(8,128)(2,1)} %q_ref) | copy-start | bytes 393220
  35.7 5.0 %copy-start.2 = (bf16[64,1024]{1,0:T(8,128)(2,1)S(1)}, bf16[64,1024]{1,0:T(8,128)(2,1)}, u32[]{:S(2)}) copy-start(bf16[64,1024]{1,0:T(8,128)(2,1)} %pos_ref) | copy-start | bytes 393220
  35.7 5.0 %copy-start.5 = (f32[1024]{0:T(1024)S(1)}, f32[1024]{0:T(1024)}, u32[]{:S(2)}) copy-start(f32[1024]{0:T(1024)} %param.17) | copy-start | bytes 12292
  35.7 58.4 %all-to-all-start.1 = ((bf16[64,112,128]{2,1,0:T(8,128)(2,1)}), bf16[64,112,128]{2,1,0:T(8,128)(2,1)S(1)}, u32[]{:S(2)}, u32[]{:S(2)}) async-start(bf16[64,112,128]{2,1,0:T(8,128)(2,1)} %bitcast.53), calls=%async_computation.1 | async-start | bytes 3670016 | tf_op jit(solution)/shard_map/all_to_all | solution.py:460
  40.7 10.3 %copy-start.7 = (bf16[2048,1024]{1,0:T(8,128)(2,1)S(1)}, bf16[2048,1024]{1,0:T(8,128)(2,1)}, u32[]{:S(2)}) copy-start(bf16[2048,1024]{1,0:T(8,128)(2,1)} %param.16) | copy-start | bytes 12582916
  45.0 6.0 %copy-start.12 = (bf16[256,1024]{1,0:T(8,128)(2,1)}, bf16[256,1024]{1,0:T(8,128)(2,1)S(1)}, u32[]{:S(2)}) copy-start(bf16[256,1024]{1,0:T(8,128)(2,1)S(1)} %get-tuple-element.80) | copy-start | bytes 1572868
  45.0 6.0 %copy-start.13 = (bf16[256,1024]{1,0:T(8,128)(2,1)}, bf16[256,1024]{1,0:T(8,128)(2,1)S(1)}, u32[]{:S(2)}) copy-start(bf16[256,1024]{1,0:T(8,128)(2,1)S(1)} %get-tuple-element.81) | copy-start | bytes 1572868
  45.9 5.1 %copy-start.15 = (f32[8,256]{1,0:T(8,128)}, f32[8,256]{1,0:T(8,128)S(1)}, u32[]{:S(2)}) copy-start(f32[8,256]{1,0:T(8,128)S(1)} %broadcast_in_dim.28) | copy-start | bytes 24580
  46.6 16.5 %collective-permute-start = (f32[152,256]{1,0:T(8,128)}, f32[152,256]{1,0:T(8,128)}, u32[]{:S(2)}, u32[]{:S(2)}) collective-permute-start(f32[152,256]{1,0:T(8,128)} %pad_maximum_fusion.1), channel_id=1, source_target_pairs={{0,1},{1,2},{2,3},{3,0},{4,5},{5,6},{6,7},{7,4},{8,9},{9,10},{10,1... | collective-permute-start | bytes 466952 | tf_op jit(solution)/shard_map/ppermute | solution.py:53
  47.9 15.3 %collective-permute-start.1 = (f32[152,256]{1,0:T(8,128)}, f32[152,256]{1,0:T(8,128)}, u32[]{:S(2)}, u32[]{:S(2)}) collective-permute-start(f32[152,256]{1,0:T(8,128)} %pad_maximum_fusion.1), channel_id=1, source_target_pairs={{0,3},{1,0},{2,1},{3,2},{4,7},{5,4},{6,5},{7,6},{8,11},{9,8},{10,9... | collective-permute-start | bytes 466952 | tf_op jit(solution)/shard_map/ppermute | solution.py:53
  49.4 13.9 %collective-permute-start.2 = (f32[152,256]{1,0:T(8,128)}, f32[152,256]{1,0:T(8,128)}, u32[]{:S(2)}, u32[]{:S(2)}) collective-permute-start(f32[152,256]{1,0:T(8,128)} %pad_maximum_fusion.1), channel_id=1, source_target_pairs={{0,2},{1,3},{2,0},{3,1},{4,6},{5,7},{6,4},{7,5},{8,10},{9,11},{10,... | collective-permute-start | bytes 466952 | tf_op jit(solution)/shard_map/ppermute | solution.py:53
  53.6 1.3 copy-start.9
  58.1 5.0 %copy-start.14 = (bf16[64,2048]{1,0:T(8,128)(2,1)S(1)}, bf16[64,2048]{1,0:T(8,128)(2,1)}, u32[]{:S(2)}) copy-start(bf16[64,2048]{1,0:T(8,128)(2,1)} %get-tuple-element.78) | copy-start | bytes 786436
  58.1 5.1 %copy-start.16 = (f32[8,256]{1,0:T(8,128)S(1)}, f32[8,256]{1,0:T(8,128)}, u32[]{:S(2)}) copy-start(f32[8,256]{1,0:T(8,128)} %copy-done.15) | copy-start | bytes 24580
  58.1 7.8 %collective-permute-start.3 = (bf16[64,2048]{1,0:T(8,128)(2,1)}, bf16[64,2048]{1,0:T(8,128)(2,1)S(1)}, u32[]{:S(2)}, u32[]{:S(2)}) collective-permute-start(bf16[64,2048]{1,0:T(8,128)(2,1)} %get-tuple-element.77), channel_id=1, source_target_pairs={{0,1},{1,2},{2,3},{3,0},{4,5},{5,6},{6,7},{7,4},{8,9},{9,10},{10,1... | collective-permute-start | bytes 786440 | tf_op jit(solution)/shard_map/ppermute | solution.py:53
  58.5 7.4 %collective-permute-start.4 = (bf16[64,2048]{1,0:T(8,128)(2,1)}, bf16[64,2048]{1,0:T(8,128)(2,1)S(1)}, u32[]{:S(2)}, u32[]{:S(2)}) collective-permute-start(bf16[64,2048]{1,0:T(8,128)(2,1)} %get-tuple-element.79), channel_id=1, source_target_pairs={{0,3},{1,0},{2,1},{3,2},{4,7},{5,4},{6,5},{7,6},{8,11},{9,8},{10,9... | collective-permute-start | bytes 786440 | tf_op jit(solution)/shard_map/ppermute | solution.py:53
  63.1 7.4 %collective-permute-start.5 = (bf16[64,2048]{1,0:T(8,128)(2,1)S(1)}, bf16[64,2048]{1,0:T(8,128)(2,1)S(1)}, u32[]{:S(2)}, u32[]{:S(2)}) collective-permute-start(bf16[64,2048]{1,0:T(8,128)(2,1)S(1)} %copy-done.14), channel_id=1, source_target_pairs={{0,2},{1,3},{2,0},{3,1},{4,6},{5,7},{6,4},{7,5},{8,10},{9,11},{10,... | collective-permute-start | bytes 786440 | tf_op jit(solution)/shard_map/ppermute | solution.py:53
  94.1 2.4 %copy-start.10 = (bf16[512,1024]{1,0:T(8,128)(2,1)S(1)}, bf16[512,1024]{1,0:T(8,128)(2,1)}, u32[]{:S(2)}) copy-start(bf16[512,1024]{1,0:T(8,128)(2,1)} %pad_maximum_fusion) | copy-start | bytes 3145732
  94.1 12.7 %copy-start.8 = (bf16[2048,1024]{1,0:T(8,128)(2,1)S(1)}, bf16[2048,1024]{1,0:T(8,128)(2,1)}, u32[]{:S(2)}) copy-start(bf16[2048,1024]{1,0:T(8,128)(2,1)} %param.16) | copy-start | bytes 12582916
  97.2 4.7 %collective-permute-start.6 = (f32[8,384]{1,0:T(8,128)S(1)}, f32[8,384]{1,0:T(8,128)S(1)}, u32[]{:S(2)}, u32[]{:S(2)}) collective-permute-start(f32[8,384]{1,0:T(8,128)S(1)} %select_maximum_fusion), channel_id=1, source_target_pairs={{0,1},{1,2},{2,3},{3,0},{4,5},{5,6},{6,7},{7,4},{8,9},{9,10},{10,1... | collective-permute-start | bytes 36872 | tf_op jit(solution)/shard_map/ppermute | solution.py:53
  98.7 3.3 %collective-permute-start.7 = (f32[8,384]{1,0:T(8,128)S(1)}, f32[8,384]{1,0:T(8,128)S(1)}, u32[]{:S(2)}, u32[]{:S(2)}) collective-permute-start(f32[8,384]{1,0:T(8,128)S(1)} %select_maximum_fusion), channel_id=1, source_target_pairs={{0,3},{1,0},{2,1},{3,2},{4,7},{5,4},{6,5},{7,6},{8,11},{9,8},{10,9... | collective-permute-start | bytes 36872 | tf_op jit(solution)/shard_map/ppermute | solution.py:53
  100.3 4.1 %collective-permute-start.8 = (f32[8,384]{1,0:T(8,128)S(1)}, f32[8,384]{1,0:T(8,128)S(1)}, u32[]{:S(2)}, u32[]{:S(2)}) collective-permute-start(f32[8,384]{1,0:T(8,128)S(1)} %select_maximum_fusion), channel_id=1, source_target_pairs={{0,2},{1,3},{2,0},{3,1},{4,6},{5,7},{6,4},{7,5},{8,10},{9,11},{10,... | collective-permute-start | bytes 36872 | tf_op jit(solution)/shard_map/ppermute | solution.py:53
  106.8 11.3 %copy-start.3 = (bf16[256,2048]{0,1:T(8,128)(2,1)S(1)}, bf16[256,2048]{0,1:T(8,128)(2,1)}, u32[]{:S(2)}) copy-start(bf16[256,2048]{0,1:T(8,128)(2,1)} %copy.16) | copy-start | bytes 3145732
  108.2 9.8 %collective-permute-start.9 = (f32[8,2048]{1,0:T(8,128)S(1)}, f32[8,2048]{1,0:T(8,128)S(1)}, u32[]{:S(2)}, u32[]{:S(2)}) collective-permute-start(f32[8,2048]{1,0:T(8,128)S(1)} %constant_dynamic-slice_fusion.2), channel_id=1, source_target_pairs={{0,3},{1,2},{2,1},{3,0},{4,7},{5,6},{6,5},{7,4},{8,11},{9,10},{10,... | collective-permute-start | bytes 196616 | tf_op jit(solution)/shard_map/ppermute | solution.py:57
  109.6 17.5 %all-to-all-start.2 = ((f32[64,1,32]{2,1,0:T(1,128)}), f32[64,1,32]{2,1,0:T(1,128)S(1)}, u32[]{:S(2)}, u32[]{:S(2)}) async-start(f32[64,1,32]{2,1,0:T(1,128)} %bitcast.18), calls=%async_computation.2 | async-start | bytes 65536 | tf_op jit(solution)/shard_map/all_to_all | solution.py:525
  118.0 3.2 %copy-start.11 = (f32[64,2048]{1,0:T(8,128)S(1)}, f32[64,2048]{1,0:T(8,128)}, u32[]{:S(2)}) copy-start(f32[64,2048]{1,0:T(8,128)} %convert_add_fusion) | copy-start | bytes 1572868
  118.0 3.1 %collective-permute-start.10 = (f32[4,2048]{1,0:T(4,128)S(1)}, f32[4,2048]{1,0:T(4,128)S(1)}, u32[]{:S(2)}, u32[]{:S(2)}) collective-permute-start(f32[4,2048]{1,0:T(4,128)S(1)} %constant_dynamic-slice_fusion.1), channel_id=1, source_target_pairs={{0,1},{1,0},{2,3},{3,2},{4,5},{5,4},{6,7},{7,6},{8,9},{9,8},{10,11... | collective-permute-start | bytes 98312 | tf_op jit(solution)/shard_map/ppermute | solution.py:57
  118.1 9.0 %copy-start.4 = (bf16[128,1024]{1,0:T(8,128)(2,1)S(1)}, bf16[128,1024]{1,0:T(8,128)(2,1)}, u32[]{:S(2)}) copy-start(bf16[128,1024]{1,0:T(8,128)(2,1)} %pool_ref.1) | copy-start | bytes 786436
  127.1 3.4 %copy-start.6 = (bf16[4096,1024]{1,0:T(8,128)(2,1)S(1)}, bf16[4096,1024]{1,0:T(8,128)(2,1)}, u32[]{:S(2)}) copy-start(bf16[4096,1024]{1,0:T(8,128)(2,1)} %all-gather.2.cloned.1.call-done.q_ref) | copy-start | bytes 25165828
Sparse Core Ops, SparseCore 0:
  10.8 100.1 all-gather.1
